TPU v7x, 32 devices: a whole 2x2x4 slice. The times are simulated.
32 devices in a mesh: groups: 2 (over y), tensor: 8 (over z, x), dp: 2 (over core).
Axes of the slice: x: 2, y: 2, z: 4, core: 2. Of those that a mesh axis runs over, the one named last changes fastest.
Arguments:
- tokens: bfloat16 [2048, 4096], P(('groups', 'tensor', 'dp')), parts along dimension 0, may hold values from -6 to 6
- norm_gain: float32 [4096], replicated, may hold values from 0.5 to 1.5
- gate_codes: bfloat16 [4096, 28672], P(None, 'tensor'), may hold values from -127 to 127, as said below
- gate_scales: float32 [32, 28672], P(None, 'tensor'), may hold values from 0.00010625 to 0.000421875
- up_codes: bfloat16 [4096, 28672], P(None, 'tensor'), may hold values from -127 to 127, as said below
- up_scales: float32 [32, 28672], P(None, 'tensor'), may hold values from 0.00010625 to 0.000421875
- down_codes: bfloat16 [28672, 4096], P('tensor'), may hold values from -127 to 127, as said below
- down_scales: float32 [1024, 4096], P('tensor'), may hold values from 4.0158724e-05 to 0.00015945376
Outputs:
- layer_out: bfloat16 [2048, 4096], P(('groups', 'tensor', 'dp')), parts along dimension 0
There are 2 independent parts, one for each index of `groups`. A program takes and returns all parts, laid end to end along the dimension named above; an argument that names none is the same for every part. Nothing has to cross between parts.
Inputs may be any that keep to these rules, and one draw needn't show every extreme that they name: `gate_codes`: every entry is a whole number. `up_codes`: every entry is a whole number. `down_codes`: every entry is a whole number.
All inputs are finite; a program needn't handle non-finite values.
Results may differ from a plain program's by a relative error of at most 0.012.
Values may be sent and summed in bfloat16 or wider, within the bound.
No kernel may reach another device: no remote copies, remote signals or barrier semaphores. Data moves between devices by JAX's collectives and lax.ppermute only.
A program may use at most 320 MiB of HBM per device.

v0:
```python
import jax
import jax.numpy as jnp
from jax import lax
from jax.sharding import PartitionSpec as P

HB = 28
FF = 28672


EPSILON = 1e-05


def from_partner(value, axis, stride):
    return lax.ppermute(value, axis, [(i, i ^ 1 << stride) for i in range(lax.axis_size(axis))])


def hadamard_small():
    modulus = 13
    residues = [number * number % modulus for number in range(1, modulus)]
    legendre = [0] + [1 if number in residues else -1 for number in range(1, modulus)]
    plus_block = [[1, 1], [1, -1]]
    zero_block = [[1, -1], [-1, -1]]

    def conference_entry(row_number, column_number):
        if row_number == 0 and column_number == 0:
            return 0
        if row_number == 0 or column_number == 0:
            return 1
        return legendre[(column_number - row_number) % modulus]

    table = [
        [
            conference_entry(row_block, column_block) * plus_block[row_inner][column_inner]
            + (zero_block[row_inner][column_inner] if row_block == column_block else 0)
            for column_block in range(modulus + 1)
            for column_inner in range(2)
        ]
        for row_block in range(modulus + 1)
        for row_inner in range(2)
    ]
    return jnp.asarray(table, jnp.float32)


def walsh(order):
    counter = jnp.arange(order, dtype=jnp.int32)
    common = counter[:, None] & counter[None, :]
    parity = jnp.zeros((order, order), jnp.int32)
    for level in range(order.bit_length() - 1):
        parity = parity + (common >> level & 1)
    return (1 - 2 * (parity % 2)).astype(jnp.float32)


def dequantize(codes, scales):
    blocks = scales.shape[0]
    height = codes.shape[0]
    width = codes.shape[1]
    spread = codes.astype(jnp.float32).reshape(blocks, height // blocks, width) * scales[:, None, :]
    return spread.reshape(height, width).astype(jnp.bfloat16)


def shards(
    tokens, norm_gain, gate_codes, gate_scales, up_codes, up_scales, down_codes, down_scales
):
    floated = tokens.astype(jnp.float32)
    normed = (
        floated
        * lax.rsqrt(jnp.mean(floated * floated, axis=1, keepdims=True) + EPSILON)
        * norm_gain
    ).astype(jnp.bfloat16)
    gate_weight = dequantize(gate_codes, gate_scales)
    up_weight = dequantize(up_codes, up_scales)
    down_weight = dequantize(down_codes, down_scales)
    piece = lax.all_gather(normed, "tensor", axis=0, tiled=True)
    gate = jnp.dot(piece, gate_weight, preferred_element_type=jnp.float32)
    upward = jnp.dot(piece, up_weight, preferred_element_type=jnp.float32)
    hidden = (jax.nn.silu(gate) * upward).astype(jnp.bfloat16)
    total_rows = hidden.shape[0]
    local_width = hidden.shape[1]
    devices = lax.axis_size("tensor")
    local_walsh = local_width // HB
    small_table = hadamard_small()
    blocks = hidden.astype(jnp.float32).reshape(total_rows, local_walsh, HB)
    blocks = jnp.einsum("tia,ac->tic", blocks, small_table, precision=lax.Precision.HIGHEST)
    blocks = jnp.einsum("ji,tic->tjc", walsh(local_walsh), blocks, precision=lax.Precision.HIGHEST)
    blocks = blocks.reshape(total_rows, local_width)
    position = lax.axis_index("tensor")
    for level in range(devices.bit_length() - 1):
        partner = from_partner(blocks.astype(jnp.bfloat16), "tensor", level).astype(blocks.dtype)
        upper_bit = position >> level & 1
        signed = (1 - 2 * upper_bit).astype(jnp.float32)
        blocks = partner + signed * blocks
    rotated = (blocks * FF ** (-0.5)).astype(jnp.bfloat16)
    piece = rotated
    summed = lax.psum_scatter(
        jnp.dot(piece, down_weight, preferred_element_type=jnp.float32),
        "tensor",
        scatter_dimension=0,
        tiled=True,
    )
    return (floated + summed).astype(jnp.bfloat16)


def solution(mesh):
    return jax.shard_map(
        shards,
        mesh=mesh,
        in_specs=(
            P(("groups", "tensor", "dp"), None),
            P(),
            P(None, "tensor"),
            P(None, "tensor"),
            P(None, "tensor"),
            P(None, "tensor"),
            P("tensor", None),
            P("tensor", None),
        ),
        out_specs=P(("groups", "tensor", "dp"), None),
        check_vma=False,
    )
```

profile of v0, /device:TPU:0, one launch (start us, length us, event | category | flops | bytes accessed | tf_op | source)
XLA Modules:
  0.0 707.0 jit_solution(13522373603107353627)
XLA Ops:
  9.9 21.0 %fusion.1 = bf16[4096,3584]{1,0:T(8,128)(2,1)} fusion(bf16[4096,3584]{1,0:T(8,128)(2,1)} %param.11, f32[32,3584]{1,0:T(8,128)} %param.12), kind=kLoop, calls=%fused_computation.3 | loop fusion | flops 44040192 | bytes 59179008 | tf_op jit(solution)/shard_map/convert_element_type | solution.py:58
  31.0 20.9 %fusion = bf16[4096,3584]{1,0:T(8,128)(2,1)} fusion(bf16[4096,3584]{1,0:T(8,128)(2,1)} %param.13, f32[32,3584]{1,0:T(8,128)S(1)} %copy-done.2), kind=kLoop, calls=%fused_computation.1 | loop fusion | flops 44040192 | bytes 59179008 | tf_op jit(solution)/shard_map/convert_element_type | solution.py:58
  51.8 34.3 %all-gather.2.cloned.1.call-done = bf16[512,4096]{1,0:T(8,128)(2,1)} async-done(((bf16[64,4096]{1,0:T(8,128)(2,1)}), bf16[512,4096]{1,0:T(8,128)(2,1)}) %all-gather.2.cloned.1.call-update) | async-done | bytes 4194320 | tf_op jit(solution)/shard_map/all_gather | solution.py:73
  86.1 23.7 %fusion.41 = f32[512,3584]{1,0:T(8,128)} fusion(bf16[512,4096]{1,0:T(8,128)(2,1)} %all-gather.2.cloned.1.call-done, bf16[4096,3584]{1,0:T(8,128)(2,1)} %fusion.1), kind=kOutput, calls=%fused_computation.52 | convolution fusion | flops 15032385536 | bytes 40894464 | tf_op jit(solution)/shard_map/dot_general | solution.py:74
  109.8 24.5 %multiply_convert_fusion.3 = bf16[512,3584]{1,0:T(8,128)(2,1)} fusion(f32[512,3584]{1,0:T(8,128)} %fusion.41, bf16[512,4096]{1,0:T(8,128)(2,1)} %all-gather.2.cloned.1.call-done, bf16[4096,3584]{1,0:T(8,128)(2,1)} %fusion), kind=kOutput, calls=%fused_computation.12 | convolution fusion | flops 15043395584 | bytes 44564480 | tf_op jit(solution)/shard_map/dot_general | solution.py:75
  134.3 5.9 copy.10
  140.2 6.4 reshape.28
  146.7 6.0 fusion.42
  152.7 11.9 %convert_bitcast_fusion = (bf16[512,128,28]{0,1,2:T(8,128)(2,1)S(1)}, f32[512,128,28]{0,1,2:T(8,128)}) fusion(f32[]{:T(128)S(6)} %convert_element_type.82, f32[512,128,28]{0,2,1:T(8,128)S(1)} %fusion.42), kind=kOutput, calls=%fused_computation.16 | convolution fusion | flops 2822815744 | bytes 18350084 | tf_op jit(solution)/shard_map/ji,tic->tjc/dot_general | solution.py:84
  164.6 4.1 copy.11
  168.7 6.5 convert_element_type.80
  175.7 10.6 %copy.12 = f32[512,128,28]{0,2,1:T(8,128)} copy(f32[512,128,28]{0,1,2:T(8,128)} %get-tuple-element.6) | data formatting | bytes 14680064 | tf_op jit(solution)/shard_map/mul | solution.py:91
  186.3 9.0 %mul.119 = f32[512,3584]{0,1:T(8,128)} reshape(f32[512,128,28]{0,2,1:T(8,128)} %copy.12) | data formatting | bytes 14680064 | tf_op jit(solution)/shard_map/mul | solution.py:91
  195.3 60.0 %collective-permute-done = bf16[512,3584]{0,1:T(8,128)(2,1)} collective-permute-done((bf16[512,3584]{0,1:T(8,128)(2,1)}, bf16[512,3584]{0,1:T(8,128)(2,1)}, u32[]{:S(2)}, u32[]{:S(2)}) %collective-permute-start) | collective-permute-done | bytes 3670048 | tf_op jit(solution)/shard_map/ppermute | solution.py:14
  255.3 7.2 %fusion.5 = bf16[512,3584]{0,1:T(8,128)(2,1)} fusion(f32[512,3584]{0,1:T(8,128)} %mul.119, bf16[512,3584]{0,1:T(8,128)(2,1)} %collective-permute-done), kind=kLoop, calls=%fused_computation.13 | loop fusion | flops 5505024 | bytes 14680064 | tf_op jit(solution)/shard_map/convert_element_type | solution.py:88
  263.5 78.3 %collective-permute-done.1 = bf16[512,3584]{0,1:T(8,128)(2,1)} collective-permute-done((bf16[512,3584]{0,1:T(8,128)(2,1)}, bf16[512,3584]{0,1:T(8,128)(2,1)}, u32[]{:S(2)}, u32[]{:S(2)}) %collective-permute-start.1) | collective-permute-done | bytes 3670048 | tf_op jit(solution)/shard_map/ppermute | solution.py:14
  341.8 8.8 %fusion.8 = bf16[512,3584]{0,1:T(8,128)(2,1)} fusion(f32[512,3584]{0,1:T(8,128)} %mul.119, bf16[512,3584]{0,1:T(8,128)(2,1)} %collective-permute-done, f32[]{:T(128)S(6)} %convert_element_type.85, bf16[512,3584]{0,1:T(8,128)(2,1)} %collective-permute-done.1), kind=kLoop, calls=%fused_computation.17 | loop fusion | flops 11010048 | bytes 18350084 | tf_op jit(solution)/shard_map/convert_element_type | solution.py:88
  350.6 3.2 collective-permute-start.2
  353.8 21.2 %mul.128 = f32[128,28,4096]{2,1,0:T(8,128)} broadcast(f32[128,4096]{1,0:T(8,128)S(1)} %copy-done.1), dimensions={0,2} | broadcast | bytes 60817408 | tf_op jit(solution)/shard_map/mul | solution.py:57
  375.0 51.6 %mul.129 = f32[3584,4096]{1,0:T(8,128)} reshape(f32[128,28,4096]{2,1,0:T(8,128)} %mul.128) | data formatting | bytes 117440512 | tf_op jit(solution)/shard_map/mul | solution.py:57
  426.7 83.3 %collective-permute-done.2 = bf16[512,3584]{0,1:T(8,128)(2,1)} collective-permute-done((bf16[512,3584]{0,1:T(8,128)(2,1)}, bf16[512,3584]{0,1:T(8,128)(2,1)}, u32[]{:S(2)}, u32[]{:S(2)}) %collective-permute-start.2) | collective-permute-done | bytes 3670048 | tf_op jit(solution)/shard_map/ppermute | solution.py:14
  509.9 38.7 %fusion.2 = f32[512,4096]{1,0:T(8,128)} fusion(f32[3584,4096]{1,0:T(8,128)} %mul.129, bf16[3584,4096]{1,0:T(8,128)(2,1)} %param.15, bf16[512,3584]{0,1:T(8,128)(2,1)} %collective-permute-done.2, f32[]{:T(128)S(6)} %convert_element_type.88, bf16[512,3584]{0,1:T(8,128)(2,1)} %collective-permute-done.1, f32[512,3584]{0,1:T(8,128)} %mul.119, ...), kind=kOutput, calls=%fused_computation.5 | convolution fusion | flops 15094775808 | bytes 114819080 | tf_op jit(solution)/shard_map/dot_general | solution.py:95
  548.6 149.4 %reduce-scatter.2.cloned.1.call-done = f32[64,4096]{1,0:T(8,128)} async-done(((f32[512,4096]{1,0:T(8,128)}), f32[64,4096]{1,0:T(8,128)}) %reduce-scatter.2.cloned.1.call-update) | async-done | bytes 1048592 | tf_op jit(solution)/shard_map/reduce_scatter | solution.py:94
  698.1 2.1 fusion.12
  (17 shorter events, 4.9 us)
Async XLA Ops:
  6.5 79.6 %all-gather.2.cloned.1.call-start = ((), (), s32[]{:S(2)}) async-start(), calls=%async_computation.1 | async-start | bytes 4718592 | tf_op jit(solution)/shard_map/all_gather | solution.py:73
  9.9 688.2 %reduce-scatter.2.cloned.1.call-start = ((), (), s32[]{:S(2)}) async-start(), calls=%async_computation.2 | async-start | bytes 9437184 | tf_op jit(solution)/shard_map/reduce_scatter | solution.py:94
  9.9 21.1 %copy-start.2 = (f32[32,3584]{1,0:T(8,128)S(1)}, f32[32,3584]{1,0:T(8,128)}, u32[]{:S(2)}) copy-start(f32[32,3584]{1,0:T(8,128)} %param.14) | copy-start | bytes 1376260
  134.3 12.4 %copy-start.3 = (f32[28,28,1]{1,0,2:T(8,128)S(1)}, f32[28,28,1]{1,0,2:T(8,128)}, u32[]{:S(2)}) copy-start(f32[28,28,1]{1,0,2:T(8,128)} %constant.49) | copy-start | bytes 9412
  175.2 80.2 %collective-permute-start = (bf16[512,3584]{0,1:T(8,128)(2,1)}, bf16[512,3584]{0,1:T(8,128)(2,1)}, u32[]{:S(2)}, u32[]{:S(2)}) collective-permute-start(bf16[512,3584]{0,1:T(8,128)(2,1)} %convert_element_type.80), channel_id=1, source_target_pairs={{0,2},{2,0},{4,6},{6,4},{8,10},{10,8},{12,14},{14,12},{1,3},{3,1},... | collective-permute-start | bytes 11010056 | tf_op jit(solution)/shard_map/ppermute | solution.py:14
  262.5 79.3 %collective-permute-start.1 = (bf16[512,3584]{0,1:T(8,128)(2,1)}, bf16[512,3584]{0,1:T(8,128)(2,1)}, u32[]{:S(2)}, u32[]{:S(2)}) collective-permute-start(bf16[512,3584]{0,1:T(8,128)(2,1)} %fusion.5), channel_id=1, source_target_pairs={{0,4},{2,6},{4,0},{6,2},{8,12},{10,14},{12,8},{14,10},{1,5},{3,7},... | collective-permute-start | bytes 11010056 | tf_op jit(solution)/shard_map/ppermute | solution.py:14
  263.5 90.3 %copy-start.1 = (f32[128,4096]{1,0:T(8,128)S(1)}, f32[128,4096]{1,0:T(8,128)}, u32[]{:S(2)}) copy-start(f32[128,4096]{1,0:T(8,128)} %param.16) | copy-start | bytes 6291460
  350.6 159.3 %collective-permute-start.2 = (bf16[512,3584]{0,1:T(8,128)(2,1)}, bf16[512,3584]{0,1:T(8,128)(2,1)}, u32[]{:S(2)}, u32[]{:S(2)}) collective-permute-start(bf16[512,3584]{0,1:T(8,128)(2,1)} %fusion.8), channel_id=1, source_target_pairs={{0,8},{2,10},{4,12},{6,14},{8,0},{10,2},{12,4},{14,6},{1,9},{3,11}... | collective-permute-start | bytes 11010056 | tf_op jit(solution)/shard_map/ppermute | solution.py:14
  548.6 149.5 %copy-start = (bf16[64,4096]{1,0:T(8,128)(2,1)S(1)}, bf16[64,4096]{1,0:T(8,128)(2,1)}, u32[]{:S(2)}) copy-start(bf16[64,4096]{1,0:T(8,128)(2,1)} %param.9) | copy-start | bytes 1572868
Sparse Core Ops, SparseCore 0:
  10.0 76.0 all-gather.1
  548.8 149.2 reduce-scatter.1
where the time goes:
time: 708 us; the launch traced here: 707 us
  waiting for transfers between devices  405 us (57%)
  local copies, waits for them, and re-layouts  115 us (16%)
  matrix products  105 us (15%)
  other arithmetic  63.3 us (9%)
  between operations  13.5 us (2%)
    ppermute x3, waiting for transfers between devices, from_partner(): lax.ppermute(value, axis, [(i, i ^ 1 << stride) for i in range(lax.axis_s...  222 us
    reduce_scatter x1, waiting for transfers between devices, shards(): lax.psum_scatter(jnp.dot(piece, down_weight, preferred_element_type=jnp.f...  149 us
    mul x2, local copies, waits for them, and re-layouts, dequantize(): codes.astype(jnp.float32).reshape(blocks, height // blocks, width)  72.8 us
    convert_element_type x2, other arithmetic, dequantize(): return spread.reshape(height, width).astype(jnp.bfloat16)  41.9 us
    dot_general x1, matrix products, shards(): jnp.dot(piece, down_weight, preferred_element_type=jnp.float32)  38.7 us
    all_gather x1, waiting for transfers between devices, shards(): piece = lax.all_gather(normed, 'tensor', axis=0, tiled=True)  34.3 us
    dot_general x1, matrix products, shards(): upward = jnp.dot(piece, up_weight, preferred_element_type=jnp.float32)  24.5 us
    dot_general x1, matrix products, shards(): gate = jnp.dot(piece, gate_weight, preferred_element_type=jnp.float32)  23.7 us
  transfers between devices with their start and end apart: 5, of which 5 were waited for; matrix products, arithmetic and copies ran while one was open for 19% of the time, Pallas kernels for 0%

commit v1 on v0

v1 whole, which is shorter than its diff:
```python
import functools
import math

import jax
import jax.numpy as jnp
import ml_dtypes
import numpy as np
from jax import lax
from jax.experimental import pallas as pl
from jax.experimental.pallas import tpu as pltpu
from jax.sharding import PartitionSpec as P

EPSILON = 1e-05
AXIS = "tensor"
MIB = 1 << 20


def hadamard_small():
    modulus = 13
    residues = [number * number % modulus for number in range(1, modulus)]
    legendre = [0] + [1 if number in residues else -1 for number in range(1, modulus)]
    conference = np.zeros((modulus + 1, modulus + 1), np.int64)
    conference[0, 1:] = 1
    conference[1:, 0] = 1
    for row in range(1, modulus + 1):
        for column in range(1, modulus + 1):
            conference[row, column] = legendre[(column - row) % modulus]
    plus_block = np.array([[1, 1], [1, -1]])
    zero_block = np.array([[1, -1], [-1, -1]])
    return np.kron(conference, plus_block) + np.kron(np.eye(modulus + 1, dtype=np.int64), zero_block)


def walsh(order):
    table = np.ones((1, 1), np.int64)
    while table.shape[0] < order:
        table = np.kron(np.array([[1, 1], [1, -1]]), table)
    return table


def exchange(value, stride):
    return lax.ppermute(value, AXIS, [(i, i ^ stride) for i in range(lax.axis_size(AXIS))])


def gather_pieces(own, devices):
    pieces = {0: own}
    order = sorted(range(1, devices), key=lambda k: (bin(k).count("1"), -k))
    for k in order:
        low = k & -k
        pieces[k] = exchange(pieces[k ^ low], low)
    return [pieces[k] for k in range(devices)]


def swap_pieces(pieces):
    devices = len(pieces)
    out = list(pieces)
    for k in range(devices - 1, 0, -1):
        out[k] = exchange(pieces[k], k)
    return out


def reversed_bits(k, devices):
    levels = devices.bit_length() - 1
    return sum(((k >> level) & 1) << (levels - 1 - level) for level in range(levels))


def norm_kernel(cuts, tokens_ref, gain_ref, *out_refs):
    floated = tokens_ref[...].astype(jnp.float32)
    inverse = lax.rsqrt(jnp.mean(floated * floated, axis=1, keepdims=True) + EPSILON)
    normed = (floated * inverse * gain_ref[...]).astype(jnp.bfloat16)
    for (start, rows), out_ref in zip(cuts, out_refs):
        out_ref[...] = normed[start : start + rows]


def norm(tokens, gain, cuts):
    rows, width = tokens.shape
    return pl.pallas_call(
        functools.partial(norm_kernel, cuts),
        out_shape=[jax.ShapeDtypeStruct((count, width), jnp.bfloat16) for _, count in cuts],
        compiler_params=pltpu.CompilerParams(vmem_limit_bytes=16 * MIB),
        cost_estimate=pl.CostEstimate(
            flops=5 * rows * width, bytes_accessed=4 * rows * width, transcendentals=rows
        ),
        name="norm",
    )(tokens, gain.reshape(1, width))


def gate_up_kernel(devices, depth, qblock, *refs):
    piece_refs = refs[:devices]
    gate_ref, gate_scale_ref, up_ref, up_scale_ref = refs[devices : devices + 4]
    out_refs = refs[devices + 4 : 2 * devices + 4]
    held = refs[2 * devices + 4]
    rows = piece_refs[0].shape[0]

    @pl.when(pl.program_id(0) == 0)
    def _():
        for k in range(devices):
            held[k * rows : (k + 1) * rows, :] = piece_refs[k][...]

    def weight(code_ref, scale_ref, at):
        parts = []
        for block in range(at // qblock, (at + depth) // qblock):
            codes = code_ref[block * qblock : (block + 1) * qblock, :].astype(jnp.float32)
            parts.append((codes * scale_ref[block : block + 1, :]).astype(jnp.bfloat16))
        return jnp.concatenate(parts, axis=0)

    gate = up = None
    for at in range(0, gate_ref.shape[0], depth):
        left = held[:, at : at + depth]
        term = jnp.dot(left, weight(gate_ref, gate_scale_ref, at), preferred_element_type=jnp.float32)
        gate = term if gate is None else gate + term
        term = jnp.dot(left, weight(up_ref, up_scale_ref, at), preferred_element_type=jnp.float32)
        up = term if up is None else up + term
    hidden = (gate / (1.0 + jnp.exp(-gate)) * up).astype(jnp.bfloat16)
    for k in range(devices):
        out_refs[k][...] = hidden[k * rows : (k + 1) * rows]


def gate_up(pieces, gate_codes, gate_scales, up_codes, up_scales):
    devices = len(pieces)
    rows, width = pieces[0].shape
    local = gate_codes.shape[1]
    blocks = gate_scales.shape[0]
    tile = 256
    codes = pl.BlockSpec((width, tile), lambda i: (0, i))
    scales = pl.BlockSpec((blocks, tile), lambda i: (0, i))
    return pl.pallas_call(
        functools.partial(gate_up_kernel, devices, 512, width // blocks),
        grid=(local // tile,),
        in_specs=[pl.BlockSpec((rows, width), lambda i: (0, 0))] * devices
        + [codes, scales, codes, scales],
        out_specs=[pl.BlockSpec((rows, tile), lambda i: (0, i))] * devices,
        out_shape=[jax.ShapeDtypeStruct((rows, local), jnp.bfloat16)] * devices,
        scratch_shapes=[pltpu.VMEM((devices * rows, width), jnp.bfloat16)],
        compiler_params=pltpu.CompilerParams(
            dimension_semantics=("arbitrary",), vmem_limit_bytes=40 * MIB
        ),
        cost_estimate=pl.CostEstimate(
            flops=4 * devices * rows * width * local,
            bytes_accessed=4 * width * local,
            transcendentals=devices * rows * local,
        ),
        name="gate_up",
    )(*pieces, gate_codes, gate_scales, up_codes, up_scales)


def rotate_kernel(devices, factor, sign_ref, *refs):
    piece_refs = refs[:devices]
    table_ref = refs[devices]
    out_refs = refs[devices + 1 : 2 * devices + 1]
    held = refs[2 * devices + 1]
    rows, local = piece_refs[0].shape
    block = table_ref.shape[0]
    inner = local // block
    count = devices * inner
    for k in range(devices):
        sign = sign_ref[0, k].astype(jnp.bfloat16)
        for q in range(inner):
            at = (k * inner + q) * rows
            held[at : at + rows, :] = piece_refs[k][:, q * block : (q + 1) * block] * sign
    for start in range(0, block, 256):
        stop = min(start + 256, block)
        product = jnp.dot(
            held[...], table_ref[:, start:stop], preferred_element_type=jnp.float32
        )
        values = [product[index * rows : (index + 1) * rows] for index in range(count)]
        stride = 1
        while stride < count:
            values = [
                values[index] + values[index ^ stride]
                if not index & stride
                else values[index ^ stride] - values[index]
                for index in range(count)
            ]
            stride *= 2
        for k in range(devices):
            scale = sign_ref[1, k] * factor
            for q in range(inner):
                out_refs[k][:, q * block + start : q * block + stop] = (
                    values[k * inner + q] * scale
                ).astype(jnp.bfloat16)


def rotate(pieces, signs, table):
    devices = len(pieces)
    rows, local = pieces[0].shape
    block = table.shape[0]
    vmem = pl.BlockSpec(memory_space=pltpu.VMEM)
    return pl.pallas_call(
        functools.partial(rotate_kernel, devices, (devices * local) ** (-0.5)),
        in_specs=[pl.BlockSpec(memory_space=pltpu.SMEM)] + [vmem] * (devices + 1),
        out_specs=[vmem] * devices,
        out_shape=[jax.ShapeDtypeStruct((rows, local), jnp.bfloat16)] * devices,
        scratch_shapes=[pltpu.VMEM((devices * rows * local // block, block), jnp.bfloat16)],
        compiler_params=pltpu.CompilerParams(vmem_limit_bytes=40 * MIB),
        cost_estimate=pl.CostEstimate(
            flops=2 * devices * rows * local * block,
            bytes_accessed=4 * devices * rows * local,
            transcendentals=0,
        ),
        name="rotate",
    )(signs, *pieces, table)


def down_kernel(devices, group, order, *refs):
    piece_refs = refs[:devices]
    code_ref, scale_ref, keep_ref, send_ref, held, weight = refs[devices:]
    rows, local = piece_refs[0].shape
    half = devices // 2

    @pl.when(pl.program_id(0) == 0)
    def _():
        for place, k in enumerate(order):
            held[place * rows : (place + 1) * rows, :] = piece_refs[k][...]

    tile = code_ref.shape[1]
    repeat = math.lcm(group, 16)
    low_rows = lax.broadcasted_iota(jnp.int32, (8, tile), 0)
    parts = 2 if local % (2 * repeat) == 0 and local % 512 == 0 else 1
    depth = local // parts
    total = None
    for part in range(parts):
        for at in range(part * depth, (part + 1) * depth, repeat):
            steps = []
            for row in range(at, at + repeat, 8):
                first, last = row // group, (row + 7) // group
                step = jnp.broadcast_to(scale_ref[first : first + 1, :], (8, tile))
                if last != first:
                    other = jnp.broadcast_to(scale_ref[last : last + 1, :], (8, tile))
                    step = jnp.where(low_rows < last * group - row, step, other)
                steps.append(step)
            codes = code_ref[at : at + repeat, :].astype(jnp.float32)
            weight[at : at + repeat, :] = (codes * jnp.concatenate(steps, axis=0)).astype(
                jnp.bfloat16
            )
        term = jnp.dot(
            held[:, part * depth : (part + 1) * depth],
            weight[part * depth : (part + 1) * depth, :],
            preferred_element_type=jnp.float32,
        )
        total = term if total is None else total + term
    keep_ref[...] = total[: half * rows]
    send_ref[...] = total[half * rows :].astype(jnp.bfloat16)


def down(pieces, codes, scales):
    devices = len(pieces)
    rows, local = pieces[0].shape
    width = codes.shape[1]
    blocks = scales.shape[0]
    tile = 512
    order = sorted(range(devices), key=lambda k: reversed_bits(k, devices))
    out_rows = devices // 2 * rows
    return pl.pallas_call(
        functools.partial(down_kernel, devices, local // blocks, order),
        grid=(width // tile,),
        in_specs=[pl.BlockSpec((rows, local), lambda i: (0, 0))] * devices
        + [
            pl.BlockSpec((local, tile), lambda i: (0, i)),
            pl.BlockSpec((blocks, tile), lambda i: (0, i)),
        ],
        out_specs=[pl.BlockSpec((out_rows, tile), lambda i: (0, i))] * 2,
        out_shape=[
            jax.ShapeDtypeStruct((out_rows, width), jnp.float32),
            jax.ShapeDtypeStruct((out_rows, width), jnp.bfloat16),
        ],
        scratch_shapes=[
            pltpu.VMEM((devices * rows, local), jnp.bfloat16),
            pltpu.VMEM((local, tile), jnp.bfloat16),
        ],
        compiler_params=pltpu.CompilerParams(
            dimension_semantics=("arbitrary",), vmem_limit_bytes=40 * MIB
        ),
        cost_estimate=pl.CostEstimate(
            flops=2 * devices * rows * width * local,
            bytes_accessed=2 * width * local,
            transcendentals=0,
        ),
        name="down",
    )(*pieces, codes, scales)


def sum_over_devices(keep, send):
    stride = 1
    while True:
        got = exchange(send, stride)
        total = keep + got.astype(jnp.float32)
        rows = total.shape[0]
        stride *= 2
        if stride == lax.axis_size(AXIS):
            return total
        keep, send = total[: rows // 2], total[rows // 2 :].astype(jnp.bfloat16)


def block_order(local, group):
    order = local // group
    while order > 32:
        order //= 2
    return order


def shards_piped(
    chunks, tokens, norm_gain, gate_codes, gate_scales, up_codes, up_scales, down_codes, down_scales
):
    devices = lax.axis_size(AXIS)
    local = gate_codes.shape[1]
    group = down_codes.shape[0] // down_scales.shape[0]
    table = np.kron(walsh(block_order(local, group)), hadamard_small())
    table = jnp.asarray(table.astype(ml_dtypes.bfloat16))

    grid = walsh(devices)
    both = np.stack(
        [[grid[me], [grid[me ^ k, me] for k in range(devices)]] for me in range(devices)]
    )
    signs = lax.dynamic_index_in_dim(
        jnp.asarray(both, jnp.float32), lax.axis_index(AXIS), 0, keepdims=False
    )

    own = norm(tokens, norm_gain, chunks)
    gathered = [gather_pieces(piece, devices) for piece in own]
    hidden = [
        swap_pieces(gate_up(pieces, gate_codes, gate_scales, up_codes, up_scales))
        for pieces in gathered
    ]
    rotated = [swap_pieces(rotate(pieces, signs, table)) for pieces in hidden]
    summed = [sum_over_devices(*down(pieces, down_codes, down_scales)) for pieces in rotated]
    outs = [
        (tokens[start : start + rows].astype(jnp.float32) + total).astype(jnp.bfloat16)
        for (start, rows), total in zip(chunks, summed)
    ]
    return jnp.concatenate(outs, axis=0)


def dequantize(codes, scales):
    blocks = scales.shape[0]
    height, width = codes.shape
    spread = codes.astype(jnp.float32).reshape(blocks, height // blocks, width) * scales[:, None, :]
    return spread.reshape(height, width).astype(jnp.bfloat16)


def shards_plain(
    tokens, norm_gain, gate_codes, gate_scales, up_codes, up_scales, down_codes, down_scales
):
    floated = tokens.astype(jnp.float32)
    normed = (
        floated
        * lax.rsqrt(jnp.mean(floated * floated, axis=1, keepdims=True) + EPSILON)
        * norm_gain
    ).astype(jnp.bfloat16)
    gate_weight = dequantize(gate_codes, gate_scales)
    up_weight = dequantize(up_codes, up_scales)
    down_weight = dequantize(down_codes, down_scales)
    piece = lax.all_gather(normed, AXIS, axis=0, tiled=True)
    gate = jnp.dot(piece, gate_weight, preferred_element_type=jnp.float32)
    upward = jnp.dot(piece, up_weight, preferred_element_type=jnp.float32)
    hidden = (jax.nn.silu(gate) * upward).astype(jnp.bfloat16)
    total_rows, local_width = hidden.shape
    devices = lax.axis_size(AXIS)
    local_walsh = down_scales.shape[0]
    group = down_codes.shape[0] // local_walsh
    blocks = hidden.astype(jnp.float32).reshape(total_rows, local_walsh, group)
    small_table = jnp.asarray(hadamard_small(), jnp.float32)
    local_table = jnp.asarray(walsh(local_walsh), jnp.float32)
    blocks = jnp.einsum("tia,ac->tic", blocks, small_table, precision=lax.Precision.HIGHEST)
    blocks = jnp.einsum("ji,tic->tjc", local_table, blocks, precision=lax.Precision.HIGHEST)
    blocks = blocks.reshape(total_rows, local_width)
    position = lax.axis_index(AXIS)
    for level in range(devices.bit_length() - 1):
        partner = exchange(blocks.astype(jnp.bfloat16), 1 << level).astype(blocks.dtype)
        signed = (1 - 2 * (position >> level & 1)).astype(jnp.float32)
        blocks = partner + signed * blocks
    rotated = (blocks * (devices * local_width) ** (-0.5)).astype(jnp.bfloat16)
    summed = lax.psum_scatter(
        jnp.dot(rotated, down_weight, preferred_element_type=jnp.float32),
        AXIS,
        scatter_dimension=0,
        tiled=True,
    )
    return (floated + summed).astype(jnp.bfloat16)


CHUNKS = 2


def shards(tokens, norm_gain, gate_codes, *others):
    devices = lax.axis_size(AXIS)
    rows, width = tokens.shape
    local = gate_codes.shape[1]
    if devices in (2, 4, 8) and rows % (16 * CHUNKS) == 0 and local % 896 == 0 and width % 512 == 0:
        size = rows // CHUNKS
        chunks = [(index * size, size) for index in range(CHUNKS)]
        return shards_piped(chunks, tokens, norm_gain, gate_codes, *others)
    return shards_plain(tokens, norm_gain, gate_codes, *others)


def solution(mesh):
    return jax.shard_map(
        shards,
        mesh=mesh,
        in_specs=(
            P(("groups", "tensor", "dp"), None),
            P(),
            P(None, "tensor"),
            P(None, "tensor"),
            P(None, "tensor"),
            P(None, "tensor"),
            P("tensor", None),
            P("tensor", None),
        ),
        out_specs=P(("groups", "tensor", "dp"), None),
        check_vma=False,
    )
```

time: 708 us -> 333 us (0.47)
  waiting for transfers between devices: 405 us -> 118 us
  starting transfers between devices: 4.79 us -> 112 us
  local copies, waits for them, and re-layouts: 115 us -> 8.13 us
  matrix products: 105 us -> 0 us
  Pallas kernels: 0 us -> 92.4 us
  other arithmetic: 63.3 us -> 1.61 us
  between operations: 13.5 us -> 0.24 us
    reduce_scatter x1 -> x0, waiting for transfers between devices: 149 us -> none  [shards(): lax.psum_scatter(jnp.dot(piece, down_weight, preferred_element_type=jnp.f...]
    ppermute x3 -> x48, starting transfers between devices: 4.74 us -> 112 us  [exchange(): lax.ppermute(value, AXIS, [(i, i ^ stride) for i in range(lax.axis_size(A...]
    dot_general x5 -> x0, matrix products: 105 us -> none  [the longest x1 38.7 us: shards(): jnp.dot(piece, down_weight, preferred_element_type=jnp.float32)]
    ppermute x3 -> x48, waiting for transfers between devices: 222 us -> 118 us  [exchange(): lax.ppermute(value, AXIS, [(i, i ^ stride) for i in range(lax.axis_size(A...]
    mul x4 -> x0, local copies, waits for them, and re-layouts: 92.4 us -> none  [the longest x2 72.8 us: dequantize(): codes.astype(jnp.float32).reshape(blocks, height // blocks, width)]
    pallas_call x0 -> x7, Pallas kernels: none -> 92.4 us  [the longest x2 55.5 us: gate_up(): pl.pallas_call(functools.partial(gate_up_kernel, devices, 512, width // b...]
    convert_element_type x6 -> x1, other arithmetic: 62 us -> 0.16 us  [shards_piped(): (tokens[start:start + rows].astype(jnp.float32) + total).astype(jnp.bfloa...]
    all_gather x1 -> x0, waiting for transfers between devices: 34.3 us -> none  [shards(): piece = lax.all_gather(normed, 'tensor', axis=0, tiled=True)]
  transfers between devices with their start and end apart: 5 -> 48, of which waited for: 5 -> 16; matrix products, arithmetic and copies ran while one was open for 19% -> 0% of each run, Pallas kernels for 0% -> 28%
where the time goes in v1:
time: 333 us; the launch traced here: 332 us
  waiting for transfers between devices  118 us (35%)
  starting transfers between devices  112 us (34%)
  Pallas kernels  92.4 us (28%)
  local copies, waits for them, and re-layouts  8.13 us (2%)
    ppermute x48, waiting for transfers between devices, exchange(): lax.ppermute(value, AXIS, [(i, i ^ stride) for i in range(lax.axis_size(A...  118 us
    ppermute x48, starting transfers between devices, exchange(): lax.ppermute(value, AXIS, [(i, i ^ stride) for i in range(lax.axis_size(A...  112 us
    pallas_call x2, Pallas kernels, gate_up(): pl.pallas_call(functools.partial(gate_up_kernel, devices, 512, width // b...  55.5 us
    pallas_call x2, Pallas kernels, down(): pl.pallas_call(functools.partial(down_kernel, devices, local // blocks, o...  29.6 us
    unnamed x28, local copies, waits for them, and re-layouts  7.29 us
    pallas_call x2, Pallas kernels, rotate(): pl.pallas_call(functools.partial(rotate_kernel, devices, (devices * local...  6.99 us
  transfers between devices with their start and end apart: 48, of which 16 were waited for; matrix products, arithmetic and copies ran while one was open for 0% of the time, Pallas kernels for 28%

profile of v1, /device:TPU:0, one launch (start us, length us, event | category | flops | bytes accessed | tf_op | source)
XLA Modules:
  0.0 332.5 jit_solution(16329819907894702096)
XLA Ops:
  2.0 4.1 %collective-permute-start.27 = (bf16[32,4096]{1,0:T(8,128)(2,1)S(1)}, bf16[32,4096]{1,0:T(8,128)(2,1)S(1)}, u32[]{:S(2)}, u32[]{:S(2)}) collective-permute-start(bf16[32,4096]{1,0:T(8,128)(2,1)S(1)} %get-tuple-element.62.refs_0_), channel_id=1, source_target_pairs={{0,8},{2,10},{4,12},{6,14},{8,0},{10,2},{12,4},{14,6},{1,9},{3,11}... | collective-permute-start | bytes 786440 | tf_op jit(solution)/shard_map/ppermute | solution.py:41
  9.5 10.3 %collective-permute-done.27.refs_4_ = bf16[32,4096]{1,0:T(8,128)(2,1)S(1)} collective-permute-done((bf16[32,4096]{1,0:T(8,128)(2,1)S(1)}, bf16[32,4096]{1,0:T(8,128)(2,1)S(1)}, u32[]{:S(2)}, u32[]{:S(2)}) %collective-permute-start.27) | collective-permute-done | bytes 262176 | tf_op jit(solution)/shard_map/ppermute | solution.py:41
  21.8 5.5 %collective-permute-start.28 = (bf16[32,4096]{1,0:T(8,128)(2,1)S(1)}, bf16[32,4096]{1,0:T(8,128)(2,1)S(1)}, u32[]{:S(2)}, u32[]{:S(2)}) collective-permute-start(bf16[32,4096]{1,0:T(8,128)(2,1)S(1)} %collective-permute-done.27.refs_4_), channel_id=1, source_target_pairs={{0,2},{2,0},{4,6},{6,4},{8,10},{10,8},{12,14},{14,12},{1,3},{3,1},... | collective-permute-start | bytes 786440 | tf_op jit(solution)/shard_map/ppermute | solution.py:41
  45.9 28.1 %gate_up.3 = (bf16[32,3584]{1,0:T(8,128)(2,1)S(1)}, bf16[32,3584]{1,0:T(8,128)(2,1)}, bf16[32,3584]{1,0:T(8,128)(2,1)}, bf16[32,3584]{1,0:T(8,128)(2,1)S(1)}, bf...) custom-call(bf16[32,4096]{1,0:T(8,128)(2,1)S(1)} %get-tuple-element., ...), custom_call_target="tpu_custom_call" | custom-call | flops 15032385536 | bytes 58720256 | tf_op jit(solution)/shard_map/gate_up/pallas_call | solution.py:126
  85.4 4.1 %collective-permute-start.36 = (bf16[32,3584]{1,0:T(8,128)(2,1)}, bf16[32,3584]{1,0:T(8,128)(2,1)S(1)}, u32[]{:S(2)}, u32[]{:S(2)}) collective-permute-start(bf16[32,3584]{1,0:T(8,128)(2,1)} %copy-done.9), channel_id=1, source_target_pairs={{0,12},{2,14},{4,8},{6,10},{8,4},{10,6},{12,0},{14,2},{1,13},{3,15... | collective-permute-start | bytes 688136 | tf_op jit(solution)/shard_map/ppermute | solution.py:41
  96.3 27.5 %gate_up.2 = (bf16[32,3584]{1,0:T(8,128)(2,1)S(1)}, bf16[32,3584]{1,0:T(8,128)(2,1)S(1)}, bf16[32,3584]{1,0:T(8,128)(2,1)S(1)}, bf16[32,3584]{1,0:T(8,128)(2,1)S...) custom-call(bf16[32,4096]{1,0:T(8,128)(2,1)S(1)} %get-tuple-element., ...), custom_call_target="tpu_custom_call" | custom-call | flops 15032385536 | bytes 58720256 | tf_op jit(solution)/shard_map/gate_up/pallas_call | solution.py:126
  136.3 14.2 %collective-permute-done.10.refs_4_ = bf16[32,3584]{1,0:T(8,128)(2,1)S(1)} collective-permute-done((bf16[32,3584]{1,0:T(8,128)(2,1)S(1)}, bf16[32,3584]{1,0:T(8,128)(2,1)S(1)}, u32[]{:S(2)}, u32[]{:S(2)}) %collective-permute-start.10) | collective-permute-done | bytes 229408 | tf_op jit(solution)/shard_map/ppermute | solution.py:41
  151.3 4.6 %collective-permute-done.11.refs_5_ = bf16[32,3584]{1,0:T(8,128)(2,1)S(1)} collective-permute-done((bf16[32,3584]{1,0:T(8,128)(2,1)S(1)}, bf16[32,3584]{1,0:T(8,128)(2,1)S(1)}, u32[]{:S(2)}, u32[]{:S(2)}) %collective-permute-start.11) | collective-permute-done | bytes 229408 | tf_op jit(solution)/shard_map/ppermute | solution.py:41
  156.9 9.2 %collective-permute-start.39 = (bf16[32,3584]{1,0:T(8,128)(2,1)S(1)}, bf16[32,3584]{1,0:T(8,128)(2,1)S(1)}, u32[]{:S(2)}, u32[]{:S(2)}) collective-permute-start(bf16[32,3584]{1,0:T(8,128)(2,1)S(1)} %get-tuple-element.73), channel_id=1, source_target_pairs={{0,4},{2,6},{4,0},{6,2},{8,12},{10,14},{12,8},{14,10},{1,5},{3,7},... | collective-permute-start | bytes 688136 | tf_op jit(solution)/shard_map/ppermute | solution.py:41
  166.1 4.4 %collective-permute-start.41 = (bf16[32,3584]{1,0:T(8,128)(2,1)S(1)}, bf16[32,3584]{1,0:T(8,128)(2,1)S(1)}, u32[]{:S(2)}, u32[]{:S(2)}) collective-permute-start(bf16[32,3584]{1,0:T(8,128)(2,1)S(1)} %get-tuple-element.75), channel_id=1, source_target_pairs={{0,8},{2,10},{4,12},{6,14},{8,0},{10,2},{12,4},{14,6},{1,9},{3,11}... | collective-permute-start | bytes 688136 | tf_op jit(solution)/shard_map/ppermute | solution.py:41
  173.3 5.1 %collective-permute-done.39.refs_2_ = bf16[32,3584]{1,0:T(8,128)(2,1)S(1)} collective-permute-done((bf16[32,3584]{1,0:T(8,128)(2,1)S(1)}, bf16[32,3584]{1,0:T(8,128)(2,1)S(1)}, u32[]{:S(2)}, u32[]{:S(2)}) %collective-permute-start.39) | collective-permute-done | bytes 229408 | tf_op jit(solution)/shard_map/ppermute | solution.py:41
  178.4 3.9 %collective-permute-start.44 = (bf16[32,3584]{1,0:T(8,128)(2,1)S(1)}, bf16[32,3584]{1,0:T(8,128)(2,1)S(1)}, u32[]{:S(2)}, u32[]{:S(2)}) collective-permute-start(bf16[32,3584]{1,0:T(8,128)(2,1)S(1)} %get-tuple-element.78), channel_id=1, source_target_pairs={{0,14},{2,12},{4,10},{6,8},{8,6},{10,4},{12,2},{14,0},{1,15},{3,13... | collective-permute-start | bytes 688136 | tf_op jit(solution)/shard_map/ppermute | solution.py:41
  186.5 6.2 %collective-permute-start.15 = (bf16[32,3584]{1,0:T(8,128)(2,1)S(1)}, bf16[32,3584]{1,0:T(8,128)(2,1)S(1)}, u32[]{:S(2)}, u32[]{:S(2)}) collective-permute-start(bf16[32,3584]{1,0:T(8,128)(2,1)S(1)} %get-tuple-element.54), channel_id=1, source_target_pairs={{0,4},{2,6},{4,0},{6,2},{8,12},{10,14},{12,8},{14,10},{1,5},{3,7},... | collective-permute-start | bytes 688136 | tf_op jit(solution)/shard_map/ppermute | solution.py:41
  192.7 9.3 %collective-permute-done.42.refs_5_ = bf16[32,3584]{1,0:T(8,128)(2,1)S(1)} collective-permute-done((bf16[32,3584]{1,0:T(8,128)(2,1)S(1)}, bf16[32,3584]{1,0:T(8,128)(2,1)S(1)}, u32[]{:S(2)}, u32[]{:S(2)}) %collective-permute-start.42) | collective-permute-done | bytes 229408 | tf_op jit(solution)/shard_map/ppermute | solution.py:41
  202.0 14.7 %down.3 = (f32[128,4096]{1,0:T(8,128)S(1)}, bf16[128,4096]{1,0:T(8,128)(2,1)S(1)}) custom-call(bf16[32,3584]{1,0:T(8,128)(2,1)S(1)} %get-tuple-element.71.refs_0_, bf16[32,3584]{1,0:T(8,128)(2,1)S(1)} %collective-permute-done.38.refs_1_, bf16[32,3584]{1,0:T(8,128)(2,1)S(1)} %collective-permute-done.39.refs_2_, ...), custom_call_target="tpu_custom_call" | custom-call | flops 7516192768 | bytes 29360128 | tf_op jit(solution)/shard_map/down/pallas_call | solution.py:253
  217.7 10.1 %collective-permute-start.17 = (bf16[32,3584]{1,0:T(8,128)(2,1)S(1)}, bf16[32,3584]{1,0:T(8,128)(2,1)S(1)}, u32[]{:S(2)}, u32[]{:S(2)}) collective-permute-start(bf16[32,3584]{1,0:T(8,128)(2,1)S(1)} %get-tuple-element.56), channel_id=1, source_target_pairs={{0,8},{2,10},{4,12},{6,14},{8,0},{10,2},{12,4},{14,6},{1,9},{3,11}... | collective-permute-start | bytes 688136 | tf_op jit(solution)/shard_map/ppermute | solution.py:41
  232.5 17.4 %collective-permute-done.17.refs_4_ = bf16[32,3584]{1,0:T(8,128)(2,1)S(1)} collective-permute-done((bf16[32,3584]{1,0:T(8,128)(2,1)S(1)}, bf16[32,3584]{1,0:T(8,128)(2,1)S(1)}, u32[]{:S(2)}, u32[]{:S(2)}) %collective-permute-start.17) | collective-permute-done | bytes 229408 | tf_op jit(solution)/shard_map/ppermute | solution.py:41
  249.9 5.9 %collective-permute-done.18.refs_5_ = bf16[32,3584]{1,0:T(8,128)(2,1)S(1)} collective-permute-done((bf16[32,3584]{1,0:T(8,128)(2,1)S(1)}, bf16[32,3584]{1,0:T(8,128)(2,1)S(1)}, u32[]{:S(2)}, u32[]{:S(2)}) %collective-permute-start.18) | collective-permute-done | bytes 229408 | tf_op jit(solution)/shard_map/ppermute | solution.py:41
  255.9 14.9 %down.2 = (f32[128,4096]{1,0:T(8,128)S(1)}, bf16[128,4096]{1,0:T(8,128)(2,1)S(1)}) custom-call(bf16[32,3584]{1,0:T(8,128)(2,1)S(1)} %get-tuple-element.52.refs_0_, bf16[32,3584]{1,0:T(8,128)(2,1)S(1)} %collective-permute-done.14.refs_1_, bf16[32,3584]{1,0:T(8,128)(2,1)S(1)} %collective-permute-done.15.refs_2_, ...), custom_call_target="tpu_custom_call" | custom-call | flops 7516192768 | bytes 29360128 | tf_op jit(solution)/shard_map/down/pallas_call | solution.py:253
  271.5 9.4 %collective-permute-start.46 = (bf16[64,4096]{1,0:T(8,128)(2,1)S(1)}, bf16[64,4096]{1,0:T(8,128)(2,1)S(1)}, u32[]{:S(2)}, u32[]{:S(2)}) collective-permute-start(bf16[64,4096]{1,0:T(8,128)(2,1)S(1)} %slice.70), channel_id=1, source_target_pairs={{0,4},{2,6},{4,0},{6,2},{8,12},{10,14},{12,8},{14,10},{1,5},{3,7},... | collective-permute-start | bytes 1572872 | tf_op jit(solution)/shard_map/ppermute | solution.py:41
  280.9 12.0 %collective-permute-done.21 = bf16[128,4096]{1,0:T(8,128)(2,1)S(1)} collective-permute-done((bf16[128,4096]{1,0:T(8,128)(2,1)S(1)}, bf16[128,4096]{1,0:T(8,128)(2,1)S(1)}, u32[]{:S(2)}, u32[]{:S(2)}) %collective-permute-start.21) | collective-permute-done | bytes 1048608 | tf_op jit(solution)/shard_map/ppermute | solution.py:41
  293.2 10.3 %collective-permute-start.22 = (bf16[64,4096]{1,0:T(8,128)(2,1)S(1)}, bf16[64,4096]{1,0:T(8,128)(2,1)S(1)}, u32[]{:S(2)}, u32[]{:S(2)}) collective-permute-start(bf16[64,4096]{1,0:T(8,128)(2,1)S(1)} %slice.71), channel_id=1, source_target_pairs={{0,4},{2,6},{4,0},{6,2},{8,12},{10,14},{12,8},{14,10},{1,5},{3,7},... | collective-permute-start | bytes 1572872 | tf_op jit(solution)/shard_map/ppermute | solution.py:41
  304.0 15.5 %collective-permute-done.22 = bf16[64,4096]{1,0:T(8,128)(2,1)S(1)} collective-permute-done((bf16[64,4096]{1,0:T(8,128)(2,1)S(1)}, bf16[64,4096]{1,0:T(8,128)(2,1)S(1)}, u32[]{:S(2)}, u32[]{:S(2)}) %collective-permute-start.22) | collective-permute-done | bytes 524320 | tf_op jit(solution)/shard_map/ppermute | solution.py:41
  319.8 11.7 %collective-permute-done.23 = bf16[32,4096]{1,0:T(8,128)(2,1)S(1)} collective-permute-done((bf16[32,4096]{1,0:T(8,128)(2,1)S(1)}, bf16[32,4096]{1,0:T(8,128)(2,1)S(1)}, u32[]{:S(2)}, u32[]{:S(2)}) %collective-permute-start.23) | collective-permute-done | bytes 262176 | tf_op jit(solution)/shard_map/ppermute | solution.py:41
  (118 shorter events, 73.8 us)
Async XLA Ops:
  38.8 40.7 %collective-permute-start = (bf16[32,4096]{1,0:T(8,128)(2,1)S(1)}, bf16[32,4096]{1,0:T(8,128)(2,1)S(1)}, u32[]{:S(2)}, u32[]{:S(2)}) collective-permute-start(bf16[32,4096]{1,0:T(8,128)(2,1)S(1)} %get-tuple-element.43.refs_0_), channel_id=1, source_target_pairs={{0,2},{2,0},{4,6},{6,4},{8,10},{10,8},{12,14},{14,12},{1,3},{3,1},... | collective-permute-start | bytes 786440 | tf_op jit(solution)/shard_map/ppermute | solution.py:41
  40.4 39.1 %collective-permute-start.4 = (bf16[32,4096]{1,0:T(8,128)(2,1)S(1)}, bf16[32,4096]{1,0:T(8,128)(2,1)S(1)}, u32[]{:S(2)}, u32[]{:S(2)}) collective-permute-start(bf16[32,4096]{1,0:T(8,128)(2,1)S(1)} %collective-permute-done.3.refs_4_), channel_id=1, source_target_pairs={{0,2},{2,0},{4,6},{6,4},{8,10},{10,8},{12,14},{14,12},{1,3},{3,1},... | collective-permute-start | bytes 786440 | tf_op jit(solution)/shard_map/ppermute | solution.py:41
  40.9 40.1 %collective-permute-start.2 = (bf16[32,4096]{1,0:T(8,128)(2,1)S(1)}, bf16[32,4096]{1,0:T(8,128)(2,1)S(1)}, u32[]{:S(2)}, u32[]{:S(2)}) collective-permute-start(bf16[32,4096]{1,0:T(8,128)(2,1)S(1)} %collective-permute-done.1.refs_2_), channel_id=1, source_target_pairs={{0,2},{2,0},{4,6},{6,4},{8,10},{10,8},{12,14},{14,12},{1,3},{3,1},... | collective-permute-start | bytes 786440 | tf_op jit(solution)/shard_map/ppermute | solution.py:41
  42.4 42.3 %collective-permute-start.6 = (bf16[32,4096]{1,0:T(8,128)(2,1)S(1)}, bf16[32,4096]{1,0:T(8,128)(2,1)S(1)}, u32[]{:S(2)}, u32[]{:S(2)}) collective-permute-start(bf16[32,4096]{1,0:T(8,128)(2,1)S(1)} %collective-permute-done.5.refs_6_), channel_id=1, source_target_pairs={{0,2},{2,0},{4,6},{6,4},{8,10},{10,8},{12,14},{14,12},{1,3},{3,1},... | collective-permute-start | bytes 786440 | tf_op jit(solution)/shard_map/ppermute | solution.py:41
  79.5 44.3 %collective-permute-start.33 = (bf16[32,3584]{1,0:T(8,128)(2,1)}, bf16[32,3584]{1,0:T(8,128)(2,1)S(1)}, u32[]{:S(2)}, u32[]{:S(2)}) collective-permute-start(bf16[32,3584]{1,0:T(8,128)(2,1)} %copy-done.12), channel_id=1, source_target_pairs={{0,6},{2,4},{4,2},{6,0},{8,14},{10,12},{12,10},{14,8},{1,7},{3,5},... | collective-permute-start | bytes 688136 | tf_op jit(solution)/shard_map/ppermute | solution.py:41
  81.0 42.9 %collective-permute-start.34 = (bf16[32,3584]{1,0:T(8,128)(2,1)}, bf16[32,3584]{1,0:T(8,128)(2,1)S(1)}, u32[]{:S(2)}, u32[]{:S(2)}) collective-permute-start(bf16[32,3584]{1,0:T(8,128)(2,1)} %copy-done.11), channel_id=1, source_target_pairs={{0,8},{2,10},{4,12},{6,14},{8,0},{10,2},{12,4},{14,6},{1,9},{3,11}... | collective-permute-start | bytes 688136 | tf_op jit(solution)/shard_map/ppermute | solution.py:41
  84.7 41.9 %collective-permute-start.35 = (bf16[32,3584]{1,0:T(8,128)(2,1)}, bf16[32,3584]{1,0:T(8,128)(2,1)S(1)}, u32[]{:S(2)}, u32[]{:S(2)}) collective-permute-start(bf16[32,3584]{1,0:T(8,128)(2,1)} %copy-done.10), channel_id=1, source_target_pairs={{0,10},{2,8},{4,14},{6,12},{8,2},{10,0},{12,6},{14,4},{1,11},{3,9}... | collective-permute-start | bytes 688136 | tf_op jit(solution)/shard_map/ppermute | solution.py:41
  85.4 43.1 %collective-permute-start.36 = (bf16[32,3584]{1,0:T(8,128)(2,1)}, bf16[32,3584]{1,0:T(8,128)(2,1)S(1)}, u32[]{:S(2)}, u32[]{:S(2)}) collective-permute-start(bf16[32,3584]{1,0:T(8,128)(2,1)} %copy-done.9), channel_id=1, source_target_pairs={{0,12},{2,14},{4,8},{6,10},{8,4},{10,6},{12,0},{14,2},{1,13},{3,15... | collective-permute-start | bytes 688136 | tf_op jit(solution)/shard_map/ppermute | solution.py:41
  93.3 38.9 %collective-permute-start.37 = (bf16[32,3584]{1,0:T(8,128)(2,1)}, bf16[32,3584]{1,0:T(8,128)(2,1)S(1)}, u32[]{:S(2)}, u32[]{:S(2)}) collective-permute-start(bf16[32,3584]{1,0:T(8,128)(2,1)} %copy-done.8), channel_id=1, source_target_pairs={{0,14},{2,12},{4,10},{6,8},{8,6},{10,4},{12,2},{14,0},{1,15},{3,13... | collective-permute-start | bytes 688136 | tf_op jit(solution)/shard_map/ppermute | solution.py:41
  123.8 26.7 %collective-permute-start.10 = (bf16[32,3584]{1,0:T(8,128)(2,1)S(1)}, bf16[32,3584]{1,0:T(8,128)(2,1)S(1)}, u32[]{:S(2)}, u32[]{:S(2)}) collective-permute-start(bf16[32,3584]{1,0:T(8,128)(2,1)S(1)} %get-tuple-element.48), channel_id=1, source_target_pairs={{0,8},{2,10},{4,12},{6,14},{8,0},{10,2},{12,4},{14,6},{1,9},{3,11}... | collective-permute-start | bytes 688136 | tf_op jit(solution)/shard_map/ppermute | solution.py:41
  123.8 32.1 %collective-permute-start.11 = (bf16[32,3584]{1,0:T(8,128)(2,1)S(1)}, bf16[32,3584]{1,0:T(8,128)(2,1)S(1)}, u32[]{:S(2)}, u32[]{:S(2)}) collective-permute-start(bf16[32,3584]{1,0:T(8,128)(2,1)S(1)} %get-tuple-element.49), channel_id=1, source_target_pairs={{0,10},{2,8},{4,14},{6,12},{8,2},{10,0},{12,6},{14,4},{1,11},{3,9}... | collective-permute-start | bytes 688136 | tf_op jit(solution)/shard_map/ppermute | solution.py:41
  126.6 29.3 %collective-permute-start.12 = (bf16[32,3584]{1,0:T(8,128)(2,1)S(1)}, bf16[32,3584]{1,0:T(8,128)(2,1)S(1)}, u32[]{:S(2)}, u32[]{:S(2)}) collective-permute-start(bf16[32,3584]{1,0:T(8,128)(2,1)S(1)} %get-tuple-element.50), channel_id=1, source_target_pairs={{0,12},{2,14},{4,8},{6,10},{8,4},{10,6},{12,0},{14,2},{1,13},{3,15... | collective-permute-start | bytes 688136 | tf_op jit(solution)/shard_map/ppermute | solution.py:41
  128.5 28.4 %collective-permute-start.13 = (bf16[32,3584]{1,0:T(8,128)(2,1)S(1)}, bf16[32,3584]{1,0:T(8,128)(2,1)S(1)}, u32[]{:S(2)}, u32[]{:S(2)}) collective-permute-start(bf16[32,3584]{1,0:T(8,128)(2,1)S(1)} %get-tuple-element.51), channel_id=1, source_target_pairs={{0,14},{2,12},{4,10},{6,8},{8,6},{10,4},{12,2},{14,0},{1,15},{3,13... | collective-permute-start | bytes 688136 | tf_op jit(solution)/shard_map/ppermute | solution.py:41
  132.2 33.9 %collective-permute-start.7 = (bf16[32,3584]{1,0:T(8,128)(2,1)S(1)}, bf16[32,3584]{1,0:T(8,128)(2,1)S(1)}, u32[]{:S(2)}, u32[]{:S(2)}) collective-permute-start(bf16[32,3584]{1,0:T(8,128)(2,1)S(1)} %get-tuple-element.45), channel_id=1, source_target_pairs={{0,2},{2,0},{4,6},{6,4},{8,10},{10,8},{12,14},{14,12},{1,3},{3,1},... | collective-permute-start | bytes 688136 | tf_op jit(solution)/shard_map/ppermute | solution.py:41
  170.4 31.6 %collective-permute-start.42 = (bf16[32,3584]{1,0:T(8,128)(2,1)S(1)}, bf16[32,3584]{1,0:T(8,128)(2,1)S(1)}, u32[]{:S(2)}, u32[]{:S(2)}) collective-permute-start(bf16[32,3584]{1,0:T(8,128)(2,1)S(1)} %get-tuple-element.76), channel_id=1, source_target_pairs={{0,10},{2,8},{4,14},{6,12},{8,2},{10,0},{12,6},{14,4},{1,11},{3,9}... | collective-permute-start | bytes 688136 | tf_op jit(solution)/shard_map/ppermute | solution.py:41
  171.0 31.0 %collective-permute-start.43 = (bf16[32,3584]{1,0:T(8,128)(2,1)S(1)}, bf16[32,3584]{1,0:T(8,128)(2,1)S(1)}, u32[]{:S(2)}, u32[]{:S(2)}) collective-permute-start(bf16[32,3584]{1,0:T(8,128)(2,1)S(1)} %get-tuple-element.77), channel_id=1, source_target_pairs={{0,12},{2,14},{4,8},{6,10},{8,4},{10,6},{12,0},{14,2},{1,13},{3,15... | collective-permute-start | bytes 688136 | tf_op jit(solution)/shard_map/ppermute | solution.py:41
  185.7 42.1 %collective-permute-start.14 = (bf16[32,3584]{1,0:T(8,128)(2,1)S(1)}, bf16[32,3584]{1,0:T(8,128)(2,1)S(1)}, u32[]{:S(2)}, u32[]{:S(2)}) collective-permute-start(bf16[32,3584]{1,0:T(8,128)(2,1)S(1)} %get-tuple-element.53), channel_id=1, source_target_pairs={{0,2},{2,0},{4,6},{6,4},{8,10},{10,8},{12,14},{14,12},{1,3},{3,1},... | collective-permute-start | bytes 688136 | tf_op jit(solution)/shard_map/ppermute | solution.py:41
  186.5 41.4 %collective-permute-start.15 = (bf16[32,3584]{1,0:T(8,128)(2,1)S(1)}, bf16[32,3584]{1,0:T(8,128)(2,1)S(1)}, u32[]{:S(2)}, u32[]{:S(2)}) collective-permute-start(bf16[32,3584]{1,0:T(8,128)(2,1)S(1)} %get-tuple-element.54), channel_id=1, source_target_pairs={{0,4},{2,6},{4,0},{6,2},{8,12},{10,14},{12,8},{14,10},{1,5},{3,7},... | collective-permute-start | bytes 688136 | tf_op jit(solution)/shard_map/ppermute | solution.py:41
  202.0 27.9 %collective-permute-start.16 = (bf16[32,3584]{1,0:T(8,128)(2,1)S(1)}, bf16[32,3584]{1,0:T(8,128)(2,1)S(1)}, u32[]{:S(2)}, u32[]{:S(2)}) collective-permute-start(bf16[32,3584]{1,0:T(8,128)(2,1)S(1)} %get-tuple-element.55), channel_id=1, source_target_pairs={{0,6},{2,4},{4,2},{6,0},{8,14},{10,12},{12,10},{14,8},{1,7},{3,5},... | collective-permute-start | bytes 688136 | tf_op jit(solution)/shard_map/ppermute | solution.py:41
  216.8 54.5 %collective-permute-start.45 = (bf16[128,4096]{1,0:T(8,128)(2,1)S(1)}, bf16[128,4096]{1,0:T(8,128)(2,1)S(1)}, u32[]{:S(2)}, u32[]{:S(2)}) collective-permute-start(bf16[128,4096]{1,0:T(8,128)(2,1)S(1)} %get-tuple-element.80), channel_id=1, source_target_pairs={{0,2},{2,0},{4,6},{6,4},{8,10},{10,8},{12,14},{14,12},{1,3},{3,1},... | collective-permute-start | bytes 3145736 | tf_op jit(solution)/shard_map/ppermute | solution.py:41
  217.7 32.2 %collective-permute-start.17 = (bf16[32,3584]{1,0:T(8,128)(2,1)S(1)}, bf16[32,3584]{1,0:T(8,128)(2,1)S(1)}, u32[]{:S(2)}, u32[]{:S(2)}) collective-permute-start(bf16[32,3584]{1,0:T(8,128)(2,1)S(1)} %get-tuple-element.56), channel_id=1, source_target_pairs={{0,8},{2,10},{4,12},{6,14},{8,0},{10,2},{12,4},{14,6},{1,9},{3,11}... | collective-permute-start | bytes 688136 | tf_op jit(solution)/shard_map/ppermute | solution.py:41
  227.8 28.1 %collective-permute-start.18 = (bf16[32,3584]{1,0:T(8,128)(2,1)S(1)}, bf16[32,3584]{1,0:T(8,128)(2,1)S(1)}, u32[]{:S(2)}, u32[]{:S(2)}) collective-permute-start(bf16[32,3584]{1,0:T(8,128)(2,1)S(1)} %get-tuple-element.57), channel_id=1, source_target_pairs={{0,10},{2,8},{4,14},{6,12},{8,2},{10,0},{12,6},{14,4},{1,11},{3,9}... | collective-permute-start | bytes 688136 | tf_op jit(solution)/shard_map/ppermute | solution.py:41
  227.9 28.0 %collective-permute-start.19 = (bf16[32,3584]{1,0:T(8,128)(2,1)S(1)}, bf16[32,3584]{1,0:T(8,128)(2,1)S(1)}, u32[]{:S(2)}, u32[]{:S(2)}) collective-permute-start(bf16[32,3584]{1,0:T(8,128)(2,1)S(1)} %get-tuple-element.58), channel_id=1, source_target_pairs={{0,12},{2,14},{4,8},{6,10},{8,4},{10,6},{12,0},{14,2},{1,13},{3,15... | collective-permute-start | bytes 688136 | tf_op jit(solution)/shard_map/ppermute | solution.py:41
  271.5 32.0 %collective-permute-start.46 = (bf16[64,4096]{1,0:T(8,128)(2,1)S(1)}, bf16[64,4096]{1,0:T(8,128)(2,1)S(1)}, u32[]{:S(2)}, u32[]{:S(2)}) collective-permute-start(bf16[64,4096]{1,0:T(8,128)(2,1)S(1)} %slice.70), channel_id=1, source_target_pairs={{0,4},{2,6},{4,0},{6,2},{8,12},{10,14},{12,8},{14,10},{1,5},{3,7},... | collective-permute-start | bytes 1572872 | tf_op jit(solution)/shard_map/ppermute | solution.py:41
  (38 other events, 654.7 us)

commit v2 on v1

v2 whole, which is shorter than its diff:
```python
import functools
import math

import jax
import jax.numpy as jnp
import ml_dtypes
import numpy as np
from jax import lax
from jax.experimental import pallas as pl
from jax.experimental.pallas import tpu as pltpu
from jax.sharding import PartitionSpec as P

EPSILON = 1e-05
AXIS = "tensor"
MIB = 1 << 20


def hadamard_small():
    modulus = 13
    residues = [number * number % modulus for number in range(1, modulus)]
    legendre = [0] + [1 if number in residues else -1 for number in range(1, modulus)]
    conference = np.zeros((modulus + 1, modulus + 1), np.int64)
    conference[0, 1:] = 1
    conference[1:, 0] = 1
    for row in range(1, modulus + 1):
        for column in range(1, modulus + 1):
            conference[row, column] = legendre[(column - row) % modulus]
    plus_block = np.array([[1, 1], [1, -1]])
    zero_block = np.array([[1, -1], [-1, -1]])
    return np.kron(conference, plus_block) + np.kron(np.eye(modulus + 1, dtype=np.int64), zero_block)


def walsh(order):
    table = np.ones((1, 1), np.int64)
    while table.shape[0] < order:
        table = np.kron(np.array([[1, 1], [1, -1]]), table)
    return table


def exchange(value, stride):
    return lax.ppermute(value, AXIS, [(i, i ^ stride) for i in range(lax.axis_size(AXIS))])


def after(value, *earlier):
    return lax.optimization_barrier((value, earlier))[0]


def reversed_bits(k, devices):
    levels = devices.bit_length() - 1
    return sum(((k >> level) & 1) << (levels - 1 - level) for level in range(levels))


def gather_tree(own, devices):
    pieces = {0: own}
    for k in sorted(range(1, devices), key=lambda k: (bin(k).count("1"), -k)):
        low = k & -k
        pieces[k] = exchange(pieces[k ^ low], low)
    return [(pieces[k], 0) for k in range(devices)]


def gather_step(held, stride):
    return jnp.concatenate([held, exchange(held, stride)], axis=0)


def gathered_pieces(near, far, devices, rows, start):
    half = devices // 2
    places = [reversed_bits(k, devices) for k in range(devices)]
    return [
        (near, place * rows + start) if place < half else (far, (place - half) * rows + start)
        for place in places
    ]


def swap_far(arrays):
    out = list(arrays)
    for j in range(len(arrays) - 1, 0, -1):
        out[j] = exchange(arrays[j], 2 * j)
    return out


def swap_near(arrays):
    rows = arrays[0].shape[0] // 2
    came = exchange(jnp.concatenate([array[rows:] for array in arrays], axis=0), 1)
    pieces = []
    for j, array in enumerate(arrays):
        pieces += [(array, 0), (came, j * rows)]
    return pieces


def swap_direct(arrays):
    out = list(arrays)
    for k in range(len(arrays) - 1, 0, -1):
        out[k] = exchange(arrays[k], k)
    return [(array, 0) for array in out]


def distinct(pieces):
    arrays, places = [], []
    for array, start in pieces:
        at = next((i for i, other in enumerate(arrays) if other is array), len(arrays))
        if at == len(arrays):
            arrays.append(array)
        places.append((at, start))
    return arrays, places


def whole_blocks(arrays):
    return [pl.BlockSpec(array.shape, lambda i: (0, 0)) for array in arrays]


def norm_kernel(cuts, tokens_ref, gain_ref, *out_refs):
    floated = tokens_ref[...].astype(jnp.float32)
    inverse = lax.rsqrt(jnp.mean(floated * floated, axis=1, keepdims=True) + EPSILON)
    normed = (floated * inverse * gain_ref[...]).astype(jnp.bfloat16)
    for (start, rows), out_ref in zip(cuts, out_refs):
        out_ref[...] = normed[start : start + rows]


def norm(tokens, gain, cuts):
    rows, width = tokens.shape
    return pl.pallas_call(
        functools.partial(norm_kernel, cuts),
        out_shape=[jax.ShapeDtypeStruct((count, width), jnp.bfloat16) for _, count in cuts],
        compiler_params=pltpu.CompilerParams(vmem_limit_bytes=16 * MIB),
        cost_estimate=pl.CostEstimate(
            flops=5 * rows * width, bytes_accessed=4 * rows * width, transcendentals=rows
        ),
        name="norm",
    )(tokens, gain.reshape(1, width))


def gate_up_kernel(places, rows, depth, qblock, ins, *refs):
    devices = len(places)
    piece_refs = refs[:ins]
    gate_ref, gate_scale_ref, up_ref, up_scale_ref = refs[ins : ins + 4]
    out_refs = refs[ins + 4 : -1]
    held = refs[-1]

    @pl.when(pl.program_id(0) == 0)
    def _():
        for k, (at, start) in enumerate(places):
            held[k * rows : (k + 1) * rows, :] = piece_refs[at][start : start + rows, :]

    def weight(code_ref, scales, at):
        parts = []
        for block in range(at // qblock, (at + depth) // qblock):
            codes = code_ref[block * qblock : (block + 1) * qblock, :]
            parts.append(codes * scales[block : block + 1, :])
        return jnp.concatenate(parts, axis=0)

    gate_scales = gate_scale_ref[...].astype(jnp.bfloat16)
    up_scales = up_scale_ref[...].astype(jnp.bfloat16)
    gate = up = None
    for at in range(0, gate_ref.shape[0], depth):
        left = held[:, at : at + depth]
        term = jnp.dot(left, weight(gate_ref, gate_scales, at), preferred_element_type=jnp.float32)
        gate = term if gate is None else gate + term
        term = jnp.dot(left, weight(up_ref, up_scales, at), preferred_element_type=jnp.float32)
        up = term if up is None else up + term
    hidden = (gate / (1.0 + jnp.exp(-gate)) * up).astype(jnp.bfloat16)
    per = devices // len(out_refs)
    for index, out_ref in enumerate(out_refs):
        out_ref[...] = hidden[index * per * rows : (index + 1) * per * rows]


def gate_up(pieces, rows, per, gate_codes, gate_scales, up_codes, up_scales):
    devices = len(pieces)
    arrays, places = distinct(pieces)
    width, local = gate_codes.shape
    blocks = gate_scales.shape[0]
    tile = 256
    codes = pl.BlockSpec((width, tile), lambda i: (0, i))
    scales = pl.BlockSpec((blocks, tile), lambda i: (0, i))
    return pl.pallas_call(
        functools.partial(gate_up_kernel, places, rows, 1024, width // blocks, len(arrays)),
        grid=(local // tile,),
        in_specs=whole_blocks(arrays) + [codes, scales, codes, scales],
        out_specs=[pl.BlockSpec((per * rows, tile), lambda i: (0, i))] * (devices // per),
        out_shape=[jax.ShapeDtypeStruct((per * rows, local), jnp.bfloat16)] * (devices // per),
        scratch_shapes=[pltpu.VMEM((devices * rows, width), jnp.bfloat16)],
        compiler_params=pltpu.CompilerParams(
            dimension_semantics=("arbitrary",), vmem_limit_bytes=40 * MIB
        ),
        cost_estimate=pl.CostEstimate(
            flops=4 * devices * rows * width * local,
            bytes_accessed=4 * width * local,
            transcendentals=devices * rows * local,
        ),
        name="gate_up",
    )(*arrays, gate_codes, gate_scales, up_codes, up_scales)


def rotate_kernel(places, rows, factor, ins, sign_ref, *refs):
    devices = len(places)
    piece_refs = refs[:ins]
    table_ref = refs[ins]
    out_refs = refs[ins + 1 : -1]
    held = refs[-1]
    local = piece_refs[0].shape[1]
    block = table_ref.shape[0]
    inner = local // block
    count = devices * inner
    per = devices // len(out_refs)
    for k, (source, start) in enumerate(places):
        sign = sign_ref[0, k].astype(jnp.bfloat16)
        for q in range(inner):
            at = (k * inner + q) * rows
            held[at : at + rows, :] = (
                piece_refs[source][start : start + rows, q * block : (q + 1) * block] * sign
            )
    for start in range(0, block, 256):
        stop = min(start + 256, block)
        product = jnp.dot(
            held[...], table_ref[:, start:stop], preferred_element_type=jnp.float32
        )
        values = [product[index * rows : (index + 1) * rows] for index in range(count)]
        stride = 1
        while stride < count:
            values = [
                values[index] + values[index ^ stride]
                if not index & stride
                else values[index ^ stride] - values[index]
                for index in range(count)
            ]
            stride *= 2
        for k in range(devices):
            scale = sign_ref[1, k] * factor
            low = (k % per) * rows
            for q in range(inner):
                out_refs[k // per][low : low + rows, q * block + start : q * block + stop] = (
                    values[k * inner + q] * scale
                ).astype(jnp.bfloat16)


def rotate(pieces, rows, per, signs, table):
    devices = len(pieces)
    arrays, places = distinct(pieces)
    local = arrays[0].shape[1]
    block = table.shape[0]
    vmem = pl.BlockSpec(memory_space=pltpu.VMEM)
    return pl.pallas_call(
        functools.partial(rotate_kernel, places, rows, (devices * local) ** (-0.5), len(arrays)),
        in_specs=[pl.BlockSpec(memory_space=pltpu.SMEM)] + [vmem] * (len(arrays) + 1),
        out_specs=[vmem] * (devices // per),
        out_shape=[jax.ShapeDtypeStruct((per * rows, local), jnp.bfloat16)] * (devices // per),
        scratch_shapes=[pltpu.VMEM((devices * rows * local // block, block), jnp.bfloat16)],
        compiler_params=pltpu.CompilerParams(vmem_limit_bytes=40 * MIB),
        cost_estimate=pl.CostEstimate(
            flops=2 * devices * rows * local * block,
            bytes_accessed=4 * devices * rows * local,
            transcendentals=0,
        ),
        name="rotate",
    )(signs, *arrays, table)


def down_kernel(places, rows, group, order, ins, *refs):
    devices = len(places)
    piece_refs = refs[:ins]
    code_ref, scale_ref, keep_ref, send_ref, held, weight = refs[ins:]
    half = devices // 2

    @pl.when(pl.program_id(0) == 0)
    def _():
        for place, k in enumerate(order):
            at, start = places[k]
            held[place * rows : (place + 1) * rows, :] = piece_refs[at][start : start + rows, :]

    local, tile = code_ref.shape
    pack = 16
    repeat = math.lcm(group, pack)
    pack_rows = lax.broadcasted_iota(jnp.int32, (pack, tile), 0)
    scales = scale_ref[...].astype(jnp.bfloat16)
    masks = {}

    def first_rows(cut):
        if cut not in masks:
            mask = jnp.where(pack_rows < cut, 1.0, 0.0)
            masks[cut] = (mask.astype(jnp.bfloat16), (1.0 - mask).astype(jnp.bfloat16))
        return masks[cut]

    parts = 2 if local % (2 * repeat) == 0 and local % 512 == 0 else 1
    depth = local // parts
    total = None
    for part in range(parts):
        for at in range(part * depth, (part + 1) * depth, repeat):
            steps = []
            for row in range(at, at + repeat, pack):
                first, last = row // group, (row + pack - 1) // group
                step = jnp.broadcast_to(scales[first : first + 1, :], (pack, tile))
                if last != first:
                    head, rest = first_rows(last * group - row)
                    step = step * head + scales[last : last + 1, :] * rest
                steps.append(step)
            weight[at : at + repeat, :] = code_ref[at : at + repeat, :] * jnp.concatenate(
                steps, axis=0
            )
        term = jnp.dot(
            held[:, part * depth : (part + 1) * depth],
            weight[part * depth : (part + 1) * depth, :],
            preferred_element_type=jnp.float32,
        )
        total = term if total is None else total + term
    keep_ref[...] = total[: half * rows]
    send_ref[...] = total[half * rows :].astype(jnp.bfloat16)


def down(pieces, rows, strides, first_column, columns, codes, scales):
    devices = len(pieces)
    arrays, places = distinct(pieces)
    local = codes.shape[0]
    blocks = scales.shape[0]
    tile = 512
    skip = first_column // tile
    levels = len(strides)
    order = sorted(
        range(devices),
        key=lambda k: sum(1 << (levels - 1 - i) for i, stride in enumerate(strides) if k & stride),
    )
    out_rows = devices // 2 * rows
    return pl.pallas_call(
        functools.partial(down_kernel, places, rows, local // blocks, order, len(arrays)),
        grid=(columns // tile,),
        in_specs=whole_blocks(arrays)
        + [
            pl.BlockSpec((local, tile), lambda i: (0, i + skip)),
            pl.BlockSpec((blocks, tile), lambda i: (0, i + skip)),
        ],
        out_specs=[pl.BlockSpec((out_rows, tile), lambda i: (0, i))] * 2,
        out_shape=[
            jax.ShapeDtypeStruct((out_rows, columns), jnp.float32),
            jax.ShapeDtypeStruct((out_rows, columns), jnp.bfloat16),
        ],
        scratch_shapes=[
            pltpu.VMEM((devices * rows, local), jnp.bfloat16),
            pltpu.VMEM((local, tile), jnp.bfloat16),
        ],
        compiler_params=pltpu.CompilerParams(
            dimension_semantics=("arbitrary",), vmem_limit_bytes=40 * MIB
        ),
        cost_estimate=pl.CostEstimate(
            flops=2 * devices * rows * columns * local,
            bytes_accessed=2 * columns * local,
            transcendentals=0,
        ),
        name="down",
    )(*arrays, codes, scales)


def add_step(keep, send, stride):
    total = keep + exchange(send, stride).astype(jnp.float32)
    return total


def split_step(total):
    half = total.shape[0] // 2
    return total[:half], total[half:].astype(jnp.bfloat16)


def block_order(local, group):
    order = local // group
    while order > 32:
        order //= 2
    return order


def shards_piped(
    tokens, norm_gain, gate_codes, gate_scales, up_codes, up_scales, down_codes, down_scales
):
    devices = lax.axis_size(AXIS)
    width = tokens.shape[1]
    local = gate_codes.shape[1]
    group = down_codes.shape[0] // down_scales.shape[0]
    rows = tokens.shape[0] // 4
    table = np.kron(walsh(block_order(local, group)), hadamard_small())
    table = jnp.asarray(table.astype(ml_dtypes.bfloat16))

    grid = walsh(devices)
    both = np.stack(
        [[grid[me], [grid[me ^ k, me] for k in range(devices)]] for me in range(devices)]
    )
    signs = lax.dynamic_index_in_dim(
        jnp.asarray(both, jnp.float32), lax.axis_index(AXIS), 0, keepdims=False
    )
    strides = [1 << level for level in range(devices.bit_length() - 1)]
    weights = (gate_codes, gate_scales, up_codes, up_scales)

    own = norm(tokens, norm_gain, [(0, rows), (rows, rows), (2 * rows, 2 * rows)])
    pieces = [None] * 4
    pieces[0] = gather_tree(own[0], devices)
    pieces[1] = gather_tree(own[1], devices)
    late = after(own[2], pieces[0][-1][0])

    hidden, rotated, sums = [None] * 4, [None] * 4, [None] * 4
    last = None

    def expand(c):
        nonlocal last
        source = [(after(array, last) if last is not None else array, start) for array, start in pieces[c]] \
            if c < 2 else pieces[c]
        if c >= 2 and last is not None:
            arrays, places = distinct(source)
            arrays = after(arrays, last)
            source = [(arrays[at], start) for at, start in places]
        arrays = gate_up(source, rows, 2, *weights)
        last = arrays[0]
        hidden[c] = swap_far(arrays)

    def turn(c):
        nonlocal last
        source = swap_near(hidden[c])
        arrays, places = distinct(source)
        arrays = after(arrays, last)
        direct = c == 3
        arrays = rotate([(arrays[at], start) for at, start in places], rows, 1 if direct else 2, signs, table)
        last = arrays[0]
        rotated[c] = swap_direct(arrays) if direct else swap_far(arrays)

    def contract(c, strides, first_column, columns):
        nonlocal last
        source = rotated[c] if c == 3 else swap_near(rotated[c])
        arrays, places = distinct(source)
        arrays = after(arrays, last)
        keep, send = down(
            [(arrays[at], start) for at, start in places],
            rows,
            strides,
            first_column,
            columns,
            down_codes,
            down_scales,
        )
        last = send
        return keep, send

    def reduce_step(state, stride, final=False):
        nonlocal last
        keep, send = state
        came = after(exchange(send, stride), last)
        total = keep + came.astype(jnp.float32)
        if final:
            return total
        state = split_step(total)
        last = state[1]
        return state

    near = late
    expand(0)
    for stride in strides[:0:-1]:
        near = after(near, last) if stride != strides[-1] else near
        near = gather_step(near, stride)
    far = exchange(near, 1)
    for c in (2, 3):
        pieces[c] = gathered_pieces(near, far, devices, 2 * rows, (c - 2) * rows)
    expand(1)
    turn(0)
    expand(2)
    turn(1)
    sums[0] = contract(0, strides, 0, width)
    expand(3)
    sums[0] = reduce_step(sums[0], strides[0])
    turn(2)
    sums[0] = reduce_step(sums[0], strides[1])
    sums[1] = contract(1, strides, 0, width)
    sums[0] = reduce_step(sums[0], strides[2], True)
    turn(3)
    sums[1] = reduce_step(sums[1], strides[0])
    sums[2] = contract(2, strides, 0, width)
    sums[1] = reduce_step(sums[1], strides[1])
    sums[1] = reduce_step(sums[1], strides[2], True)
    sums[2] = reduce_step(sums[2], strides[0])
    half = width // 2
    other = [strides[1], strides[0], strides[2]]
    left = contract(3, strides, 0, half)
    sums[2] = reduce_step(sums[2], strides[1])
    right = contract(3, other, half, half)
    left = reduce_step(left, strides[0])
    right = reduce_step(right, other[0])
    sums[2] = reduce_step(sums[2], strides[2], True)
    left = reduce_step(left, strides[1])
    right = reduce_step(right, other[1])
    left = reduce_step(left, strides[2], True)
    right = reduce_step(right, other[2], True)
    sums[3] = jnp.concatenate([left, right], axis=1)
    total = jnp.concatenate(sums, axis=0)
    return (tokens.astype(jnp.float32) + total).astype(jnp.bfloat16)


def dequantize(codes, scales):
    blocks = scales.shape[0]
    height, width = codes.shape
    spread = codes.astype(jnp.float32).reshape(blocks, height // blocks, width) * scales[:, None, :]
    return spread.reshape(height, width).astype(jnp.bfloat16)


def shards_plain(
    tokens, norm_gain, gate_codes, gate_scales, up_codes, up_scales, down_codes, down_scales
):
    floated = tokens.astype(jnp.float32)
    normed = (
        floated
        * lax.rsqrt(jnp.mean(floated * floated, axis=1, keepdims=True) + EPSILON)
        * norm_gain
    ).astype(jnp.bfloat16)
    gate_weight = dequantize(gate_codes, gate_scales)
    up_weight = dequantize(up_codes, up_scales)
    down_weight = dequantize(down_codes, down_scales)
    piece = lax.all_gather(normed, AXIS, axis=0, tiled=True)
    gate = jnp.dot(piece, gate_weight, preferred_element_type=jnp.float32)
    upward = jnp.dot(piece, up_weight, preferred_element_type=jnp.float32)
    hidden = (jax.nn.silu(gate) * upward).astype(jnp.bfloat16)
    total_rows, local_width = hidden.shape
    devices = lax.axis_size(AXIS)
    local_walsh = down_scales.shape[0]
    group = down_codes.shape[0] // local_walsh
    blocks = hidden.astype(jnp.float32).reshape(total_rows, local_walsh, group)
    small_table = jnp.asarray(hadamard_small(), jnp.float32)
    local_table = jnp.asarray(walsh(local_walsh), jnp.float32)
    blocks = jnp.einsum("tia,ac->tic", blocks, small_table, precision=lax.Precision.HIGHEST)
    blocks = jnp.einsum("ji,tic->tjc", local_table, blocks, precision=lax.Precision.HIGHEST)
    blocks = blocks.reshape(total_rows, local_width)
    position = lax.axis_index(AXIS)
    for level in range(devices.bit_length() - 1):
        partner = exchange(blocks.astype(jnp.bfloat16), 1 << level).astype(blocks.dtype)
        signed = (1 - 2 * (position >> level & 1)).astype(jnp.float32)
        blocks = partner + signed * blocks
    rotated = (blocks * (devices * local_width) ** (-0.5)).astype(jnp.bfloat16)
    summed = lax.psum_scatter(
        jnp.dot(rotated, down_weight, preferred_element_type=jnp.float32),
        AXIS,
        scatter_dimension=0,
        tiled=True,
    )
    return (floated + summed).astype(jnp.bfloat16)


def shards(tokens, norm_gain, gate_codes, *others):
    devices = lax.axis_size(AXIS)
    rows, width = tokens.shape
    local = gate_codes.shape[1]
    if devices == 8 and rows % 64 == 0 and local % 896 == 0 and width % 1024 == 0:
        return shards_piped(tokens, norm_gain, gate_codes, *others)
    return shards_plain(tokens, norm_gain, gate_codes, *others)


def solution(mesh):
    return jax.shard_map(
        shards,
        mesh=mesh,
        in_specs=(
            P(("groups", "tensor", "dp"), None),
            P(),
            P(None, "tensor"),
            P(None, "tensor"),
            P(None, "tensor"),
            P(None, "tensor"),
            P("tensor", None),
            P("tensor", None),
        ),
        out_specs=P(("groups", "tensor", "dp"), None),
        check_vma=False,
    )
```

time: 333 us -> 399 us (1.20)
  Pallas kernels: 92.4 us -> 157 us
  waiting for transfers between devices: 118 us -> 133 us
  starting transfers between devices: 112 us -> 101 us
    pallas_call x6 -> x13, Pallas kernels: 92.1 us -> 157 us  [the longest x4 94.2 us: gate_up(): pl.pallas_call(functools.partial(gate_up_kernel, places, rows, 1024, widt...]
    ppermute x48 -> x67, waiting for transfers between devices: 118 us -> 133 us  [exchange(): lax.ppermute(value, AXIS, [(i, i ^ stride) for i in range(lax.axis_size(A...]
    ppermute x48 -> x67, starting transfers between devices: 112 us -> 101 us  [exchange(): lax.ppermute(value, AXIS, [(i, i ^ stride) for i in range(lax.axis_size(A...]
  transfers between devices with their start and end apart: 48 -> 67, of which waited for: 16 -> 26; matrix products, arithmetic and copies ran while one was open for 0% -> 1% of each run, Pallas kernels for 28% -> 30%
where the time goes in v2:
time: 399 us; the launch traced here: 398 us
  Pallas kernels  157 us (39%)
  waiting for transfers between devices  133 us (33%)
  starting transfers between devices  101 us (25%)
  local copies, waits for them, and re-layouts  5 us (1%)
    ppermute x67, waiting for transfers between devices, exchange(): lax.ppermute(value, AXIS, [(i, i ^ stride) for i in range(lax.axis_size(A...  133 us
    ppermute x67, starting transfers between devices, exchange(): lax.ppermute(value, AXIS, [(i, i ^ stride) for i in range(lax.axis_size(A...  101 us
    pallas_call x4, Pallas kernels, gate_up(): pl.pallas_call(functools.partial(gate_up_kernel, places, rows, 1024, widt...  94.2 us
    pallas_call x5, Pallas kernels, down(): pl.pallas_call(functools.partial(down_kernel, places, rows, local // bloc...  54.6 us
  transfers between devices with their start and end apart: 67, of which 26 were waited for; matrix products, arithmetic and copies ran while one was open for 1% of the time, Pallas kernels for 30%

profile of v2, /device:TPU:0, one launch (start us, length us, event | category | flops | bytes accessed | tf_op | source)
XLA Modules:
  0.0 398.2 jit_solution(4734667679215527200)
XLA Ops:
  6.1 6.3 %collective-permute-done.3.refs_4_ = bf16[16,4096]{1,0:T(8,128)(2,1)S(1)} collective-permute-done((bf16[16,4096]{1,0:T(8,128)(2,1)S(1)}, bf16[16,4096]{1,0:T(8,128)(2,1)S(1)}, u32[]{:S(2)}, u32[]{:S(2)}) %collective-permute-start.3) | collective-permute-done | bytes 131104 | tf_op jit(solution)/shard_map/ppermute | solution.py:41
  16.6 5.1 %collective-permute-done.5.refs_6_ = bf16[16,4096]{1,0:T(8,128)(2,1)S(1)} collective-permute-done((bf16[16,4096]{1,0:T(8,128)(2,1)S(1)}, bf16[16,4096]{1,0:T(8,128)(2,1)S(1)}, u32[]{:S(2)}, u32[]{:S(2)}) %collective-permute-start.5) | collective-permute-done | bytes 131104 | tf_op jit(solution)/shard_map/ppermute | solution.py:41
  38.5 23.5 %gate_up.4 = (bf16[32,3584]{1,0:T(8,128)(2,1)S(1)}, bf16[32,3584]{1,0:T(8,128)(2,1)S(1)}, bf16[32,3584]{1,0:T(8,128)(2,1)S(1)}, bf16[32,3584]{1,0:T(8,128)(2,1)S(1)}) custom-call(bf16[16,4096]{1,0:T(8,128)(2,1)S(1)} %get-tuple-element.134.refs_0_, bf16[16,4096]{1,0:T(8,128)(2,1)S(1)} %collective-permute-done.refs_1_, ...), custom_call_target="tpu_custom_call" | custom-call | flops 7516192768 | bytes 58720256 | tf_op jit(solution)/shard_map/gate_up/pallas_call | solution.py:174
  66.9 23.7 %gate_up.5 = (bf16[32,3584]{1,0:T(8,128)(2,1)S(1)}, bf16[32,3584]{1,0:T(8,128)(2,1)S(1)}, bf16[32,3584]{1,0:T(8,128)(2,1)S(1)}, bf16[32,3584]{1,0:T(8,128)(2,1)S(1)}) custom-call(bf16[16,4096]{1,0:T(8,128)(2,1)S(1)} %get-tuple-element.140.refs_0_, bf16[16,4096]{1,0:T(8,128)(2,1)S(1)} %collective-permute-done.11.refs_1_, ...), custom_call_target="tpu_custom_call" | custom-call | flops 7516192768 | bytes 58720256 | tf_op jit(solution)/shard_map/gate_up/pallas_call | solution.py:174
  98.0 18.0 %collective-permute-done.27 = bf16[64,4096]{1,0:T(8,128)(2,1)S(1)} collective-permute-done((bf16[64,4096]{1,0:T(8,128)(2,1)S(1)}, bf16[64,4096]{1,0:T(8,128)(2,1)S(1)}, u32[]{:S(2)}, u32[]{:S(2)}) %collective-permute-start.27) | collective-permute-done | bytes 524320 | tf_op jit(solution)/shard_map/ppermute | solution.py:41
  129.4 7.2 %collective-permute-done.19.refs_3_ = bf16[32,3584]{1,0:T(8,128)(2,1)S(1)} collective-permute-done((bf16[32,3584]{1,0:T(8,128)(2,1)S(1)}, bf16[32,3584]{1,0:T(8,128)(2,1)S(1)}, u32[]{:S(2)}, u32[]{:S(2)}) %collective-permute-start.19) | collective-permute-done | bytes 229408 | tf_op jit(solution)/shard_map/ppermute | solution.py:41
  142.2 23.5 %gate_up.6 = (bf16[32,3584]{1,0:T(8,128)(2,1)S(1)}, bf16[32,3584]{1,0:T(8,128)(2,1)S(1)}, bf16[32,3584]{1,0:T(8,128)(2,1)S(1)}, bf16[32,3584]{1,0:T(8,128)(2,1)S(1)}) custom-call(bf16[128,4096]{1,0:T(8,128)(2,1)S(1)} %constant_dynamic-update-slice_fusion.refs_0_, bf16[128,4096]{1,0:T(8,128)(2,1)S(1)} %collective-permute-done.28.refs_1_, ...), custom_call_target="tpu_custom_call" | custom-call | flops 7516192768 | bytes 58720256 | tf_op jit(solution)/shard_map/gate_up/pallas_call | solution.py:174
  167.7 13.4 %down.5 = (f32[64,4096]{1,0:T(8,128)S(1)}, bf16[64,4096]{1,0:T(8,128)(2,1)S(1)}) custom-call(bf16[32,3584]{1,0:T(8,128)(2,1)S(1)} %get-tuple-element.173.refs_0_, bf16[64,3584]{1,0:T(8,128)(2,1)S(1)} %collective-permute-done.21.refs_1_, bf16[32,3584]{1,0:T(8,128)(2,1)S(1)} %collective-permute-done.18.refs_2_, ...), custom_call_target="tpu_custom_call" | custom-call | flops 3758096384 | bytes 29360128 | tf_op jit(solution)/shard_map/down/pallas_call | solution.py:321
  181.0 23.5 %gate_up.7 = (bf16[32,3584]{1,0:T(8,128)(2,1)S(1)}, bf16[32,3584]{1,0:T(8,128)(2,1)S(1)}, bf16[32,3584]{1,0:T(8,128)(2,1)S(1)}, bf16[32,3584]{1,0:T(8,128)(2,1)S(1)}) custom-call(bf16[128,4096]{1,0:T(8,128)(2,1)S(1)} %constant_dynamic-update-slice_fusion.refs_0_, bf16[128,4096]{1,0:T(8,128)(2,1)S(1)} %collective-permute-done.28.refs_1_, ...), custom_call_target="tpu_custom_call" | custom-call | flops 7516192768 | bytes 58720256 | tf_op jit(solution)/shard_map/gate_up/pallas_call | solution.py:174
  216.8 17.7 %collective-permute-done.42.refs_3_ = bf16[32,3584]{1,0:T(8,128)(2,1)S(1)} collective-permute-done((bf16[32,3584]{1,0:T(8,128)(2,1)S(1)}, bf16[32,3584]{1,0:T(8,128)(2,1)S(1)}, u32[]{:S(2)}, u32[]{:S(2)}) %collective-permute-start.42) | collective-permute-done | bytes 229408 | tf_op jit(solution)/shard_map/ppermute | solution.py:41
  237.5 13.1 %collective-permute-start.37 = (bf16[32,3584]{1,0:T(8,128)(2,1)S(1)}, bf16[32,3584]{1,0:T(8,128)(2,1)S(1)}, u32[]{:S(2)}, u32[]{:S(2)}) collective-permute-start(bf16[32,3584]{1,0:T(8,128)(2,1)S(1)} %get-tuple-element.195), channel_id=1, source_target_pairs={{0,8},{2,10},{4,12},{6,14},{8,0},{10,2},{12,4},{14,6},{1,9},{3,11}... | collective-permute-start | bytes 688136 | tf_op jit(solution)/shard_map/ppermute | solution.py:41
  250.6 5.8 %collective-permute-done.32.refs_3_ = bf16[32,3584]{1,0:T(8,128)(2,1)S(1)} collective-permute-done((bf16[32,3584]{1,0:T(8,128)(2,1)S(1)}, bf16[32,3584]{1,0:T(8,128)(2,1)S(1)}, u32[]{:S(2)}, u32[]{:S(2)}) %collective-permute-start.32) | collective-permute-done | bytes 229408 | tf_op jit(solution)/shard_map/ppermute | solution.py:41
  258.9 5.5 %collective-permute-done.36.refs_2_ = bf16[32,3584]{1,0:T(8,128)(2,1)S(1)} collective-permute-done((bf16[32,3584]{1,0:T(8,128)(2,1)S(1)}, bf16[32,3584]{1,0:T(8,128)(2,1)S(1)}, u32[]{:S(2)}, u32[]{:S(2)}) %collective-permute-start.36) | collective-permute-done | bytes 229408 | tf_op jit(solution)/shard_map/ppermute | solution.py:41
  265.0 10.8 %collective-permute-done.34.refs_1_ = bf16[64,3584]{1,0:T(8,128)(2,1)S(1)} collective-permute-done((bf16[64,3584]{1,0:T(8,128)(2,1)S(1)}, bf16[64,3584]{1,0:T(8,128)(2,1)S(1)}, u32[]{:S(2)}, u32[]{:S(2)}) %collective-permute-start.34) | collective-permute-done | bytes 458784 | tf_op jit(solution)/shard_map/ppermute | solution.py:41
  282.9 13.5 %down.6 = (f32[64,4096]{1,0:T(8,128)S(1)}, bf16[64,4096]{1,0:T(8,128)(2,1)S(1)}) custom-call(bf16[32,3584]{1,0:T(8,128)(2,1)S(1)} %get-tuple-element.197.refs_0_, bf16[64,3584]{1,0:T(8,128)(2,1)S(1)} %collective-permute-done.39.refs_1_, bf16[32,3584]{1,0:T(8,128)(2,1)S(1)} %collective-permute-done.36.refs_2_, ...), custom_call_target="tpu_custom_call" | custom-call | flops 3758096384 | bytes 29360128 | tf_op jit(solution)/shard_map/down/pallas_call | solution.py:321
  305.1 6.7 %collective-permute-done.40 = bf16[64,4096]{1,0:T(8,128)(2,1)S(1)} collective-permute-done((bf16[64,4096]{1,0:T(8,128)(2,1)S(1)}, bf16[64,4096]{1,0:T(8,128)(2,1)S(1)}, u32[]{:S(2)}, u32[]{:S(2)}) %collective-permute-start.40) | collective-permute-done | bytes 524320 | tf_op jit(solution)/shard_map/ppermute | solution.py:41
  313.6 6.7 %collective-permute-done.49.refs_1_ = bf16[64,3584]{1,0:T(8,128)(2,1)S(1)} collective-permute-done((bf16[64,3584]{1,0:T(8,128)(2,1)S(1)}, bf16[64,3584]{1,0:T(8,128)(2,1)S(1)}, u32[]{:S(2)}, u32[]{:S(2)}) %collective-permute-start.49) | collective-permute-done | bytes 458784 | tf_op jit(solution)/shard_map/ppermute | solution.py:41
  320.3 13.3 %down.7 = (f32[64,4096]{1,0:T(8,128)S(1)}, bf16[64,4096]{1,0:T(8,128)(2,1)S(1)}) custom-call(bf16[32,3584]{1,0:T(8,128)(2,1)S(1)} %get-tuple-element.218.refs_0_, bf16[64,3584]{1,0:T(8,128)(2,1)S(1)} %collective-permute-done.49.refs_1_, bf16[32,3584]{1,0:T(8,128)(2,1)S(1)} %collective-permute-done.46.refs_2_, ...), custom_call_target="tpu_custom_call" | custom-call | flops 3758096384 | bytes 29360128 | tf_op jit(solution)/shard_map/down/pallas_call | solution.py:321
  335.5 9.1 %collective-permute-done.51 = bf16[64,4096]{1,0:T(8,128)(2,1)S(1)} collective-permute-done((bf16[64,4096]{1,0:T(8,128)(2,1)S(1)}, bf16[64,4096]{1,0:T(8,128)(2,1)S(1)}, u32[]{:S(2)}, u32[]{:S(2)}) %collective-permute-start.51) | collective-permute-done | bytes 524320 | tf_op jit(solution)/shard_map/ppermute | solution.py:41
  352.7 4.8 %collective-permute-done.57.refs_5_ = bf16[16,3584]{1,0:T(8,128)(2,1)S(1)} collective-permute-done((bf16[16,3584]{1,0:T(8,128)(2,1)S(1)}, bf16[16,3584]{1,0:T(8,128)(2,1)S(1)}, u32[]{:S(2)}, u32[]{:S(2)}) %collective-permute-start.57) | collective-permute-done | bytes 114720 | tf_op jit(solution)/shard_map/ppermute | solution.py:41
  359.4 7.2 %down.8 = (f32[64,2048]{1,0:T(8,128)S(1)}, bf16[64,2048]{1,0:T(8,128)(2,1)S(1)}) custom-call(bf16[16,3584]{1,0:T(8,128)(2,1)S(1)} %get-tuple-element.245.refs_0_, bf16[16,3584]{1,0:T(8,128)(2,1)S(1)} %collective-permute-done.53.refs_1_, bf16[16,3584]{1,0:T(8,128)(2,1)S(1)} %collective-permute-done.54.refs_2_, ...), custom_call_target="tpu_custom_call" | custom-call | flops 1879048192 | bytes 14680064 | tf_op jit(solution)/shard_map/down/pallas_call | solution.py:321
  366.8 6.3 %collective-permute-start.60 = (bf16[16,4096]{1,0:T(8,128)(2,1)S(1)}, bf16[16,4096]{1,0:T(8,128)(2,1)S(1)}, u32[]{:S(2)}, u32[]{:S(2)}) collective-permute-start(bf16[16,4096]{1,0:T(8,128)(2,1)S(1)} %slice.268), channel_id=1, source_target_pairs={{0,8},{2,10},{4,12},{6,14},{8,0},{10,2},{12,4},{14,6},{1,9},{3,11}... | collective-permute-start | bytes 393224 | tf_op jit(solution)/shard_map/ppermute | solution.py:41
  373.1 7.2 %down.9 = (f32[64,2048]{1,0:T(8,128)S(1)}, bf16[64,2048]{1,0:T(8,128)(2,1)S(1)}) custom-call(bf16[16,3584]{1,0:T(8,128)(2,1)S(1)} %get-tuple-element.245.refs_0_, bf16[16,3584]{1,0:T(8,128)(2,1)S(1)} %collective-permute-done.53.refs_1_, bf16[16,3584]{1,0:T(8,128)(2,1)S(1)} %collective-permute-done.54.refs_2_, ...), custom_call_target="tpu_custom_call" | custom-call | flops 1879048192 | bytes 14680064 | tf_op jit(solution)/shard_map/down/pallas_call | solution.py:321
  382.5 4.2 %collective-permute-done.61 = bf16[64,2048]{1,0:T(8,128)(2,1)S(1)} collective-permute-done((bf16[64,2048]{1,0:T(8,128)(2,1)S(1)}, bf16[64,2048]{1,0:T(8,128)(2,1)S(1)}, u32[]{:S(2)}, u32[]{:S(2)}) %collective-permute-start.61) | collective-permute-done | bytes 262176 | tf_op jit(solution)/shard_map/ppermute | solution.py:41
  (205 shorter events, 121.2 us)
Async XLA Ops:
  28.5 33.6 %collective-permute-start.11 = (bf16[16,4096]{1,0:T(8,128)(2,1)S(1)}, bf16[16,4096]{1,0:T(8,128)(2,1)S(1)}, u32[]{:S(2)}, u32[]{:S(2)}) collective-permute-start(bf16[16,4096]{1,0:T(8,128)(2,1)S(1)} %get-tuple-element.140.refs_0_), channel_id=1, source_target_pairs={{0,2},{2,0},{4,6},{6,4},{8,10},{10,8},{12,14},{14,12},{1,3},{3,1},... | collective-permute-start | bytes 393224 | tf_op jit(solution)/shard_map/ppermute | solution.py:41
  29.7 37.1 %collective-permute-start.15 = (bf16[16,4096]{1,0:T(8,128)(2,1)S(1)}, bf16[16,4096]{1,0:T(8,128)(2,1)S(1)}, u32[]{:S(2)}, u32[]{:S(2)}) collective-permute-start(bf16[16,4096]{1,0:T(8,128)(2,1)S(1)} %collective-permute-done.14.refs_4_), channel_id=1, source_target_pairs={{0,2},{2,0},{4,6},{6,4},{8,10},{10,8},{12,14},{14,12},{1,3},{3,1},... | collective-permute-start | bytes 393224 | tf_op jit(solution)/shard_map/ppermute | solution.py:41
  31.3 33.5 %collective-permute-start.13 = (bf16[16,4096]{1,0:T(8,128)(2,1)S(1)}, bf16[16,4096]{1,0:T(8,128)(2,1)S(1)}, u32[]{:S(2)}, u32[]{:S(2)}) collective-permute-start(bf16[16,4096]{1,0:T(8,128)(2,1)S(1)} %collective-permute-done.12.refs_2_), channel_id=1, source_target_pairs={{0,2},{2,0},{4,6},{6,4},{8,10},{10,8},{12,14},{14,12},{1,3},{3,1},... | collective-permute-start | bytes 393224 | tf_op jit(solution)/shard_map/ppermute | solution.py:41
  32.5 34.4 %collective-permute-start.17 = (bf16[16,4096]{1,0:T(8,128)(2,1)S(1)}, bf16[16,4096]{1,0:T(8,128)(2,1)S(1)}, u32[]{:S(2)}, u32[]{:S(2)}) collective-permute-start(bf16[16,4096]{1,0:T(8,128)(2,1)S(1)} %collective-permute-done.16.refs_6_), channel_id=1, source_target_pairs={{0,2},{2,0},{4,6},{6,4},{8,10},{10,8},{12,14},{14,12},{1,3},{3,1},... | collective-permute-start | bytes 393224 | tf_op jit(solution)/shard_map/ppermute | solution.py:41
  34.1 61.2 %collective-permute-start.26 = (bf16[32,4096]{1,0:T(8,128)(2,1)S(1)}, bf16[32,4096]{1,0:T(8,128)(2,1)S(1)}, u32[]{:S(2)}, u32[]{:S(2)}) collective-permute-start(bf16[32,4096]{1,0:T(8,128)(2,1)S(1)} %get-tuple-element.162), channel_id=1, source_target_pairs={{0,8},{2,10},{4,12},{6,14},{8,0},{10,2},{12,4},{14,6},{1,9},{3,11}... | collective-permute-start | bytes 786440 | tf_op jit(solution)/shard_map/ppermute | solution.py:41
  62.1 30.9 %collective-permute-start.9 = (bf16[32,3584]{1,0:T(8,128)(2,1)S(1)}, bf16[32,3584]{1,0:T(8,128)(2,1)S(1)}, u32[]{:S(2)}, u32[]{:S(2)}) collective-permute-start(bf16[32,3584]{1,0:T(8,128)(2,1)S(1)} %get-tuple-element.138), channel_id=1, source_target_pairs={{0,12},{2,14},{4,8},{6,10},{8,4},{10,6},{12,0},{14,2},{1,13},{3,15... | collective-permute-start | bytes 688136 | tf_op jit(solution)/shard_map/ppermute | solution.py:41
  64.8 29.2 %collective-permute-start.8 = (bf16[32,3584]{1,0:T(8,128)(2,1)S(1)}, bf16[32,3584]{1,0:T(8,128)(2,1)S(1)}, u32[]{:S(2)}, u32[]{:S(2)}) collective-permute-start(bf16[32,3584]{1,0:T(8,128)(2,1)S(1)} %get-tuple-element.137), channel_id=1, source_target_pairs={{0,8},{2,10},{4,12},{6,14},{8,0},{10,2},{12,4},{14,6},{1,9},{3,11}... | collective-permute-start | bytes 688136 | tf_op jit(solution)/shard_map/ppermute | solution.py:41
  66.9 28.4 %collective-permute-start.7 = (bf16[32,3584]{1,0:T(8,128)(2,1)S(1)}, bf16[32,3584]{1,0:T(8,128)(2,1)S(1)}, u32[]{:S(2)}, u32[]{:S(2)}) collective-permute-start(bf16[32,3584]{1,0:T(8,128)(2,1)S(1)} %get-tuple-element.136), channel_id=1, source_target_pairs={{0,4},{2,6},{4,0},{6,2},{8,12},{10,14},{12,8},{14,10},{1,5},{3,7},... | collective-permute-start | bytes 688136 | tf_op jit(solution)/shard_map/ppermute | solution.py:41
  90.7 27.1 %collective-permute-start.24 = (bf16[32,3584]{1,0:T(8,128)(2,1)S(1)}, bf16[32,3584]{1,0:T(8,128)(2,1)S(1)}, u32[]{:S(2)}, u32[]{:S(2)}) collective-permute-start(bf16[32,3584]{1,0:T(8,128)(2,1)S(1)} %get-tuple-element.160), channel_id=1, source_target_pairs={{0,12},{2,14},{4,8},{6,10},{8,4},{10,6},{12,0},{14,2},{1,13},{3,15... | collective-permute-start | bytes 688136 | tf_op jit(solution)/shard_map/ppermute | solution.py:41
  92.9 24.8 %collective-permute-start.23 = (bf16[32,3584]{1,0:T(8,128)(2,1)S(1)}, bf16[32,3584]{1,0:T(8,128)(2,1)S(1)}, u32[]{:S(2)}, u32[]{:S(2)}) collective-permute-start(bf16[32,3584]{1,0:T(8,128)(2,1)S(1)} %get-tuple-element.159), channel_id=1, source_target_pairs={{0,8},{2,10},{4,12},{6,14},{8,0},{10,2},{12,4},{14,6},{1,9},{3,11}... | collective-permute-start | bytes 688136 | tf_op jit(solution)/shard_map/ppermute | solution.py:41
  94.1 23.7 %collective-permute-start.22 = (bf16[32,3584]{1,0:T(8,128)(2,1)S(1)}, bf16[32,3584]{1,0:T(8,128)(2,1)S(1)}, u32[]{:S(2)}, u32[]{:S(2)}) collective-permute-start(bf16[32,3584]{1,0:T(8,128)(2,1)S(1)} %get-tuple-element.158), channel_id=1, source_target_pairs={{0,4},{2,6},{4,0},{6,2},{8,12},{10,14},{12,8},{14,10},{1,5},{3,7},... | collective-permute-start | bytes 688136 | tf_op jit(solution)/shard_map/ppermute | solution.py:41
  116.0 26.2 %collective-permute-start.28 = (bf16[128,4096]{1,0:T(8,128)(2,1)S(1)}, bf16[128,4096]{1,0:T(8,128)(2,1)S(1)}, u32[]{:S(2)}, u32[]{:S(2)}) collective-permute-start(bf16[128,4096]{1,0:T(8,128)(2,1)S(1)} %constant_dynamic-update-slice_fusion.refs_0_), channel_id=1, source_target_pairs={{0,2},{2,0},{4,6},{6,4},{8,10},{10,8},{12,14},{14,12},{1,3},{3,1},... | collective-permute-start | bytes 3145736 | tf_op jit(solution)/shard_map/ppermute | solution.py:41
  124.3 41.4 %collective-permute-start.25 = (bf16[64,3584]{1,0:T(8,128)(2,1)S(1)}, bf16[64,3584]{1,0:T(8,128)(2,1)S(1)}, u32[]{:S(2)}, u32[]{:S(2)}) collective-permute-start(bf16[64,3584]{1,0:T(8,128)(2,1)S(1)} %pad_maximum_fusion.3), channel_id=1, source_target_pairs={{0,2},{2,0},{4,6},{6,4},{8,10},{10,8},{12,14},{14,12},{1,3},{3,1},... | collective-permute-start | bytes 1376264 | tf_op jit(solution)/shard_map/ppermute | solution.py:41
  136.7 31.0 %collective-permute-start.21 = (bf16[64,3584]{1,0:T(8,128)(2,1)S(1)}, bf16[64,3584]{1,0:T(8,128)(2,1)S(1)}, u32[]{:S(2)}, u32[]{:S(2)}) collective-permute-start(bf16[64,3584]{1,0:T(8,128)(2,1)S(1)} %pad_maximum_fusion.2), channel_id=1, source_target_pairs={{0,2},{2,0},{4,6},{6,4},{8,10},{10,8},{12,14},{14,12},{1,3},{3,1},... | collective-permute-start | bytes 1376264 | tf_op jit(solution)/shard_map/ppermute | solution.py:41
  206.2 28.3 %collective-permute-start.42 = (bf16[32,3584]{1,0:T(8,128)(2,1)S(1)}, bf16[32,3584]{1,0:T(8,128)(2,1)S(1)}, u32[]{:S(2)}, u32[]{:S(2)}) collective-permute-start(bf16[32,3584]{1,0:T(8,128)(2,1)S(1)} %get-tuple-element.206), channel_id=1, source_target_pairs={{0,8},{2,10},{4,12},{6,14},{8,0},{10,2},{12,4},{14,6},{1,9},{3,11}... | collective-permute-start | bytes 688136 | tf_op jit(solution)/shard_map/ppermute | solution.py:41
  206.2 28.3 %collective-permute-start.41 = (bf16[32,3584]{1,0:T(8,128)(2,1)S(1)}, bf16[32,3584]{1,0:T(8,128)(2,1)S(1)}, u32[]{:S(2)}, u32[]{:S(2)}) collective-permute-start(bf16[32,3584]{1,0:T(8,128)(2,1)S(1)} %get-tuple-element.205), channel_id=1, source_target_pairs={{0,4},{2,6},{4,0},{6,2},{8,12},{10,14},{12,8},{14,10},{1,5},{3,7},... | collective-permute-start | bytes 688136 | tf_op jit(solution)/shard_map/ppermute | solution.py:41
  209.0 55.4 %collective-permute-start.29 = (bf16[64,4096]{1,0:T(8,128)(2,1)S(1)}, bf16[64,4096]{1,0:T(8,128)(2,1)S(1)}, u32[]{:S(2)}, u32[]{:S(2)}) collective-permute-start(bf16[64,4096]{1,0:T(8,128)(2,1)S(1)} %get-tuple-element.179), channel_id=1, source_target_pairs={{0,2},{2,0},{4,6},{6,4},{8,10},{10,8},{12,14},{14,12},{1,3},{3,1},... | collective-permute-start | bytes 1572872 | tf_op jit(solution)/shard_map/ppermute | solution.py:41
  210.0 46.6 %collective-permute-start.38 = (bf16[32,3584]{1,0:T(8,128)(2,1)S(1)}, bf16[32,3584]{1,0:T(8,128)(2,1)S(1)}, u32[]{:S(2)}, u32[]{:S(2)}) collective-permute-start(bf16[32,3584]{1,0:T(8,128)(2,1)S(1)} %get-tuple-element.196), channel_id=1, source_target_pairs={{0,12},{2,14},{4,8},{6,10},{8,4},{10,6},{12,0},{14,2},{1,13},{3,15... | collective-permute-start | bytes 688136 | tf_op jit(solution)/shard_map/ppermute | solution.py:41
  256.5 40.0 %collective-permute-start.44 = (bf16[64,3584]{1,0:T(8,128)(2,1)S(1)}, bf16[64,3584]{1,0:T(8,128)(2,1)S(1)}, u32[]{:S(2)}, u32[]{:S(2)}) collective-permute-start(bf16[64,3584]{1,0:T(8,128)(2,1)S(1)} %pad_maximum_fusion.6), channel_id=1, source_target_pairs={{0,2},{2,0},{4,6},{6,4},{8,10},{10,8},{12,14},{14,12},{1,3},{3,1},... | collective-permute-start | bytes 1376264 | tf_op jit(solution)/shard_map/ppermute | solution.py:41
  278.9 22.9 %collective-permute-start.47 = (bf16[32,3584]{1,0:T(8,128)(2,1)S(1)}, bf16[32,3584]{1,0:T(8,128)(2,1)S(1)}, u32[]{:S(2)}, u32[]{:S(2)}) collective-permute-start(bf16[32,3584]{1,0:T(8,128)(2,1)S(1)} %get-tuple-element.216), channel_id=1, source_target_pairs={{0,8},{2,10},{4,12},{6,14},{8,0},{10,2},{12,4},{14,6},{1,9},{3,11}... | collective-permute-start | bytes 688136 | tf_op jit(solution)/shard_map/ppermute | solution.py:41
  300.2 45.7 %collective-permute-start.53 = (bf16[16,3584]{1,0:T(8,128)(2,1)S(1)}, bf16[16,3584]{1,0:T(8,128)(2,1)S(1)}, u32[]{:S(2)}, u32[]{:S(2)}) collective-permute-start(bf16[16,3584]{1,0:T(8,128)(2,1)S(1)} %get-tuple-element.228), channel_id=1, source_target_pairs={{0,2},{2,0},{4,6},{6,4},{8,10},{10,8},{12,14},{14,12},{1,3},{3,1},... | collective-permute-start | bytes 344072 | tf_op jit(solution)/shard_map/ppermute | solution.py:41
  300.6 49.0 %collective-permute-start.54 = (bf16[16,3584]{1,0:T(8,128)(2,1)S(1)}, bf16[16,3584]{1,0:T(8,128)(2,1)S(1)}, u32[]{:S(2)}, u32[]{:S(2)}) collective-permute-start(bf16[16,3584]{1,0:T(8,128)(2,1)S(1)} %get-tuple-element.229), channel_id=1, source_target_pairs={{0,4},{2,6},{4,0},{6,2},{8,12},{10,14},{12,8},{14,10},{1,5},{3,7},... | collective-permute-start | bytes 344072 | tf_op jit(solution)/shard_map/ppermute | solution.py:41
  301.8 49.8 %collective-permute-start.55 = (bf16[16,3584]{1,0:T(8,128)(2,1)S(1)}, bf16[16,3584]{1,0:T(8,128)(2,1)S(1)}, u32[]{:S(2)}, u32[]{:S(2)}) collective-permute-start(bf16[16,3584]{1,0:T(8,128)(2,1)S(1)} %get-tuple-element.230), channel_id=1, source_target_pairs={{0,6},{2,4},{4,2},{6,0},{8,14},{10,12},{12,10},{14,8},{1,7},{3,5},... | collective-permute-start | bytes 344072 | tf_op jit(solution)/shard_map/ppermute | solution.py:41
  303.8 48.9 %collective-permute-start.56 = (bf16[16,3584]{1,0:T(8,128)(2,1)S(1)}, bf16[16,3584]{1,0:T(8,128)(2,1)S(1)}, u32[]{:S(2)}, u32[]{:S(2)}) collective-permute-start(bf16[16,3584]{1,0:T(8,128)(2,1)S(1)} %get-tuple-element.231), channel_id=1, source_target_pairs={{0,8},{2,10},{4,12},{6,14},{8,0},{10,2},{12,4},{14,6},{1,9},{3,11}... | collective-permute-start | bytes 344072 | tf_op jit(solution)/shard_map/ppermute | solution.py:41
  (52 other events, 827.6 us)

commit v3 on v2

v3 whole, which is shorter than its diff:
```python
import functools
import math

import jax
import jax.numpy as jnp
import ml_dtypes
import numpy as np
from jax import lax
from jax.experimental import pallas as pl
from jax.experimental.pallas import tpu as pltpu
from jax.sharding import PartitionSpec as P

EPSILON = 1e-05
AXIS = "tensor"
MIB = 1 << 20


def hadamard_small():
    modulus = 13
    residues = [number * number % modulus for number in range(1, modulus)]
    legendre = [0] + [1 if number in residues else -1 for number in range(1, modulus)]
    conference = np.zeros((modulus + 1, modulus + 1), np.int64)
    conference[0, 1:] = 1
    conference[1:, 0] = 1
    for row in range(1, modulus + 1):
        for column in range(1, modulus + 1):
            conference[row, column] = legendre[(column - row) % modulus]
    plus_block = np.array([[1, 1], [1, -1]])
    zero_block = np.array([[1, -1], [-1, -1]])
    return np.kron(conference, plus_block) + np.kron(np.eye(modulus + 1, dtype=np.int64), zero_block)


def walsh(order):
    table = np.ones((1, 1), np.int64)
    while table.shape[0] < order:
        table = np.kron(np.array([[1, 1], [1, -1]]), table)
    return table


def exchange(value, stride):
    return lax.ppermute(value, AXIS, [(i, i ^ stride) for i in range(lax.axis_size(AXIS))])


def after(value, *earlier):
    return lax.optimization_barrier((value, earlier))[0]


def gather_doubling(own, strides):
    rows = own.shape[0]
    held, places = own, {0: 0}
    for stride in strides[:-1]:
        places.update({k ^ stride: place + len(places) for k, place in places.items()})
        held = jnp.concatenate([held, exchange(held, stride)], axis=0)
    came = exchange(held, strides[-1])
    pieces = {k: (held, place * rows) for k, place in places.items()}
    pieces.update({k ^ strides[-1]: (came, place * rows) for k, place in places.items()})
    return [pieces[k] for k in range(len(pieces))]


def gather_flat_start(own, devices):
    return exchange(own, 1), [own] + [exchange(own, k) for k in range(2, devices, 2)]


def gather_flat_end(near, pieces):
    rows = near.shape[0]
    came = exchange(jnp.concatenate(pieces[1:], axis=0), 1)
    out = []
    for j, piece in enumerate(pieces):
        out += [(piece, 0), (near, 0) if j == 0 else (came, (j - 1) * rows)]
    return out


def swap_far(arrays):
    out = list(arrays)
    for j in range(len(arrays) - 1, 0, -1):
        out[j] = exchange(arrays[j], 2 * j)
    return out


def swap_near(arrays):
    rows = arrays[0].shape[0] // 2
    came = exchange(jnp.concatenate([array[rows:] for array in arrays], axis=0), 1)
    pieces = []
    for j, array in enumerate(arrays):
        pieces += [(array, 0), (came, j * rows)]
    return pieces


def pairs_near_first(arrays):
    *evens, odds = arrays
    rows = odds.shape[0] // len(evens)
    came = exchange(odds, 1)
    return [
        jnp.concatenate([even, came[j * rows : (j + 1) * rows]], axis=0)
        for j, even in enumerate(evens)
    ]


def pair_pieces(arrays):
    return [(array, start) for array in arrays for start in (0, array.shape[0] // 2)]


def swap_direct(arrays):
    out = list(arrays)
    for k in range(1, len(arrays)):
        out[k] = exchange(arrays[k], k)
    return [(array, 0) for array in out]


def single_layout(devices):
    return [(k, 0) for k in range(devices)]


def pairs_layout(devices):
    return [(k // 2, k % 2) for k in range(devices)]


def near_first_layout(devices):
    return [(devices // 2, k // 2) if k % 2 else (k // 2, 0) for k in range(devices)]


def shapes_of(layout, rows, columns):
    counts = [sum(1 for at, _ in layout if at == index) for index in range(1 + max(layout)[0])]
    return [jax.ShapeDtypeStruct((count * rows, columns), jnp.bfloat16) for count in counts]


def all_after(pieces, *earlier):
    arrays, places = distinct(pieces)
    arrays = after(arrays, *earlier)
    return [(arrays[at], start) for at, start in places]


def distinct(pieces):
    arrays = []
    for array, _ in pieces:
        if not any(other is array for other in arrays):
            arrays.append(array)
    index = {id(array): at for at, array in enumerate(arrays)}
    return arrays, [(index[id(array)], start) for array, start in pieces]


SPLIT = 2


def split_blocks(height, tile, skip):
    return [
        pl.BlockSpec((height // SPLIT, tile), functools.partial(lambda part, i: (part, i + skip), part))
        for part in range(SPLIT)
    ]


def whole_blocks(arrays):
    return [pl.BlockSpec(array.shape, lambda i: (0, 0)) for array in arrays]


def norm_kernel(cuts, tokens_ref, gain_ref, *out_refs):
    floated = tokens_ref[...].astype(jnp.float32)
    inverse = lax.rsqrt(jnp.mean(floated * floated, axis=1, keepdims=True) + EPSILON)
    normed = (floated * inverse * gain_ref[...]).astype(jnp.bfloat16)
    for (row, column), out_ref in zip(cuts, out_refs):
        rows, columns = out_ref.shape
        out_ref[...] = normed[row : row + rows, column : column + columns]


def norm(tokens, gain, cuts):
    rows, width = tokens.shape
    return pl.pallas_call(
        functools.partial(norm_kernel, [cut[:2] for cut in cuts]),
        out_shape=[jax.ShapeDtypeStruct(cut[2:], jnp.bfloat16) for cut in cuts],
        compiler_params=pltpu.CompilerParams(vmem_limit_bytes=16 * MIB),
        cost_estimate=pl.CostEstimate(
            flops=5 * rows * width, bytes_accessed=4 * rows * width, transcendentals=rows
        ),
        name="norm",
    )(tokens, gain.reshape(1, width))


def gate_up_kernel(places, devices, rows, depth, qblock, ins, *refs):
    piece_refs = refs[:ins]
    code_refs = refs[ins : ins + 2 * SPLIT]
    gate_scale_ref, up_scale_ref = refs[ins + 2 * SPLIT : ins + 2 * SPLIT + 2]
    out_refs = refs[ins + 2 * SPLIT + 2 : -1]
    held = refs[-1]
    span = code_refs[0].shape[0]

    @pl.when(pl.program_id(0) == 0)
    def _():
        for index, (at, start) in enumerate(places):
            k, columns = index % devices, piece_refs[at].shape[1]
            left = index // devices * columns
            held[k * rows : (k + 1) * rows, left : left + columns] = piece_refs[at][
                start : start + rows, :
            ]

    def weight(refs_of_codes, scales, at):
        parts = []
        for row in range(at, at + depth, qblock):
            codes = refs_of_codes[row // span][row % span : row % span + qblock, :]
            parts.append(codes * scales[row // qblock : row // qblock + 1, :])
        return jnp.concatenate(parts, axis=0)

    gate_scales = gate_scale_ref[...].astype(jnp.bfloat16)
    up_scales = up_scale_ref[...].astype(jnp.bfloat16)
    gate = up = None
    for at in range(0, SPLIT * span, depth):
        left = held[:, at : at + depth]
        right = weight(code_refs[:SPLIT], gate_scales, at)
        term = jnp.dot(left, right, preferred_element_type=jnp.float32)
        gate = term if gate is None else gate + term
        right = weight(code_refs[SPLIT:], up_scales, at)
        term = jnp.dot(left, right, preferred_element_type=jnp.float32)
        up = term if up is None else up + term
    hidden = (gate / (1.0 + jnp.exp(-gate)) * up).astype(jnp.bfloat16)
    per = devices // len(out_refs)
    for index, out_ref in enumerate(out_refs):
        out_ref[...] = hidden[index * per * rows : (index + 1) * per * rows]


def gate_up(pieces, devices, rows, per, gate_codes, gate_scales, up_codes, up_scales):
    arrays, places = distinct(pieces)
    width, local = gate_codes.shape
    blocks = gate_scales.shape[0]
    tile = 256
    codes = split_blocks(width, tile, 0)
    scales = pl.BlockSpec((blocks, tile), lambda i: (0, i))
    return pl.pallas_call(
        functools.partial(
            gate_up_kernel, places, devices, rows, 1024, width // blocks, len(arrays)
        ),
        grid=(local // tile,),
        in_specs=whole_blocks(arrays) + codes + codes + [scales, scales],
        out_specs=[pl.BlockSpec((per * rows, tile), lambda i: (0, i))] * (devices // per),
        out_shape=[jax.ShapeDtypeStruct((per * rows, local), jnp.bfloat16)] * (devices // per),
        scratch_shapes=[pltpu.VMEM((devices * rows, width), jnp.bfloat16)],
        compiler_params=pltpu.CompilerParams(
            dimension_semantics=("arbitrary",), vmem_limit_bytes=40 * MIB
        ),
        cost_estimate=pl.CostEstimate(
            flops=4 * devices * rows * width * local,
            bytes_accessed=4 * width * local,
            transcendentals=devices * rows * local,
        ),
        name="gate_up",
    )(*arrays, *[gate_codes] * SPLIT, *[up_codes] * SPLIT, gate_scales, up_scales)


def rotate_kernel(places, layout, rows, factor, ins, sign_ref, *refs):
    devices = len(places)
    piece_refs = refs[:ins]
    table_ref = refs[ins]
    out_refs = refs[ins + 1 : -1]
    held = refs[-1]
    local = piece_refs[0].shape[1]
    block = table_ref.shape[0]
    inner = local // block
    count = devices * inner
    for k, (source, start) in enumerate(places):
        sign = sign_ref[0, k].astype(jnp.bfloat16)
        for q in range(inner):
            at = (k * inner + q) * rows
            held[at : at + rows, :] = (
                piece_refs[source][start : start + rows, q * block : (q + 1) * block] * sign
            )
    for start in range(0, block, 256):
        stop = min(start + 256, block)
        product = jnp.dot(
            held[...], table_ref[:, start:stop], preferred_element_type=jnp.float32
        )
        values = [product[index * rows : (index + 1) * rows] for index in range(count)]
        stride = 1
        while stride < count:
            values = [
                values[index] + values[index ^ stride]
                if not index & stride
                else values[index ^ stride] - values[index]
                for index in range(count)
            ]
            stride *= 2
        for k in range(devices):
            scale = sign_ref[1, k] * factor
            at, low = layout[k][0], layout[k][1] * rows
            for q in range(inner):
                out_refs[at][low : low + rows, q * block + start : q * block + stop] = (
                    values[k * inner + q] * scale
                ).astype(jnp.bfloat16)


def rotate(pieces, layout, rows, signs, table):
    devices = len(pieces)
    arrays, places = distinct(pieces)
    local = arrays[0].shape[1]
    block = table.shape[0]
    vmem = pl.BlockSpec(memory_space=pltpu.VMEM)
    return pl.pallas_call(
        functools.partial(
            rotate_kernel, places, layout, rows, (devices * local) ** (-0.5), len(arrays)
        ),
        in_specs=[pl.BlockSpec(memory_space=pltpu.SMEM)] + [vmem] * (len(arrays) + 1),
        out_specs=[vmem] * (1 + max(layout)[0]),
        out_shape=shapes_of(layout, rows, local),
        scratch_shapes=[pltpu.VMEM((devices * rows * local // block, block), jnp.bfloat16)],
        compiler_params=pltpu.CompilerParams(vmem_limit_bytes=40 * MIB),
        cost_estimate=pl.CostEstimate(
            flops=2 * devices * rows * local * block,
            bytes_accessed=4 * devices * rows * local,
            transcendentals=devices * rows * local,
        ),
        name="rotate",
    )(signs, *arrays, table)


def down_kernel(places, rows, group, order, ins, *refs):
    devices = len(places)
    piece_refs = refs[:ins]
    code_refs = refs[ins : ins + SPLIT]
    scale_ref, keep_ref, send_ref, held, weight = refs[ins + SPLIT :]
    half = devices // 2

    @pl.when(pl.program_id(0) == 0)
    def _():
        for place, k in enumerate(order):
            at, start = places[k]
            held[place * rows : (place + 1) * rows, :] = piece_refs[at][start : start + rows, :]

    depth, tile = code_refs[0].shape
    pack = 16
    repeat = math.lcm(group, pack)
    pack_rows = lax.broadcasted_iota(jnp.int32, (pack, tile), 0)
    scales = scale_ref[...].astype(jnp.bfloat16)
    masks = {}

    def first_rows(cut):
        if cut not in masks:
            mask = jnp.where(pack_rows < cut, 1.0, 0.0)
            masks[cut] = (mask.astype(jnp.bfloat16), (1.0 - mask).astype(jnp.bfloat16))
        return masks[cut]

    total = None
    for part in range(SPLIT):
        for at in range(part * depth, (part + 1) * depth, repeat):
            steps = []
            for row in range(at, at + repeat, pack):
                first, last = row // group, (row + pack - 1) // group
                step = jnp.broadcast_to(scales[first : first + 1, :], (pack, tile))
                if last != first:
                    head, rest = first_rows(last * group - row)
                    step = step * head + scales[last : last + 1, :] * rest
                steps.append(step)
            low = at - part * depth
            codes = code_refs[part][low : low + repeat, :]
            weight[at : at + repeat, :] = codes * jnp.concatenate(steps, axis=0)
        term = jnp.dot(
            held[:, part * depth : (part + 1) * depth],
            weight[part * depth : (part + 1) * depth, :],
            preferred_element_type=jnp.float32,
        )
        total = term if total is None else total + term
    keep_ref[...] = total[: half * rows]
    send_ref[...] = total[half * rows :].astype(jnp.bfloat16)


def down(pieces, rows, strides, first_column, columns, codes, scales):
    devices = len(pieces)
    arrays, places = distinct(pieces)
    local = codes.shape[0]
    blocks = scales.shape[0]
    tile = 512
    skip = first_column // tile
    levels = len(strides)
    order = sorted(
        range(devices),
        key=lambda k: sum(1 << (levels - 1 - i) for i, stride in enumerate(strides) if k & stride),
    )
    out_rows = devices // 2 * rows
    return pl.pallas_call(
        functools.partial(down_kernel, places, rows, local // blocks, order, len(arrays)),
        grid=(columns // tile,),
        in_specs=whole_blocks(arrays)
        + split_blocks(local, tile, skip)
        + [pl.BlockSpec((blocks, tile), lambda i: (0, i + skip))],
        out_specs=[pl.BlockSpec((out_rows, tile), lambda i: (0, i))] * 2,
        out_shape=[
            jax.ShapeDtypeStruct((out_rows, columns), jnp.float32),
            jax.ShapeDtypeStruct((out_rows, columns), jnp.bfloat16),
        ],
        scratch_shapes=[
            pltpu.VMEM((devices * rows, local), jnp.bfloat16),
            pltpu.VMEM((local, tile), jnp.bfloat16),
        ],
        compiler_params=pltpu.CompilerParams(
            dimension_semantics=("arbitrary",), vmem_limit_bytes=40 * MIB
        ),
        cost_estimate=pl.CostEstimate(
            flops=2 * devices * rows * columns * local,
            bytes_accessed=2 * columns * local,
            transcendentals=0,
        ),
        name="down",
    )(*arrays, *[codes] * SPLIT, scales)


def add_share(shares, stride):
    keep, send = shares
    return keep + exchange(send, stride).astype(jnp.float32)


def split_share(total):
    half = total.shape[0] // 2
    return total[:half], total[half:].astype(jnp.bfloat16)


def sum_over_devices(shares, strides):
    for stride in strides:
        total = add_share(shares, stride)
        shares = split_share(total)
    return total


def block_order(local, group):
    order = local // group
    while order > 32:
        order //= 2
    return order


def shards_piped(
    tokens, norm_gain, gate_codes, gate_scales, up_codes, up_scales, down_codes, down_scales
):
    devices = lax.axis_size(AXIS)
    width = tokens.shape[1]
    local = gate_codes.shape[1]
    group = down_codes.shape[0] // down_scales.shape[0]
    rows = tokens.shape[0] // 2
    table = np.kron(walsh(block_order(local, group)), hadamard_small())
    table = jnp.asarray(table.astype(ml_dtypes.bfloat16))

    grid = walsh(devices)
    both = np.stack(
        [[grid[me], [grid[me ^ k, me] for k in range(devices)]] for me in range(devices)]
    )
    signs = lax.dynamic_index_in_dim(
        jnp.asarray(both, jnp.float32), lax.axis_index(AXIS), 0, keepdims=False
    )
    weights = (gate_codes, gate_scales, up_codes, up_scales)

    half = width // 2
    near_far, far_near = [1, 4, 2], [4, 2, 1]
    left, right, own = norm(
        tokens,
        norm_gain,
        [(0, 0, rows, half), (0, half, rows, half), (rows, 0, rows, width)],
    )
    first = gather_doubling(left, near_far) + gather_doubling(right, far_near)
    near, straight = gather_flat_start(after(own, first[-1][0], first[devices - 1][0]), devices)

    arrays = gate_up(first, devices, rows, 1, *weights)
    hidden = swap_direct(arrays)
    near, straight = after((near, straight), arrays[1])
    second = gather_flat_end(near, straight)
    later_arrays = gate_up(second, devices, rows, 1, *weights)
    later_hidden = swap_direct(later_arrays)

    layout = single_layout(devices)
    hidden = all_after(hidden, later_arrays[1])
    arrays = rotate(hidden, layout, rows, signs, table)
    rotated = swap_direct(arrays)
    later_hidden = all_after(later_hidden, arrays[1])
    later_arrays = rotate(later_hidden, layout, rows, signs, table)
    later_rotated = swap_direct(later_arrays)
    rotated = all_after(rotated, later_arrays[1])

    def contract(pieces, strides, first_column, columns):
        return down(pieces, rows, strides, first_column, columns, down_codes, down_scales)

    order, other = [1, 2, 4], [2, 1, 4]
    above = split_share(add_share(contract(rotated, order, 0, width), order[0]))
    left = contract(all_after(later_rotated, above[1]), order, 0, half)
    above = split_share(add_share((above[0], above[1]), order[1]))
    right = contract(all_after(later_rotated, left[1], above[1]), other, half, half)
    above = add_share(above, order[2])
    for step in range(len(order)):
        left_total = add_share(left, order[step])
        right_total = add_share((right[0], after(right[1], left_total)), other[step])
        left, right = split_share(left_total), split_share(right_total)
    below = jnp.concatenate([left_total, right_total], axis=1)
    total = jnp.concatenate([above, below], axis=0)
    return (tokens.astype(jnp.float32) + total).astype(jnp.bfloat16)


def dequantize(codes, scales):
    blocks = scales.shape[0]
    height, width = codes.shape
    spread = codes.astype(jnp.float32).reshape(blocks, height // blocks, width) * scales[:, None, :]
    return spread.reshape(height, width).astype(jnp.bfloat16)


def shards_plain(
    tokens, norm_gain, gate_codes, gate_scales, up_codes, up_scales, down_codes, down_scales
):
    floated = tokens.astype(jnp.float32)
    normed = (
        floated
        * lax.rsqrt(jnp.mean(floated * floated, axis=1, keepdims=True) + EPSILON)
        * norm_gain
    ).astype(jnp.bfloat16)
    gate_weight = dequantize(gate_codes, gate_scales)
    up_weight = dequantize(up_codes, up_scales)
    down_weight = dequantize(down_codes, down_scales)
    piece = lax.all_gather(normed, AXIS, axis=0, tiled=True)
    gate = jnp.dot(piece, gate_weight, preferred_element_type=jnp.float32)
    upward = jnp.dot(piece, up_weight, preferred_element_type=jnp.float32)
    hidden = (jax.nn.silu(gate) * upward).astype(jnp.bfloat16)
    total_rows, local_width = hidden.shape
    devices = lax.axis_size(AXIS)
    local_walsh = down_scales.shape[0]
    group = down_codes.shape[0] // local_walsh
    blocks = hidden.astype(jnp.float32).reshape(total_rows, local_walsh, group)
    small_table = jnp.asarray(hadamard_small(), jnp.float32)
    local_table = jnp.asarray(walsh(local_walsh), jnp.float32)
    blocks = jnp.einsum("tia,ac->tic", blocks, small_table, precision=lax.Precision.HIGHEST)
    blocks = jnp.einsum("ji,tic->tjc", local_table, blocks, precision=lax.Precision.HIGHEST)
    blocks = blocks.reshape(total_rows, local_width)
    position = lax.axis_index(AXIS)
    for level in range(devices.bit_length() - 1):
        partner = exchange(blocks.astype(jnp.bfloat16), 1 << level).astype(blocks.dtype)
        signed = (1 - 2 * (position >> level & 1)).astype(jnp.float32)
        blocks = partner + signed * blocks
    rotated = (blocks * (devices * local_width) ** (-0.5)).astype(jnp.bfloat16)
    summed = lax.psum_scatter(
        jnp.dot(rotated, down_weight, preferred_element_type=jnp.float32),
        AXIS,
        scatter_dimension=0,
        tiled=True,
    )
    return (floated + summed).astype(jnp.bfloat16)


def shards(tokens, norm_gain, gate_codes, *others):
    devices = lax.axis_size(AXIS)
    rows, width = tokens.shape
    local = gate_codes.shape[1]
    if devices == 8 and rows % 32 == 0 and local % 896 == 0 and width % 1024 == 0:
        return shards_piped(tokens, norm_gain, gate_codes, *others)
    return shards_plain(tokens, norm_gain, gate_codes, *others)


def solution(mesh):
    return jax.shard_map(
        shards,
        mesh=mesh,
        in_specs=(
            P(("groups", "tensor", "dp"), None),
            P(),
            P(None, "tensor"),
            P(None, "tensor"),
            P(None, "tensor"),
            P(None, "tensor"),
            P("tensor", None),
            P("tensor", None),
        ),
        out_specs=P(("groups", "tensor", "dp"), None),
        check_vma=False,
    )
```

time: 399 us -> 340 us (0.85)
  Pallas kernels: 157 us -> 93.4 us
  waiting for transfers between devices: 133 us -> 158 us
  starting transfers between devices: 101 us -> 79.5 us
    pallas_call x9 -> x5, Pallas kernels: 102 us -> 62.4 us  [the longest x2 55 us: gate_up(): pl.pallas_call(functools.partial(gate_up_kernel, places, devices, rows, 1...]
    ppermute x67 -> x48, waiting for transfers between devices: 133 us -> 158 us  [exchange(): lax.ppermute(value, AXIS, [(i, i ^ stride) for i in range(lax.axis_size(A...]
    pallas_call x5 -> x3, Pallas kernels: 54.6 us -> 31 us  [down(): pl.pallas_call(functools.partial(down_kernel, places, rows, local // bloc...]
    ppermute x67 -> x48, starting transfers between devices: 101 us -> 79.5 us  [exchange(): lax.ppermute(value, AXIS, [(i, i ^ stride) for i in range(lax.axis_size(A...]
  transfers between devices with their start and end apart: 67 -> 48, of which waited for: 26 -> 23; matrix products, arithmetic and copies ran while one was open for 1% -> 0% of each run, Pallas kernels for 30% -> 22%
where the time goes in v3:
time: 340 us; the launch traced here: 339 us
  waiting for transfers between devices  158 us (46%)
  Pallas kernels  93.4 us (27%)
  starting transfers between devices  79.5 us (23%)
  local copies, waits for them, and re-layouts  5.49 us (2%)
    ppermute x48, waiting for transfers between devices, exchange(): lax.ppermute(value, AXIS, [(i, i ^ stride) for i in range(lax.axis_size(A...  158 us
    ppermute x48, starting transfers between devices, exchange(): lax.ppermute(value, AXIS, [(i, i ^ stride) for i in range(lax.axis_size(A...  79.5 us
    pallas_call x2, Pallas kernels, gate_up(): pl.pallas_call(functools.partial(gate_up_kernel, places, devices, rows, 1...  55 us
    pallas_call x3, Pallas kernels, down(): pl.pallas_call(functools.partial(down_kernel, places, rows, local // bloc...  31 us
    pallas_call x2, Pallas kernels, rotate(): pl.pallas_call(functools.partial(rotate_kernel, places, layout, rows, (de...  7.1 us
  transfers between devices with their start and end apart: 48, of which 23 were waited for; matrix products, arithmetic and copies ran while one was open for 0% of the time, Pallas kernels for 22%

profile of v3, /device:TPU:0, one launch (start us, length us, event | category | flops | bytes accessed | tf_op | source)
XLA Modules:
  0.0 339.5 jit_solution(4712610659537888249)
XLA Ops:
  11.5 9.0 %collective-permute-done.3 = bf16[32,2048]{1,0:T(8,128)(2,1)S(1)} collective-permute-done((bf16[32,2048]{1,0:T(8,128)(2,1)S(1)}, bf16[32,2048]{1,0:T(8,128)(2,1)S(1)}, u32[]{:S(2)}, u32[]{:S(2)}) %collective-permute-start.3) | collective-permute-done | bytes 131104 | tf_op jit(solution)/shard_map/ppermute | solution.py:41
  20.6 9.9 %collective-permute-done.4 = bf16[64,2048]{1,0:T(8,128)(2,1)S(1)} collective-permute-done((bf16[64,2048]{1,0:T(8,128)(2,1)S(1)}, bf16[64,2048]{1,0:T(8,128)(2,1)S(1)}, u32[]{:S(2)}, u32[]{:S(2)}) %collective-permute-start.4) | collective-permute-done | bytes 262176 | tf_op jit(solution)/shard_map/ppermute | solution.py:41
  31.2 13.3 %collective-permute-done.5.refs_3_ = bf16[128,2048]{1,0:T(8,128)(2,1)S(1)} collective-permute-done((bf16[128,2048]{1,0:T(8,128)(2,1)S(1)}, bf16[128,2048]{1,0:T(8,128)(2,1)S(1)}, u32[]{:S(2)}, u32[]{:S(2)}) %collective-permute-start.5) | collective-permute-done | bytes 524320 | tf_op jit(solution)/shard_map/ppermute | solution.py:41
  50.7 27.8 %gate_up.2 = (bf16[32,3584]{1,0:T(8,128)(2,1)S(1)}, bf16[32,3584]{1,0:T(8,128)(2,1)S(1)}, bf16[32,3584]{1,0:T(8,128)(2,1)}, bf16[32,3584]{1,0:T(8,128)(2,1)}, bf...) custom-call(bf16[128,2048]{1,0:T(8,128)(2,1)S(1)} %constant_dynamic-, ...), custom_call_target="tpu_custom_call" | custom-call | flops 15032385536 | bytes 58720256 | tf_op jit(solution)/shard_map/gate_up/pallas_call | solution.py:226
  89.1 7.6 %collective-permute-done.7.refs_2_ = bf16[32,3584]{1,0:T(8,128)(2,1)} collective-permute-done((bf16[32,3584]{1,0:T(8,128)(2,1)}, bf16[32,3584]{1,0:T(8,128)(2,1)}, u32[]{:S(2)}, u32[]{:S(2)}) %collective-permute-start.7) | collective-permute-done | bytes 229408 | tf_op jit(solution)/shard_map/ppermute | solution.py:41
  102.9 6.6 %collective-permute-done.17.refs_3_ = bf16[96,4096]{1,0:T(8,128)(2,1)S(1)} collective-permute-done((bf16[96,4096]{1,0:T(8,128)(2,1)}, bf16[96,4096]{1,0:T(8,128)(2,1)S(1)}, u32[]{:S(2)}, u32[]{:S(2)}) %collective-permute-start.17) | collective-permute-done | bytes 786464 | tf_op jit(solution)/shard_map/ppermute | solution.py:41
  109.5 5.7 %collective-permute-start.12 = (bf16[32,3584]{1,0:T(8,128)(2,1)}, bf16[32,3584]{1,0:T(8,128)(2,1)S(1)}, u32[]{:S(2)}, u32[]{:S(2)}) collective-permute-start(bf16[32,3584]{1,0:T(8,128)(2,1)} %copy-done.6), channel_id=1, source_target_pairs={{0,14},{2,12},{4,10},{6,8},{8,6},{10,4},{12,2},{14,0},{1,15},{3,13... | collective-permute-start | bytes 688136 | tf_op jit(solution)/shard_map/ppermute | solution.py:41
  115.2 27.2 %gate_up.3 = (bf16[32,3584]{1,0:T(8,128)(2,1)S(1)}, bf16[32,3584]{1,0:T(8,128)(2,1)S(1)}, bf16[32,3584]{1,0:T(8,128)(2,1)S(1)}, bf16[32,3584]{1,0:T(8,128)(2,1)S...) custom-call(bf16[32,4096]{1,0:T(8,128)(2,1)S(1)} %get-tuple-element., ...), custom_call_target="tpu_custom_call" | custom-call | flops 15032385536 | bytes 58720256 | tf_op jit(solution)/shard_map/gate_up/pallas_call | solution.py:226
  151.3 4.9 %collective-permute-done.19.refs_2_ = bf16[32,3584]{1,0:T(8,128)(2,1)S(1)} collective-permute-done((bf16[32,3584]{1,0:T(8,128)(2,1)S(1)}, bf16[32,3584]{1,0:T(8,128)(2,1)S(1)}, u32[]{:S(2)}, u32[]{:S(2)}) %collective-permute-start.19) | collective-permute-done | bytes 229408 | tf_op jit(solution)/shard_map/ppermute | solution.py:41
  158.9 5.2 %collective-permute-done.20.refs_3_ = bf16[32,3584]{1,0:T(8,128)(2,1)S(1)} collective-permute-done((bf16[32,3584]{1,0:T(8,128)(2,1)S(1)}, bf16[32,3584]{1,0:T(8,128)(2,1)S(1)}, u32[]{:S(2)}, u32[]{:S(2)}) %collective-permute-start.20) | collective-permute-done | bytes 229408 | tf_op jit(solution)/shard_map/ppermute | solution.py:41
  164.7 5.1 %collective-permute-done.26.refs_2_ = bf16[32,3584]{1,0:T(8,128)(2,1)S(1)} collective-permute-done((bf16[32,3584]{1,0:T(8,128)(2,1)S(1)}, bf16[32,3584]{1,0:T(8,128)(2,1)S(1)}, u32[]{:S(2)}, u32[]{:S(2)}) %collective-permute-start.26) | collective-permute-done | bytes 229408 | tf_op jit(solution)/shard_map/ppermute | solution.py:41
  169.8 5.9 %collective-permute-done.27.refs_3_ = bf16[32,3584]{1,0:T(8,128)(2,1)S(1)} collective-permute-done((bf16[32,3584]{1,0:T(8,128)(2,1)S(1)}, bf16[32,3584]{1,0:T(8,128)(2,1)S(1)}, u32[]{:S(2)}, u32[]{:S(2)}) %collective-permute-start.27) | collective-permute-done | bytes 229408 | tf_op jit(solution)/shard_map/ppermute | solution.py:41
  176.2 22.3 %collective-permute-done.29.refs_5_ = bf16[32,3584]{1,0:T(8,128)(2,1)S(1)} collective-permute-done((bf16[32,3584]{1,0:T(8,128)(2,1)S(1)}, bf16[32,3584]{1,0:T(8,128)(2,1)S(1)}, u32[]{:S(2)}, u32[]{:S(2)}) %collective-permute-start.29) | collective-permute-done | bytes 229408 | tf_op jit(solution)/shard_map/ppermute | solution.py:41
  207.1 10.8 %collective-permute-done.21.refs_4_ = bf16[32,3584]{1,0:T(8,128)(2,1)S(1)} collective-permute-done((bf16[32,3584]{1,0:T(8,128)(2,1)S(1)}, bf16[32,3584]{1,0:T(8,128)(2,1)S(1)}, u32[]{:S(2)}, u32[]{:S(2)}) %collective-permute-start.21) | collective-permute-done | bytes 229408 | tf_op jit(solution)/shard_map/ppermute | solution.py:41
  221.9 14.8 %down.3 = (f32[128,4096]{1,0:T(8,128)S(1)}, bf16[128,4096]{1,0:T(8,128)(2,1)S(1)}) custom-call(bf16[32,3584]{1,0:T(8,128)(2,1)S(1)} %get-tuple-element.145.refs_0_, bf16[32,3584]{1,0:T(8,128)(2,1)S(1)} %collective-permute-done.18.refs_1_, bf16[32,3584]{1,0:T(8,128)(2,1)S(1)} %collective-permute-done.19.refs_2_, ...), custom_call_target="tpu_custom_call" | custom-call | flops 7516192768 | bytes 29360128 | tf_op jit(solution)/shard_map/down/pallas_call | solution.py:375
  238.2 5.5 %collective-permute-start.36 = (bf16[32,3584]{1,0:T(8,128)(2,1)S(1)}, bf16[32,3584]{1,0:T(8,128)(2,1)S(1)}, u32[]{:S(2)}, u32[]{:S(2)}) collective-permute-start(bf16[32,3584]{1,0:T(8,128)(2,1)S(1)} %get-tuple-element.156), channel_id=1, source_target_pairs={{0,4},{2,6},{4,0},{6,2},{8,12},{10,14},{12,8},{14,10},{1,5},{3,7},... | collective-permute-start | bytes 688136 | tf_op jit(solution)/shard_map/ppermute | solution.py:41
  268.2 7.6 %collective-permute-start.33 = (bf16[64,4096]{1,0:T(8,128)(2,1)S(1)}, bf16[64,4096]{1,0:T(8,128)(2,1)S(1)}, u32[]{:S(2)}, u32[]{:S(2)}) collective-permute-start(bf16[64,4096]{1,0:T(8,128)(2,1)S(1)} %slice.78), channel_id=1, source_target_pairs={{0,4},{2,6},{4,0},{6,2},{8,12},{10,14},{12,8},{14,10},{1,5},{3,7},... | collective-permute-start | bytes 1572872 | tf_op jit(solution)/shard_map/ppermute | solution.py:41
  275.9 8.2 %down.4 = (f32[128,2048]{1,0:T(8,128)S(1)}, bf16[128,2048]{1,0:T(8,128)(2,1)S(1)}) custom-call(bf16[32,3584]{1,0:T(8,128)(2,1)S(1)} %get-tuple-element.172.refs_0_, bf16[32,3584]{1,0:T(8,128)(2,1)S(1)} %collective-permute-done.35.refs_1_, bf16[32,3584]{1,0:T(8,128)(2,1)S(1)} %collective-permute-done.36.refs_2_, ...), custom_call_target="tpu_custom_call" | custom-call | flops 3758096384 | bytes 14680064 | tf_op jit(solution)/shard_map/down/pallas_call | solution.py:375
  285.4 7.9 %collective-permute-done.42 = bf16[128,2048]{1,0:T(8,128)(2,1)S(1)} collective-permute-done((bf16[128,2048]{1,0:T(8,128)(2,1)S(1)}, bf16[128,2048]{1,0:T(8,128)(2,1)S(1)}, u32[]{:S(2)}, u32[]{:S(2)}) %collective-permute-start.42) | collective-permute-done | bytes 524320 | tf_op jit(solution)/shard_map/ppermute | solution.py:41
  293.5 6.8 %collective-permute-start.43 = (bf16[64,2048]{1,0:T(8,128)(2,1)S(1)}, bf16[64,2048]{1,0:T(8,128)(2,1)S(1)}, u32[]{:S(2)}, u32[]{:S(2)}) collective-permute-start(bf16[64,2048]{1,0:T(8,128)(2,1)S(1)} %slice.80), channel_id=1, source_target_pairs={{0,4},{2,6},{4,0},{6,2},{8,12},{10,14},{12,8},{14,10},{1,5},{3,7},... | collective-permute-start | bytes 786440 | tf_op jit(solution)/shard_map/ppermute | solution.py:41
  300.3 8.0 %down.5 = (f32[128,2048]{1,0:T(8,128)S(1)}, bf16[128,2048]{1,0:T(8,128)(2,1)S(1)}) custom-call(bf16[32,3584]{1,0:T(8,128)(2,1)S(1)} %get-tuple-element.172.refs_0_, bf16[32,3584]{1,0:T(8,128)(2,1)S(1)} %collective-permute-done.35.refs_1_, bf16[32,3584]{1,0:T(8,128)(2,1)S(1)} %collective-permute-done.36.refs_2_, ...), custom_call_target="tpu_custom_call" | custom-call | flops 3758096384 | bytes 14680064 | tf_op jit(solution)/shard_map/down/pallas_call | solution.py:375
  311.5 14.0 %collective-permute-done.45 = bf16[128,2048]{1,0:T(8,128)(2,1)S(1)} collective-permute-done((bf16[128,2048]{1,0:T(8,128)(2,1)S(1)}, bf16[128,2048]{1,0:T(8,128)(2,1)S(1)}, u32[]{:S(2)}, u32[]{:S(2)}) %collective-permute-start.45) | collective-permute-done | bytes 524320 | tf_op jit(solution)/shard_map/ppermute | solution.py:41
  325.8 6.3 %collective-permute-done.46 = bf16[64,2048]{1,0:T(8,128)(2,1)S(1)} collective-permute-done((bf16[64,2048]{1,0:T(8,128)(2,1)S(1)}, bf16[64,2048]{1,0:T(8,128)(2,1)S(1)}, u32[]{:S(2)}, u32[]{:S(2)}) %collective-permute-start.46) | collective-permute-done | bytes 262176 | tf_op jit(solution)/shard_map/ppermute | solution.py:41
  332.4 6.2 %collective-permute-done.47 = bf16[32,2048]{1,0:T(8,128)(2,1)S(1)} collective-permute-done((bf16[32,2048]{1,0:T(8,128)(2,1)S(1)}, bf16[32,2048]{1,0:T(8,128)(2,1)S(1)}, u32[]{:S(2)}, u32[]{:S(2)}) %collective-permute-start.47) | collective-permute-done | bytes 131104 | tf_op jit(solution)/shard_map/ppermute | solution.py:41
  (127 shorter events, 92.3 us)
Async XLA Ops:
  44.8 36.5 %collective-permute-start.16 = (bf16[32,4096]{1,0:T(8,128)(2,1)S(1)}, bf16[32,4096]{1,0:T(8,128)(2,1)S(1)}, u32[]{:S(2)}, u32[]{:S(2)}) collective-permute-start(bf16[32,4096]{1,0:T(8,128)(2,1)S(1)} %get-tuple-element.107.refs_0_), channel_id=1, source_target_pairs={{0,12},{2,14},{4,8},{6,10},{8,4},{10,6},{12,0},{14,2},{1,13},{3,15... | collective-permute-start | bytes 786440 | tf_op jit(solution)/shard_map/ppermute | solution.py:41
  48.3 33.0 %collective-permute-start.15 = (bf16[32,4096]{1,0:T(8,128)(2,1)S(1)}, bf16[32,4096]{1,0:T(8,128)(2,1)S(1)}, u32[]{:S(2)}, u32[]{:S(2)}) collective-permute-start(bf16[32,4096]{1,0:T(8,128)(2,1)S(1)} %get-tuple-element.107.refs_0_), channel_id=1, source_target_pairs={{0,8},{2,10},{4,12},{6,14},{8,0},{10,2},{12,4},{14,6},{1,9},{3,11}... | collective-permute-start | bytes 786440 | tf_op jit(solution)/shard_map/ppermute | solution.py:41
  48.3 33.0 %collective-permute-start.14 = (bf16[32,4096]{1,0:T(8,128)(2,1)S(1)}, bf16[32,4096]{1,0:T(8,128)(2,1)S(1)}, u32[]{:S(2)}, u32[]{:S(2)}) collective-permute-start(bf16[32,4096]{1,0:T(8,128)(2,1)S(1)} %get-tuple-element.107.refs_0_), channel_id=1, source_target_pairs={{0,4},{2,6},{4,0},{6,2},{8,12},{10,14},{12,8},{14,10},{1,5},{3,7},... | collective-permute-start | bytes 786440 | tf_op jit(solution)/shard_map/ppermute | solution.py:41
  49.2 32.2 %collective-permute-start.13 = (bf16[32,4096]{1,0:T(8,128)(2,1)S(1)}, bf16[32,4096]{1,0:T(8,128)(2,1)S(1)}, u32[]{:S(2)}, u32[]{:S(2)}) collective-permute-start(bf16[32,4096]{1,0:T(8,128)(2,1)S(1)} %get-tuple-element.107.refs_0_), channel_id=1, source_target_pairs={{0,2},{2,0},{4,6},{6,4},{8,10},{10,8},{12,14},{14,12},{1,3},{3,1},... | collective-permute-start | bytes 786440 | tf_op jit(solution)/shard_map/ppermute | solution.py:41
  82.3 27.2 %collective-permute-start.17 = (bf16[96,4096]{1,0:T(8,128)(2,1)}, bf16[96,4096]{1,0:T(8,128)(2,1)S(1)}, u32[]{:S(2)}, u32[]{:S(2)}) collective-permute-start(bf16[96,4096]{1,0:T(8,128)(2,1)} %pad_maximum_fusion), channel_id=1, source_target_pairs={{0,2},{2,0},{4,6},{6,4},{8,10},{10,8},{12,14},{14,12},{1,3},{3,1},... | collective-permute-start | bytes 2359304 | tf_op jit(solution)/shard_map/ppermute | solution.py:41
  86.5 56.0 %collective-permute-start.6 = (bf16[32,3584]{1,0:T(8,128)(2,1)S(1)}, bf16[32,3584]{1,0:T(8,128)(2,1)S(1)}, u32[]{:S(2)}, u32[]{:S(2)}) collective-permute-start(bf16[32,3584]{1,0:T(8,128)(2,1)S(1)} %get-tuple-element.98), channel_id=1, source_target_pairs={{0,2},{2,0},{4,6},{6,4},{8,10},{10,8},{12,14},{14,12},{1,3},{3,1},... | collective-permute-start | bytes 688136 | tf_op jit(solution)/shard_map/ppermute | solution.py:41
  86.9 55.5 %collective-permute-start.9 = (bf16[32,3584]{1,0:T(8,128)(2,1)}, bf16[32,3584]{1,0:T(8,128)(2,1)S(1)}, u32[]{:S(2)}, u32[]{:S(2)}) collective-permute-start(bf16[32,3584]{1,0:T(8,128)(2,1)} %copy-done.9), channel_id=1, source_target_pairs={{0,8},{2,10},{4,12},{6,14},{8,0},{10,2},{12,4},{14,6},{1,9},{3,11}... | collective-permute-start | bytes 688136 | tf_op jit(solution)/shard_map/ppermute | solution.py:41
  96.7 45.8 %collective-permute-start.10 = (bf16[32,3584]{1,0:T(8,128)(2,1)}, bf16[32,3584]{1,0:T(8,128)(2,1)S(1)}, u32[]{:S(2)}, u32[]{:S(2)}) collective-permute-start(bf16[32,3584]{1,0:T(8,128)(2,1)} %copy-done.8), channel_id=1, source_target_pairs={{0,10},{2,8},{4,14},{6,12},{8,2},{10,0},{12,6},{14,4},{1,11},{3,9}... | collective-permute-start | bytes 688136 | tf_op jit(solution)/shard_map/ppermute | solution.py:41
  101.3 41.2 %collective-permute-start.11 = (bf16[32,3584]{1,0:T(8,128)(2,1)}, bf16[32,3584]{1,0:T(8,128)(2,1)S(1)}, u32[]{:S(2)}, u32[]{:S(2)}) collective-permute-start(bf16[32,3584]{1,0:T(8,128)(2,1)} %copy-done.7), channel_id=1, source_target_pairs={{0,12},{2,14},{4,8},{6,10},{8,4},{10,6},{12,0},{14,2},{1,13},{3,15... | collective-permute-start | bytes 688136 | tf_op jit(solution)/shard_map/ppermute | solution.py:41
  109.5 32.9 %collective-permute-start.12 = (bf16[32,3584]{1,0:T(8,128)(2,1)}, bf16[32,3584]{1,0:T(8,128)(2,1)S(1)}, u32[]{:S(2)}, u32[]{:S(2)}) collective-permute-start(bf16[32,3584]{1,0:T(8,128)(2,1)} %copy-done.6), channel_id=1, source_target_pairs={{0,14},{2,12},{4,10},{6,8},{8,6},{10,4},{12,2},{14,0},{1,15},{3,13... | collective-permute-start | bytes 688136 | tf_op jit(solution)/shard_map/ppermute | solution.py:41
  149.5 26.3 %collective-permute-start.27 = (bf16[32,3584]{1,0:T(8,128)(2,1)S(1)}, bf16[32,3584]{1,0:T(8,128)(2,1)S(1)}, u32[]{:S(2)}, u32[]{:S(2)}) collective-permute-start(bf16[32,3584]{1,0:T(8,128)(2,1)S(1)} %get-tuple-element.131), channel_id=1, source_target_pairs={{0,6},{2,4},{4,2},{6,0},{8,14},{10,12},{12,10},{14,8},{1,7},{3,5},... | collective-permute-start | bytes 688136 | tf_op jit(solution)/shard_map/ppermute | solution.py:41
  151.3 24.8 %collective-permute-start.28 = (bf16[32,3584]{1,0:T(8,128)(2,1)S(1)}, bf16[32,3584]{1,0:T(8,128)(2,1)S(1)}, u32[]{:S(2)}, u32[]{:S(2)}) collective-permute-start(bf16[32,3584]{1,0:T(8,128)(2,1)S(1)} %get-tuple-element.132), channel_id=1, source_target_pairs={{0,8},{2,10},{4,12},{6,14},{8,0},{10,2},{12,4},{14,6},{1,9},{3,11}... | collective-permute-start | bytes 688136 | tf_op jit(solution)/shard_map/ppermute | solution.py:41
  156.2 42.3 %collective-permute-start.29 = (bf16[32,3584]{1,0:T(8,128)(2,1)S(1)}, bf16[32,3584]{1,0:T(8,128)(2,1)S(1)}, u32[]{:S(2)}, u32[]{:S(2)}) collective-permute-start(bf16[32,3584]{1,0:T(8,128)(2,1)S(1)} %get-tuple-element.133), channel_id=1, source_target_pairs={{0,10},{2,8},{4,14},{6,12},{8,2},{10,0},{12,6},{14,4},{1,11},{3,9}... | collective-permute-start | bytes 688136 | tf_op jit(solution)/shard_map/ppermute | solution.py:41
  164.1 34.4 %collective-permute-start.30 = (bf16[32,3584]{1,0:T(8,128)(2,1)S(1)}, bf16[32,3584]{1,0:T(8,128)(2,1)S(1)}, u32[]{:S(2)}, u32[]{:S(2)}) collective-permute-start(bf16[32,3584]{1,0:T(8,128)(2,1)S(1)} %get-tuple-element.134), channel_id=1, source_target_pairs={{0,12},{2,14},{4,8},{6,10},{8,4},{10,6},{12,0},{14,2},{1,13},{3,15... | collective-permute-start | bytes 688136 | tf_op jit(solution)/shard_map/ppermute | solution.py:41
  169.8 28.8 %collective-permute-start.31 = (bf16[32,3584]{1,0:T(8,128)(2,1)S(1)}, bf16[32,3584]{1,0:T(8,128)(2,1)S(1)}, u32[]{:S(2)}, u32[]{:S(2)}) collective-permute-start(bf16[32,3584]{1,0:T(8,128)(2,1)S(1)} %get-tuple-element.135), channel_id=1, source_target_pairs={{0,14},{2,12},{4,10},{6,8},{8,6},{10,4},{12,2},{14,0},{1,15},{3,13... | collective-permute-start | bytes 688136 | tf_op jit(solution)/shard_map/ppermute | solution.py:41
  175.7 24.8 %collective-permute-start.25 = (bf16[32,3584]{1,0:T(8,128)(2,1)S(1)}, bf16[32,3584]{1,0:T(8,128)(2,1)S(1)}, u32[]{:S(2)}, u32[]{:S(2)}) collective-permute-start(bf16[32,3584]{1,0:T(8,128)(2,1)S(1)} %get-tuple-element.112), channel_id=1, source_target_pairs={{0,2},{2,0},{4,6},{6,4},{8,10},{10,8},{12,14},{14,12},{1,3},{3,1},... | collective-permute-start | bytes 688136 | tf_op jit(solution)/shard_map/ppermute | solution.py:41
  176.2 41.8 %collective-permute-start.21 = (bf16[32,3584]{1,0:T(8,128)(2,1)S(1)}, bf16[32,3584]{1,0:T(8,128)(2,1)S(1)}, u32[]{:S(2)}, u32[]{:S(2)}) collective-permute-start(bf16[32,3584]{1,0:T(8,128)(2,1)S(1)} %get-tuple-element.125), channel_id=1, source_target_pairs={{0,8},{2,10},{4,12},{6,14},{8,0},{10,2},{12,4},{14,6},{1,9},{3,11}... | collective-permute-start | bytes 688136 | tf_op jit(solution)/shard_map/ppermute | solution.py:41
  198.5 23.3 %collective-permute-start.22 = (bf16[32,3584]{1,0:T(8,128)(2,1)S(1)}, bf16[32,3584]{1,0:T(8,128)(2,1)S(1)}, u32[]{:S(2)}, u32[]{:S(2)}) collective-permute-start(bf16[32,3584]{1,0:T(8,128)(2,1)S(1)} %get-tuple-element.126), channel_id=1, source_target_pairs={{0,10},{2,8},{4,14},{6,12},{8,2},{10,0},{12,6},{14,4},{1,11},{3,9}... | collective-permute-start | bytes 688136 | tf_op jit(solution)/shard_map/ppermute | solution.py:41
  198.5 23.3 %collective-permute-start.23 = (bf16[32,3584]{1,0:T(8,128)(2,1)S(1)}, bf16[32,3584]{1,0:T(8,128)(2,1)S(1)}, u32[]{:S(2)}, u32[]{:S(2)}) collective-permute-start(bf16[32,3584]{1,0:T(8,128)(2,1)S(1)} %get-tuple-element.127), channel_id=1, source_target_pairs={{0,12},{2,14},{4,8},{6,10},{8,4},{10,6},{12,0},{14,2},{1,13},{3,15... | collective-permute-start | bytes 688136 | tf_op jit(solution)/shard_map/ppermute | solution.py:41
  198.6 23.3 %collective-permute-start.24 = (bf16[32,3584]{1,0:T(8,128)(2,1)S(1)}, bf16[32,3584]{1,0:T(8,128)(2,1)S(1)}, u32[]{:S(2)}, u32[]{:S(2)}) collective-permute-start(bf16[32,3584]{1,0:T(8,128)(2,1)S(1)} %get-tuple-element.128), channel_id=1, source_target_pairs={{0,14},{2,12},{4,10},{6,8},{8,6},{10,4},{12,2},{14,0},{1,15},{3,13... | collective-permute-start | bytes 688136 | tf_op jit(solution)/shard_map/ppermute | solution.py:41
  236.7 26.4 %collective-permute-start.32 = (bf16[128,4096]{1,0:T(8,128)(2,1)S(1)}, bf16[128,4096]{1,0:T(8,128)(2,1)S(1)}, u32[]{:S(2)}, u32[]{:S(2)}) collective-permute-start(bf16[128,4096]{1,0:T(8,128)(2,1)S(1)} %get-tuple-element.154), channel_id=1, source_target_pairs={{0,2},{2,0},{4,6},{6,4},{8,10},{10,8},{12,14},{14,12},{1,3},{3,1},... | collective-permute-start | bytes 3145736 | tf_op jit(solution)/shard_map/ppermute | solution.py:41
  243.7 32.2 %collective-permute-start.35 = (bf16[32,3584]{1,0:T(8,128)(2,1)S(1)}, bf16[32,3584]{1,0:T(8,128)(2,1)S(1)}, u32[]{:S(2)}, u32[]{:S(2)}) collective-permute-start(bf16[32,3584]{1,0:T(8,128)(2,1)S(1)} %get-tuple-element.144), channel_id=1, source_target_pairs={{0,2},{2,0},{4,6},{6,4},{8,10},{10,8},{12,14},{14,12},{1,3},{3,1},... | collective-permute-start | bytes 688136 | tf_op jit(solution)/shard_map/ppermute | solution.py:41
  250.2 25.6 %collective-permute-start.39 = (bf16[32,3584]{1,0:T(8,128)(2,1)S(1)}, bf16[32,3584]{1,0:T(8,128)(2,1)S(1)}, u32[]{:S(2)}, u32[]{:S(2)}) collective-permute-start(bf16[32,3584]{1,0:T(8,128)(2,1)S(1)} %get-tuple-element.159), channel_id=1, source_target_pairs={{0,10},{2,8},{4,14},{6,12},{8,2},{10,0},{12,6},{14,4},{1,11},{3,9}... | collective-permute-start | bytes 688136 | tf_op jit(solution)/shard_map/ppermute | solution.py:41
  308.4 23.9 %collective-permute-start.34 = (bf16[32,4096]{1,0:T(8,128)(2,1)S(1)}, bf16[32,4096]{1,0:T(8,128)(2,1)S(1)}, u32[]{:S(2)}, u32[]{:S(2)}) collective-permute-start(bf16[32,4096]{1,0:T(8,128)(2,1)S(1)} %slice.81), channel_id=1, source_target_pairs={{0,8},{2,10},{4,12},{6,14},{8,0},{10,2},{12,4},{14,6},{1,9},{3,11}... | collective-permute-start | bytes 786440 | tf_op jit(solution)/shard_map/ppermute | solution.py:41
  (35 other events, 517.4 us)

commit v4 on v3

v4 whole, which is shorter than its diff:
```python
import functools
import math

import jax
import jax.numpy as jnp
import ml_dtypes
import numpy as np
from jax import lax
from jax.experimental import pallas as pl
from jax.experimental.pallas import tpu as pltpu
from jax.sharding import PartitionSpec as P

EPSILON = 1e-05
AXIS = "tensor"
MIB = 1 << 20


def hadamard_small():
    modulus = 13
    residues = [number * number % modulus for number in range(1, modulus)]
    legendre = [0] + [1 if number in residues else -1 for number in range(1, modulus)]
    conference = np.zeros((modulus + 1, modulus + 1), np.int64)
    conference[0, 1:] = 1
    conference[1:, 0] = 1
    for row in range(1, modulus + 1):
        for column in range(1, modulus + 1):
            conference[row, column] = legendre[(column - row) % modulus]
    plus_block = np.array([[1, 1], [1, -1]])
    zero_block = np.array([[1, -1], [-1, -1]])
    return np.kron(conference, plus_block) + np.kron(np.eye(modulus + 1, dtype=np.int64), zero_block)


def walsh(order):
    table = np.ones((1, 1), np.int64)
    while table.shape[0] < order:
        table = np.kron(np.array([[1, 1], [1, -1]]), table)
    return table


def exchange(value, stride):
    return lax.ppermute(value, AXIS, [(i, i ^ stride) for i in range(lax.axis_size(AXIS))])


def after(value, *earlier):
    return lax.optimization_barrier((value, earlier))[0]


def swap_direct(arrays):
    out = list(arrays)
    for k in range(1, len(arrays)):
        out[k] = exchange(arrays[k], k)
    return [(array, 0) for array in out]


def all_after(pieces, *earlier):
    arrays, places = distinct(pieces)
    arrays = after(arrays, *earlier)
    return [(arrays[at], start) for at, start in places]


def distinct(pieces):
    arrays = []
    for array, _ in pieces:
        if not any(other is array for other in arrays):
            arrays.append(array)
    index = {id(array): at for at, array in enumerate(arrays)}
    return arrays, [(index[id(array)], start) for array, start in pieces]


SPLIT = 2


def split_blocks(height, tile, skip):
    return [
        pl.BlockSpec((height // SPLIT, tile), functools.partial(lambda part, i: (part, i + skip), part))
        for part in range(SPLIT)
    ]


def whole_blocks(arrays):
    return [pl.BlockSpec(array.shape, lambda i: (0, 0)) for array in arrays]


def norm_kernel(cuts, tokens_ref, gain_ref, *out_refs):
    floated = tokens_ref[...].astype(jnp.float32)
    inverse = lax.rsqrt(jnp.mean(floated * floated, axis=1, keepdims=True) + EPSILON)
    normed = (floated * inverse * gain_ref[...]).astype(jnp.bfloat16)
    for (row, column), out_ref in zip(cuts, out_refs):
        rows, columns = out_ref.shape
        out_ref[...] = normed[row : row + rows, column : column + columns]


def norm(tokens, gain, cuts):
    rows, width = tokens.shape
    return pl.pallas_call(
        functools.partial(norm_kernel, [cut[:2] for cut in cuts]),
        out_shape=[jax.ShapeDtypeStruct(cut[2:], jnp.bfloat16) for cut in cuts],
        compiler_params=pltpu.CompilerParams(vmem_limit_bytes=16 * MIB),
        cost_estimate=pl.CostEstimate(
            flops=5 * rows * width, bytes_accessed=4 * rows * width, transcendentals=rows
        ),
        name="norm",
    )(tokens, gain.reshape(1, width))


def gate_up_kernel(devices, rows, depth, qblock, me_ref, rows_ref, *refs):
    code_refs = refs[: 2 * SPLIT]
    gate_scale_ref, up_scale_ref = refs[2 * SPLIT : 2 * SPLIT + 2]
    out_refs = refs[2 * SPLIT + 2 : -1]
    held = refs[-1]
    span = code_refs[0].shape[0]

    @pl.when(pl.program_id(0) == 0)
    def _():
        for k in range(devices):
            start = pl.multiple_of((me_ref[0] ^ k) * rows, rows)
            held[k * rows : (k + 1) * rows, :] = rows_ref[pl.ds(start, rows), :]

    def weight(refs_of_codes, scales, at):
        parts = []
        for row in range(at, at + depth, qblock):
            codes = refs_of_codes[row // span][row % span : row % span + qblock, :]
            step = scales[row // qblock : row // qblock + 1, :]
            parts.append((codes.astype(jnp.float32) * step).astype(jnp.bfloat16))
        return jnp.concatenate(parts, axis=0)

    gate = up = None
    for at in range(0, SPLIT * span, depth):
        left = held[:, at : at + depth]
        right = weight(code_refs[:SPLIT], gate_scale_ref, at)
        term = jnp.dot(left, right, preferred_element_type=jnp.float32)
        gate = term if gate is None else gate + term
        right = weight(code_refs[SPLIT:], up_scale_ref, at)
        term = jnp.dot(left, right, preferred_element_type=jnp.float32)
        up = term if up is None else up + term
    hidden = (gate / (1.0 + jnp.exp(-gate)) * up).astype(jnp.bfloat16)
    for k, out_ref in enumerate(out_refs):
        out_ref[...] = hidden[k * rows : (k + 1) * rows]


def gate_up(me, gathered, devices, gate_codes, gate_scales, up_codes, up_scales):
    rows = gathered.shape[0] // devices
    width, local = gate_codes.shape
    blocks = gate_scales.shape[0]
    tile = 256
    codes = split_blocks(width, tile, 0)
    scales = pl.BlockSpec((blocks, tile), lambda i: (0, i))
    return pl.pallas_call(
        functools.partial(
            gate_up_kernel, devices, rows, 512, width // blocks
        ),
        grid=(local // tile,),
        in_specs=[pl.BlockSpec(memory_space=pltpu.SMEM)]
        + whole_blocks([gathered])
        + codes
        + codes
        + [scales, scales],
        out_specs=[pl.BlockSpec((rows, tile), lambda i: (0, i))] * devices,
        out_shape=[jax.ShapeDtypeStruct((rows, local), jnp.bfloat16)] * devices,
        scratch_shapes=[pltpu.VMEM((devices * rows, width), jnp.bfloat16)],
        compiler_params=pltpu.CompilerParams(
            dimension_semantics=("arbitrary",), vmem_limit_bytes=40 * MIB
        ),
        cost_estimate=pl.CostEstimate(
            flops=4 * devices * rows * width * local,
            bytes_accessed=4 * width * local,
            transcendentals=devices * rows * local,
        ),
        name="gate_up",
    )(me, gathered, *[gate_codes] * SPLIT, *[up_codes] * SPLIT, gate_scales, up_scales)


def rotate_kernel(places, rows, factor, ins, sign_ref, *refs):
    devices = len(places)
    piece_refs = refs[:ins]
    table_ref = refs[ins]
    out_refs = refs[ins + 1 : -1]
    held = refs[-1]
    local = piece_refs[0].shape[1]
    block = table_ref.shape[0]
    inner = local // block
    count = devices * inner
    for k, (source, start) in enumerate(places):
        sign = sign_ref[0, k].astype(jnp.bfloat16)
        for q in range(inner):
            at = (k * inner + q) * rows
            held[at : at + rows, :] = (
                piece_refs[source][start : start + rows, q * block : (q + 1) * block] * sign
            )
    for start in range(0, block, 256):
        stop = min(start + 256, block)
        product = jnp.dot(
            held[...], table_ref[:, start:stop], preferred_element_type=jnp.float32
        )
        values = [product[index * rows : (index + 1) * rows] for index in range(count)]
        stride = 1
        while stride < count:
            values = [
                values[index] + values[index ^ stride]
                if not index & stride
                else values[index ^ stride] - values[index]
                for index in range(count)
            ]
            stride *= 2
        for k in range(devices):
            scale = sign_ref[1, k] * factor
            for q in range(inner):
                out_refs[k][:, q * block + start : q * block + stop] = (
                    values[k * inner + q] * scale
                ).astype(jnp.bfloat16)


def rotate(pieces, rows, signs, table):
    devices = len(pieces)
    arrays, places = distinct(pieces)
    local = arrays[0].shape[1]
    block = table.shape[0]
    vmem = pl.BlockSpec(memory_space=pltpu.VMEM)
    return pl.pallas_call(
        functools.partial(
            rotate_kernel, places, rows, (devices * local) ** (-0.5), len(arrays)
        ),
        in_specs=[pl.BlockSpec(memory_space=pltpu.SMEM)] + [vmem] * (len(arrays) + 1),
        out_specs=[vmem] * devices,
        out_shape=[jax.ShapeDtypeStruct((rows, local), jnp.bfloat16)] * devices,
        scratch_shapes=[pltpu.VMEM((devices * rows * local // block, block), jnp.bfloat16)],
        compiler_params=pltpu.CompilerParams(vmem_limit_bytes=40 * MIB),
        cost_estimate=pl.CostEstimate(
            flops=2 * devices * rows * local * block,
            bytes_accessed=4 * devices * rows * local,
            transcendentals=devices * rows * local,
        ),
        name="rotate",
    )(signs, *arrays, table)


def down_kernel(places, rows, group, ins, me_ref, *refs):
    devices = len(places)
    piece_refs = refs[:ins]
    code_refs = refs[ins : ins + SPLIT]
    scale_ref, out_ref, held, weight = refs[ins + SPLIT :]

    @pl.when(pl.program_id(0) == 0)
    def _():
        for k in range(devices):
            at, start = places[k]
            into = pl.multiple_of((me_ref[0] ^ k) * rows, rows)
            held[pl.ds(into, rows), :] = piece_refs[at][start : start + rows, :]

    depth, tile = code_refs[0].shape
    repeat = math.lcm(group, 16)
    low_rows = lax.broadcasted_iota(jnp.int32, (8, tile), 0)
    total = None
    for part in range(SPLIT):
        for at in range(part * depth, (part + 1) * depth, repeat):
            steps = []
            for row in range(at, at + repeat, 8):
                first, last = row // group, (row + 7) // group
                step = jnp.broadcast_to(scale_ref[first : first + 1, :], (8, tile))
                if last != first:
                    other = jnp.broadcast_to(scale_ref[last : last + 1, :], (8, tile))
                    step = jnp.where(low_rows < last * group - row, step, other)
                steps.append(step)
            low = at - part * depth
            codes = code_refs[part][low : low + repeat, :].astype(jnp.float32)
            weight[at : at + repeat, :] = (codes * jnp.concatenate(steps, axis=0)).astype(
                jnp.bfloat16
            )
        term = jnp.dot(
            held[:, part * depth : (part + 1) * depth],
            weight[part * depth : (part + 1) * depth, :],
            preferred_element_type=jnp.float32,
        )
        total = term if total is None else total + term
    out_ref[...] = total.astype(jnp.bfloat16)


def down(me, pieces, rows, first_column, columns, codes, scales):
    devices = len(pieces)
    arrays, places = distinct(pieces)
    local = codes.shape[0]
    blocks = scales.shape[0]
    tile = 512
    skip = first_column // tile
    return pl.pallas_call(
        functools.partial(down_kernel, places, rows, local // blocks, len(arrays)),
        grid=(columns // tile,),
        in_specs=[pl.BlockSpec(memory_space=pltpu.SMEM)]
        + whole_blocks(arrays)
        + split_blocks(local, tile, skip)
        + [pl.BlockSpec((blocks, tile), lambda i: (0, i + skip))],
        out_specs=pl.BlockSpec((devices * rows, tile), lambda i: (0, i)),
        out_shape=jax.ShapeDtypeStruct((devices * rows, columns), jnp.bfloat16),
        scratch_shapes=[
            pltpu.VMEM((devices * rows, local), jnp.bfloat16),
            pltpu.VMEM((local, tile), jnp.bfloat16),
        ],
        compiler_params=pltpu.CompilerParams(
            dimension_semantics=("arbitrary",), vmem_limit_bytes=40 * MIB
        ),
        cost_estimate=pl.CostEstimate(
            flops=2 * devices * rows * columns * local,
            bytes_accessed=2 * columns * local,
            transcendentals=0,
        ),
        name="down",
    )(me, *arrays, *[codes] * SPLIT, scales)


def block_order(local, group):
    order = local // group
    while order > 32:
        order //= 2
    return order


def shards_piped(
    tokens, norm_gain, gate_codes, gate_scales, up_codes, up_scales, down_codes, down_scales
):
    devices = lax.axis_size(AXIS)
    width = tokens.shape[1]
    local = gate_codes.shape[1]
    group = down_codes.shape[0] // down_scales.shape[0]
    rows = tokens.shape[0] // 2
    table = np.kron(walsh(block_order(local, group)), hadamard_small())
    table = jnp.asarray(table.astype(ml_dtypes.bfloat16))

    grid = walsh(devices)
    both = np.stack(
        [[grid[me], [grid[me ^ k, me] for k in range(devices)]] for me in range(devices)]
    )
    signs = lax.dynamic_index_in_dim(
        jnp.asarray(both, jnp.float32), lax.axis_index(AXIS), 0, keepdims=False
    )
    weights = (gate_codes, gate_scales, up_codes, up_scales)

    me = lax.axis_index(AXIS).reshape(1)
    half = width // 2
    own = norm(tokens, norm_gain, [(0, 0, rows, width), (rows, 0, rows, width)])
    first = lax.all_gather(own[0], AXIS, axis=0, tiled=True)
    second = lax.all_gather(after(own[1], first), AXIS, axis=0, tiled=True)

    arrays = gate_up(me, first, devices, *weights)
    hidden = swap_direct(arrays)
    later_arrays = gate_up(me, after(second, arrays[1]), devices, *weights)
    later_hidden = swap_direct(later_arrays)

    hidden = all_after(hidden, later_arrays[1])
    arrays = rotate(hidden, rows, signs, table)
    rotated = swap_direct(arrays)
    later_hidden = all_after(later_hidden, arrays[1])
    later_arrays = rotate(later_hidden, rows, signs, table)
    later_rotated = swap_direct(later_arrays)
    rotated = all_after(rotated, later_arrays[1])

    def contract(pieces, first_column, columns):
        return down(me, pieces, rows, first_column, columns, down_codes, down_scales)

    def scatter(shares):
        return lax.psum_scatter(shares, AXIS, scatter_dimension=0, tiled=True)

    shares = contract(rotated, 0, width)
    above = scatter(shares)
    left = contract(all_after(later_rotated, above), 0, half)
    right = contract(all_after(later_rotated, left), half, half)
    residual = tokens.astype(jnp.float32)

    def add(start, columns, sums):
        base = residual[start : start + rows, columns : columns + sums.shape[1]]
        return (base + sums.astype(jnp.float32)).astype(jnp.bfloat16)

    above = add(0, 0, above)
    left = add(rows, 0, scatter(left))
    right = add(rows, half, after(scatter(right), left))
    return jnp.concatenate([above, jnp.concatenate([left, right], axis=1)], axis=0)


def dequantize(codes, scales):
    blocks = scales.shape[0]
    height, width = codes.shape
    spread = codes.astype(jnp.float32).reshape(blocks, height // blocks, width) * scales[:, None, :]
    return spread.reshape(height, width).astype(jnp.bfloat16)


def shards_plain(
    tokens, norm_gain, gate_codes, gate_scales, up_codes, up_scales, down_codes, down_scales
):
    floated = tokens.astype(jnp.float32)
    normed = (
        floated
        * lax.rsqrt(jnp.mean(floated * floated, axis=1, keepdims=True) + EPSILON)
        * norm_gain
    ).astype(jnp.bfloat16)
    gate_weight = dequantize(gate_codes, gate_scales)
    up_weight = dequantize(up_codes, up_scales)
    down_weight = dequantize(down_codes, down_scales)
    piece = lax.all_gather(normed, AXIS, axis=0, tiled=True)
    gate = jnp.dot(piece, gate_weight, preferred_element_type=jnp.float32)
    upward = jnp.dot(piece, up_weight, preferred_element_type=jnp.float32)
    hidden = (jax.nn.silu(gate) * upward).astype(jnp.bfloat16)
    total_rows, local_width = hidden.shape
    devices = lax.axis_size(AXIS)
    local_walsh = down_scales.shape[0]
    group = down_codes.shape[0] // local_walsh
    blocks = hidden.astype(jnp.float32).reshape(total_rows, local_walsh, group)
    small_table = jnp.asarray(hadamard_small(), jnp.float32)
    local_table = jnp.asarray(walsh(local_walsh), jnp.float32)
    blocks = jnp.einsum("tia,ac->tic", blocks, small_table, precision=lax.Precision.HIGHEST)
    blocks = jnp.einsum("ji,tic->tjc", local_table, blocks, precision=lax.Precision.HIGHEST)
    blocks = blocks.reshape(total_rows, local_width)
    position = lax.axis_index(AXIS)
    for level in range(devices.bit_length() - 1):
        partner = exchange(blocks.astype(jnp.bfloat16), 1 << level).astype(blocks.dtype)
        signed = (1 - 2 * (position >> level & 1)).astype(jnp.float32)
        blocks = partner + signed * blocks
    rotated = (blocks * (devices * local_width) ** (-0.5)).astype(jnp.bfloat16)
    summed = lax.psum_scatter(
        jnp.dot(rotated, down_weight, preferred_element_type=jnp.float32),
        AXIS,
        scatter_dimension=0,
        tiled=True,
    )
    return (floated + summed).astype(jnp.bfloat16)


def shards(tokens, norm_gain, gate_codes, *others):
    devices = lax.axis_size(AXIS)
    rows, width = tokens.shape
    local = gate_codes.shape[1]
    if devices == 8 and rows % 32 == 0 and local % 896 == 0 and width % 1024 == 0:
        return shards_piped(tokens, norm_gain, gate_codes, *others)
    return shards_plain(tokens, norm_gain, gate_codes, *others)


def solution(mesh):
    return jax.shard_map(
        shards,
        mesh=mesh,
        in_specs=(
            P(("groups", "tensor", "dp"), None),
            P(),
            P(None, "tensor"),
            P(None, "tensor"),
            P(None, "tensor"),
            P(None, "tensor"),
            P("tensor", None),
            P("tensor", None),
        ),
        out_specs=P(("groups", "tensor", "dp"), None),
        check_vma=False,
    )
```

time: 340 us -> 495 us (1.46)
  waiting for transfers between devices: 158 us -> 314 us
  starting transfers between devices: 79.5 us -> 49.4 us
  local copies, waits for them, and re-layouts: 5.49 us -> 19 us
  between operations: 0.4 us -> 13.3 us
    reduce_scatter x0 -> x3, waiting for transfers between devices: none -> 147 us  [scatter(): return lax.psum_scatter(shares, AXIS, scatter_dimension=0, tiled=True)]
    all_gather x0 -> x2, waiting for transfers between devices: none -> 76 us  [the longest x1 52.1 us: shards_piped(): first = lax.all_gather(own[0], AXIS, axis=0, tiled=True)]
    ppermute x48 -> x28, waiting for transfers between devices: 158 us -> 90.2 us  [exchange(): lax.ppermute(value, AXIS, [(i, i ^ stride) for i in range(lax.axis_size(A...]
    ppermute x48 -> x28, starting transfers between devices: 79.5 us -> 49 us  [exchange(): lax.ppermute(value, AXIS, [(i, i ^ stride) for i in range(lax.axis_size(A...]
    unnamed x25 -> x52, local copies, waits for them, and re-layouts: 4.6 us -> 18.3 us
  transfers between devices with their start and end apart: 48 -> 33, of which waited for: 23 -> 15; matrix products, arithmetic and copies ran while one was open for 0% -> 0% of each run, Pallas kernels for 22% -> 15%
where the time goes in v4:
time: 495 us
  waiting for transfers between devices  314 us (63%)
  Pallas kernels  96.6 us (20%)
  starting transfers between devices  49.4 us (10%)
  local copies, waits for them, and re-layouts  19 us (4%)
  between operations  13.3 us (3%)
    reduce_scatter x3, waiting for transfers between devices, scatter(): return lax.psum_scatter(shares, AXIS, scatter_dimension=0, tiled=True)  147 us
    ppermute x28, waiting for transfers between devices, exchange(): lax.ppermute(value, AXIS, [(i, i ^ stride) for i in range(lax.axis_size(A...  90.2 us
    pallas_call x2, Pallas kernels, gate_up(): pl.pallas_call(functools.partial(gate_up_kernel, devices, rows, 512, widt...  55.6 us
    all_gather x1, waiting for transfers between devices, shards_piped(): first = lax.all_gather(own[0], AXIS, axis=0, tiled=True)  52.1 us
    ppermute x28, starting transfers between devices, exchange(): lax.ppermute(value, AXIS, [(i, i ^ stride) for i in range(lax.axis_size(A...  49 us
    pallas_call x3, Pallas kernels, down(): pl.pallas_call(functools.partial(down_kernel, places, rows, local // bloc...  32.4 us
    all_gather x1, waiting for transfers between devices, shards_piped(): second = lax.all_gather(after(own[1], first), AXIS, axis=0, tiled=True)  23.9 us
    unnamed x52, local copies, waits for them, and re-layouts  18.3 us
  transfers between devices with their start and end apart: 33, of which 15 were waited for; matrix products, arithmetic and copies ran while one was open for 0% of the time, Pallas kernels for 15%

profile of v4, /device:TPU:0, one launch (start us, length us, event | category | flops | bytes accessed | tf_op | source)
XLA Modules:
  0.0 494.6 jit_solution(7710707609742535523)
XLA Ops:
  9.4 52.1 %all-gather.3.cloned.1.call-done.rows_ref = bf16[256,4096]{1,0:T(8,128)(2,1)} async-done(((bf16[32,4096]{1,0:T(8,128)(2,1)}), bf16[256,4096]{1,0:T(8,128)(2,1)}) %all-gather.3.cloned.1.call-update) | async-done | bytes 2097168 | tf_op jit(solution)/shard_map/all_gather | solution.py:340
  65.2 28.2 %gate_up.2 = (bf16[32,3584]{1,0:T(8,128)(2,1)S(1)}, bf16[32,3584]{1,0:T(8,128)(2,1)}, bf16[32,3584]{1,0:T(8,128)(2,1)}, bf16[32,3584]{1,0:T(8,128)(2,1)S(1)}, bf...) custom-call(s32[1]{0:T(128)} %bitcast.me_ref, ...), custom_call_target="tpu_custom_call" | custom-call | flops 15032385536 | bytes 58720256 | tf_op jit(solution)/shard_map/gate_up/pallas_call | solution.py:148
  100.1 23.9 %all-gather.5.cloned.1.call-done.rows_ref = bf16[256,4096]{1,0:T(8,128)(2,1)} async-done(((bf16[32,4096]{1,0:T(8,128)(2,1)}), bf16[256,4096]{1,0:T(8,128)(2,1)}) %all-gather.5.cloned.1.call-update) | async-done | bytes 2097168 | tf_op jit(solution)/shard_map/all_gather | solution.py:341
  130.4 27.4 %gate_up.3 = (bf16[32,3584]{1,0:T(8,128)(2,1)S(1)}, bf16[32,3584]{1,0:T(8,128)(2,1)S(1)}, bf16[32,3584]{1,0:T(8,128)(2,1)S(1)}, bf16[32,3584]{1,0:T(8,128)(2,1)S...) custom-call(s32[1]{0:T(128)} %bitcast.me_ref, ...), custom_call_target="tpu_custom_call" | custom-call | flops 15032385536 | bytes 58720256 | tf_op jit(solution)/shard_map/gate_up/pallas_call | solution.py:148
  158.4 3.0 collective-permute-start.16
  164.9 3.3 rotate.2
  170.7 3.2 collective-permute-done.15.refs_2_
  173.9 3.1 collective-permute-start.20
  177.7 22.6 %collective-permute-done.17.refs_4_ = bf16[32,3584]{1,0:T(8,128)(2,1)S(1)} collective-permute-done((bf16[32,3584]{1,0:T(8,128)(2,1)S(1)}, bf16[32,3584]{1,0:T(8,128)(2,1)S(1)}, u32[]{:S(2)}, u32[]{:S(2)}) %collective-permute-start.17) | collective-permute-done | bytes 229408 | tf_op jit(solution)/shard_map/ppermute | solution.py:41
  205.1 12.3 %collective-permute-start.13 = (bf16[32,3584]{1,0:T(8,128)(2,1)S(1)}, bf16[32,3584]{1,0:T(8,128)(2,1)S(1)}, u32[]{:S(2)}, u32[]{:S(2)}) collective-permute-start(bf16[32,3584]{1,0:T(8,128)(2,1)S(1)} %get-tuple-element.110), channel_id=1, source_target_pairs={{0,14},{2,12},{4,10},{6,8},{8,6},{10,4},{12,2},{14,0},{1,15},{3,13... | collective-permute-start | bytes 688136 | tf_op jit(solution)/shard_map/ppermute | solution.py:41
  217.4 12.5 %collective-permute-done.10.refs_4_ = bf16[32,3584]{1,0:T(8,128)(2,1)S(1)} collective-permute-done((bf16[32,3584]{1,0:T(8,128)(2,1)S(1)}, bf16[32,3584]{1,0:T(8,128)(2,1)S(1)}, u32[]{:S(2)}, u32[]{:S(2)}) %collective-permute-start.10) | collective-permute-done | bytes 229408 | tf_op jit(solution)/shard_map/ppermute | solution.py:41
  229.9 4.7 collective-permute-done.11.refs_5_
  234.6 4.2 rotate.3
  241.6 14.8 %down.3 = bf16[256,4096]{1,0:T(8,128)(2,1)S(1)} custom-call(s32[1]{0:T(128)} %bitcast.me_ref, bf16[32,3584]{1,0:T(8,128)(2,1)S(1)} %get-tuple-element.127.refs_0_, bf16[32,3584]{1,0:T(8,128)(2,1)S(1)} %collective-permute-done.7.refs_1_, bf16[32,3584]{1,0:T(8,128)(2,1)S(1)} %collective-permute-done.8.refs_2_, ...), custom_call_target="tpu_custom_call" | custom-call | flops 7516192768 | bytes 29360128 | tf_op jit(solution)/shard_map/down/pallas_call | solution.py:285
  262.2 2.6 collective-permute-start.24
  265.5 2.6 collective-permute-start.26
  268.1 8.9 %collective-permute-done.22.refs_2_ = bf16[32,3584]{1,0:T(8,128)(2,1)S(1)} collective-permute-done((bf16[32,3584]{1,0:T(8,128)(2,1)}, bf16[32,3584]{1,0:T(8,128)(2,1)S(1)}, u32[]{:S(2)}, u32[]{:S(2)}) %collective-permute-start.22) | collective-permute-done | bytes 229408 | tf_op jit(solution)/shard_map/ppermute | solution.py:41
  277.6 11.1 %collective-permute-done.23.refs_3_ = bf16[32,3584]{1,0:T(8,128)(2,1)S(1)} collective-permute-done((bf16[32,3584]{1,0:T(8,128)(2,1)}, bf16[32,3584]{1,0:T(8,128)(2,1)S(1)}, u32[]{:S(2)}, u32[]{:S(2)}) %collective-permute-start.23) | collective-permute-done | bytes 229408 | tf_op jit(solution)/shard_map/ppermute | solution.py:41
  288.8 23.5 %collective-permute-done.25.refs_5_ = bf16[32,3584]{1,0:T(8,128)(2,1)S(1)} collective-permute-done((bf16[32,3584]{1,0:T(8,128)(2,1)}, bf16[32,3584]{1,0:T(8,128)(2,1)S(1)}, u32[]{:S(2)}, u32[]{:S(2)}) %collective-permute-start.25) | collective-permute-done | bytes 229408 | tf_op jit(solution)/shard_map/ppermute | solution.py:41
  313.7 33.1 %reduce-scatter.4.cloned.1.call-done = bf16[32,4096]{1,0:T(8,128)(2,1)} async-done(((bf16[256,4096]{1,0:T(8,128)(2,1)}), bf16[32,4096]{1,0:T(8,128)(2,1)}) %reduce-scatter.4.cloned.1.call-update) | async-done | bytes 262160 | tf_op jit(solution)/shard_map/reduce_scatter | solution.py:360
  348.6 8.8 %down.4 = bf16[256,2048]{1,0:T(8,128)(2,1)} custom-call(s32[1]{0:T(128)} %bitcast.me_ref, bf16[32,3584]{1,0:T(8,128)(2,1)S(1)} %get-tuple-element.150.refs_0_, bf16[32,3584]{1,0:T(8,128)(2,1)S(1)} %collective-permute-done.21.refs_1_, bf16[32,3584]{1,0:T(8,128)(2,1)S(1)} %collective-permute-done.22.refs_2_, ...), custom_call_target="tpu_custom_call" | custom-call | flops 3758096384 | bytes 14680064 | tf_op jit(solution)/shard_map/down/pallas_call | solution.py:285
  361.4 8.8 %down.5 = bf16[256,2048]{1,0:T(8,128)(2,1)} custom-call(s32[1]{0:T(128)} %bitcast.me_ref, bf16[32,3584]{1,0:T(8,128)(2,1)S(1)} %get-tuple-element.150.refs_0_, bf16[32,3584]{1,0:T(8,128)(2,1)S(1)} %collective-permute-done.21.refs_1_, bf16[32,3584]{1,0:T(8,128)(2,1)S(1)} %collective-permute-done.22.refs_2_, ...), custom_call_target="tpu_custom_call" | custom-call | flops 3758096384 | bytes 14680064 | tf_op jit(solution)/shard_map/down/pallas_call | solution.py:285
  371.2 49.0 %reduce-scatter.6.cloned.1.call-done = bf16[32,2048]{1,0:T(8,128)(2,1)} async-done(((bf16[256,2048]{1,0:T(8,128)(2,1)}), bf16[32,2048]{1,0:T(8,128)(2,1)}) %reduce-scatter.6.cloned.1.call-update) | async-done | bytes 131088 | tf_op jit(solution)/shard_map/reduce_scatter | solution.py:360
  421.1 65.2 %reduce-scatter.8.cloned.1.call-done = bf16[32,2048]{1,0:T(8,128)(2,1)} async-done(((bf16[256,2048]{1,0:T(8,128)(2,1)}), bf16[32,2048]{1,0:T(8,128)(2,1)}) %reduce-scatter.8.cloned.1.call-update) | async-done | bytes 131088 | tf_op jit(solution)/shard_map/reduce_scatter | solution.py:360
  (113 shorter events, 52.4 us)
Async XLA Ops:
  6.5 55.0 %all-gather.3.cloned.1.call-start = ((), (), s32[]{:S(2)}) async-start(), calls=%async_computation.3 | async-start | bytes 2359296 | tf_op jit(solution)/shard_map/all_gather | solution.py:340
  9.4 114.6 %all-gather.5.cloned.1.call-start = ((), (), s32[]{:S(2)}) async-start(), calls=%async_computation.4 | async-start | bytes 2359296 | tf_op jit(solution)/shard_map/all_gather | solution.py:341
  61.5 285.2 %reduce-scatter.4.cloned.1.call-start = ((), (), s32[]{:S(2)}) async-start(), calls=%async_computation.5 | async-start | bytes 2359296 | tf_op jit(solution)/shard_map/reduce_scatter | solution.py:360
  93.4 30.6 %collective-permute-start = (bf16[32,3584]{1,0:T(8,128)(2,1)}, bf16[32,3584]{1,0:T(8,128)(2,1)S(1)}, u32[]{:S(2)}, u32[]{:S(2)}) collective-permute-start(bf16[32,3584]{1,0:T(8,128)(2,1)} %get-tuple-element.84), channel_id=1, source_target_pairs={{0,2},{2,0},{4,6},{6,4},{8,10},{10,8},{12,14},{14,12},{1,3},{3,1},... | collective-permute-start | bytes 688136 | tf_op jit(solution)/shard_map/ppermute | solution.py:41
  94.2 32.1 %collective-permute-start.1 = (bf16[32,3584]{1,0:T(8,128)(2,1)}, bf16[32,3584]{1,0:T(8,128)(2,1)S(1)}, u32[]{:S(2)}, u32[]{:S(2)}) collective-permute-start(bf16[32,3584]{1,0:T(8,128)(2,1)} %get-tuple-element.85), channel_id=1, source_target_pairs={{0,4},{2,6},{4,0},{6,2},{8,12},{10,14},{12,8},{14,10},{1,5},{3,7},... | collective-permute-start | bytes 688136 | tf_op jit(solution)/shard_map/ppermute | solution.py:41
  95.7 62.1 %collective-permute-start.2 = (bf16[32,3584]{1,0:T(8,128)(2,1)S(1)}, bf16[32,3584]{1,0:T(8,128)(2,1)S(1)}, u32[]{:S(2)}, u32[]{:S(2)}) collective-permute-start(bf16[32,3584]{1,0:T(8,128)(2,1)S(1)} %get-tuple-element.86), channel_id=1, source_target_pairs={{0,6},{2,4},{4,2},{6,0},{8,14},{10,12},{12,10},{14,8},{1,7},{3,5},... | collective-permute-start | bytes 688136 | tf_op jit(solution)/shard_map/ppermute | solution.py:41
  96.9 61.5 %collective-permute-start.3 = (bf16[32,3584]{1,0:T(8,128)(2,1)S(1)}, bf16[32,3584]{1,0:T(8,128)(2,1)S(1)}, u32[]{:S(2)}, u32[]{:S(2)}) collective-permute-start(bf16[32,3584]{1,0:T(8,128)(2,1)S(1)} %get-tuple-element.87), channel_id=1, source_target_pairs={{0,8},{2,10},{4,12},{6,14},{8,0},{10,2},{12,4},{14,6},{1,9},{3,11}... | collective-permute-start | bytes 688136 | tf_op jit(solution)/shard_map/ppermute | solution.py:41
  98.9 59.5 %collective-permute-start.4 = (bf16[32,3584]{1,0:T(8,128)(2,1)S(1)}, bf16[32,3584]{1,0:T(8,128)(2,1)S(1)}, u32[]{:S(2)}, u32[]{:S(2)}) collective-permute-start(bf16[32,3584]{1,0:T(8,128)(2,1)S(1)} %get-tuple-element.88), channel_id=1, source_target_pairs={{0,10},{2,8},{4,14},{6,12},{8,2},{10,0},{12,6},{14,4},{1,11},{3,9}... | collective-permute-start | bytes 688136 | tf_op jit(solution)/shard_map/ppermute | solution.py:41
  124.0 37.4 %collective-permute-start.5 = (bf16[32,3584]{1,0:T(8,128)(2,1)S(1)}, bf16[32,3584]{1,0:T(8,128)(2,1)S(1)}, u32[]{:S(2)}, u32[]{:S(2)}) collective-permute-start(bf16[32,3584]{1,0:T(8,128)(2,1)S(1)} %get-tuple-element.89), channel_id=1, source_target_pairs={{0,12},{2,14},{4,8},{6,10},{8,4},{10,6},{12,0},{14,2},{1,13},{3,15... | collective-permute-start | bytes 688136 | tf_op jit(solution)/shard_map/ppermute | solution.py:41
  126.3 36.5 %collective-permute-start.6 = (bf16[32,3584]{1,0:T(8,128)(2,1)S(1)}, bf16[32,3584]{1,0:T(8,128)(2,1)S(1)}, u32[]{:S(2)}, u32[]{:S(2)}) collective-permute-start(bf16[32,3584]{1,0:T(8,128)(2,1)S(1)} %get-tuple-element.90), channel_id=1, source_target_pairs={{0,14},{2,12},{4,10},{6,8},{8,6},{10,4},{12,2},{14,0},{1,15},{3,13... | collective-permute-start | bytes 688136 | tf_op jit(solution)/shard_map/ppermute | solution.py:41
  161.4 38.9 %collective-permute-start.17 = (bf16[32,3584]{1,0:T(8,128)(2,1)S(1)}, bf16[32,3584]{1,0:T(8,128)(2,1)S(1)}, u32[]{:S(2)}, u32[]{:S(2)}) collective-permute-start(bf16[32,3584]{1,0:T(8,128)(2,1)S(1)} %get-tuple-element.114), channel_id=1, source_target_pairs={{0,8},{2,10},{4,12},{6,14},{8,0},{10,2},{12,4},{14,6},{1,9},{3,11}... | collective-permute-start | bytes 688136 | tf_op jit(solution)/shard_map/ppermute | solution.py:41
  162.8 39.7 %collective-permute-start.18 = (bf16[32,3584]{1,0:T(8,128)(2,1)S(1)}, bf16[32,3584]{1,0:T(8,128)(2,1)S(1)}, u32[]{:S(2)}, u32[]{:S(2)}) collective-permute-start(bf16[32,3584]{1,0:T(8,128)(2,1)S(1)} %get-tuple-element.115), channel_id=1, source_target_pairs={{0,10},{2,8},{4,14},{6,12},{8,2},{10,0},{12,6},{14,4},{1,11},{3,9}... | collective-permute-start | bytes 688136 | tf_op jit(solution)/shard_map/ppermute | solution.py:41
  168.3 36.8 %collective-permute-start.19 = (bf16[32,3584]{1,0:T(8,128)(2,1)S(1)}, bf16[32,3584]{1,0:T(8,128)(2,1)S(1)}, u32[]{:S(2)}, u32[]{:S(2)}) collective-permute-start(bf16[32,3584]{1,0:T(8,128)(2,1)S(1)} %get-tuple-element.116), channel_id=1, source_target_pairs={{0,12},{2,14},{4,8},{6,10},{8,4},{10,6},{12,0},{14,2},{1,13},{3,15... | collective-permute-start | bytes 688136 | tf_op jit(solution)/shard_map/ppermute | solution.py:41
  173.9 43.5 %collective-permute-start.20 = (bf16[32,3584]{1,0:T(8,128)(2,1)S(1)}, bf16[32,3584]{1,0:T(8,128)(2,1)S(1)}, u32[]{:S(2)}, u32[]{:S(2)}) collective-permute-start(bf16[32,3584]{1,0:T(8,128)(2,1)S(1)} %get-tuple-element.117), channel_id=1, source_target_pairs={{0,14},{2,12},{4,10},{6,8},{8,6},{10,4},{12,2},{14,0},{1,15},{3,13... | collective-permute-start | bytes 688136 | tf_op jit(solution)/shard_map/ppermute | solution.py:41
  177.7 52.2 %collective-permute-start.10 = (bf16[32,3584]{1,0:T(8,128)(2,1)S(1)}, bf16[32,3584]{1,0:T(8,128)(2,1)S(1)}, u32[]{:S(2)}, u32[]{:S(2)}) collective-permute-start(bf16[32,3584]{1,0:T(8,128)(2,1)S(1)} %get-tuple-element.107), channel_id=1, source_target_pairs={{0,8},{2,10},{4,12},{6,14},{8,0},{10,2},{12,4},{14,6},{1,9},{3,11}... | collective-permute-start | bytes 688136 | tf_op jit(solution)/shard_map/ppermute | solution.py:41
  200.3 34.2 %collective-permute-start.11 = (bf16[32,3584]{1,0:T(8,128)(2,1)S(1)}, bf16[32,3584]{1,0:T(8,128)(2,1)S(1)}, u32[]{:S(2)}, u32[]{:S(2)}) collective-permute-start(bf16[32,3584]{1,0:T(8,128)(2,1)S(1)} %get-tuple-element.108), channel_id=1, source_target_pairs={{0,10},{2,8},{4,14},{6,12},{8,2},{10,0},{12,6},{14,4},{1,11},{3,9}... | collective-permute-start | bytes 688136 | tf_op jit(solution)/shard_map/ppermute | solution.py:41
  202.6 38.3 %collective-permute-start.12 = (bf16[32,3584]{1,0:T(8,128)(2,1)S(1)}, bf16[32,3584]{1,0:T(8,128)(2,1)S(1)}, u32[]{:S(2)}, u32[]{:S(2)}) collective-permute-start(bf16[32,3584]{1,0:T(8,128)(2,1)S(1)} %get-tuple-element.109), channel_id=1, source_target_pairs={{0,12},{2,14},{4,8},{6,10},{8,4},{10,6},{12,0},{14,2},{1,13},{3,15... | collective-permute-start | bytes 688136 | tf_op jit(solution)/shard_map/ppermute | solution.py:41
  205.1 35.8 %collective-permute-start.13 = (bf16[32,3584]{1,0:T(8,128)(2,1)S(1)}, bf16[32,3584]{1,0:T(8,128)(2,1)S(1)}, u32[]{:S(2)}, u32[]{:S(2)}) collective-permute-start(bf16[32,3584]{1,0:T(8,128)(2,1)S(1)} %get-tuple-element.110), channel_id=1, source_target_pairs={{0,14},{2,12},{4,10},{6,8},{8,6},{10,4},{12,2},{14,0},{1,15},{3,13... | collective-permute-start | bytes 688136 | tf_op jit(solution)/shard_map/ppermute | solution.py:41
  257.7 162.4 %reduce-scatter.6.cloned.1.call-start = ((), (), s32[]{:S(2)}) async-start(), calls=%async_computation.6 | async-start | bytes 1179648 | tf_op jit(solution)/shard_map/reduce_scatter | solution.py:360
  261.3 27.5 %collective-permute-start.23 = (bf16[32,3584]{1,0:T(8,128)(2,1)}, bf16[32,3584]{1,0:T(8,128)(2,1)S(1)}, u32[]{:S(2)}, u32[]{:S(2)}) collective-permute-start(bf16[32,3584]{1,0:T(8,128)(2,1)} %get-tuple-element.137), channel_id=1, source_target_pairs={{0,6},{2,4},{4,2},{6,0},{8,14},{10,12},{12,10},{14,8},{1,7},{3,5},... | collective-permute-start | bytes 688136 | tf_op jit(solution)/shard_map/ppermute | solution.py:41
  264.8 47.4 %collective-permute-start.25 = (bf16[32,3584]{1,0:T(8,128)(2,1)}, bf16[32,3584]{1,0:T(8,128)(2,1)S(1)}, u32[]{:S(2)}, u32[]{:S(2)}) collective-permute-start(bf16[32,3584]{1,0:T(8,128)(2,1)} %copy-done.23), channel_id=1, source_target_pairs={{0,10},{2,8},{4,14},{6,12},{8,2},{10,0},{12,6},{14,4},{1,11},{3,9}... | collective-permute-start | bytes 688136 | tf_op jit(solution)/shard_map/ppermute | solution.py:41
  265.5 46.7 %collective-permute-start.26 = (bf16[32,3584]{1,0:T(8,128)(2,1)}, bf16[32,3584]{1,0:T(8,128)(2,1)S(1)}, u32[]{:S(2)}, u32[]{:S(2)}) collective-permute-start(bf16[32,3584]{1,0:T(8,128)(2,1)} %copy-done.22), channel_id=1, source_target_pairs={{0,12},{2,14},{4,8},{6,10},{8,4},{10,6},{12,0},{14,2},{1,13},{3,15... | collective-permute-start | bytes 688136 | tf_op jit(solution)/shard_map/ppermute | solution.py:41
  277.0 36.0 %collective-permute-start.27 = (bf16[32,3584]{1,0:T(8,128)(2,1)}, bf16[32,3584]{1,0:T(8,128)(2,1)S(1)}, u32[]{:S(2)}, u32[]{:S(2)}) collective-permute-start(bf16[32,3584]{1,0:T(8,128)(2,1)} %copy-done.21), channel_id=1, source_target_pairs={{0,14},{2,12},{4,10},{6,8},{8,6},{10,4},{12,2},{14,0},{1,15},{3,13... | collective-permute-start | bytes 688136 | tf_op jit(solution)/shard_map/ppermute | solution.py:41
  357.5 128.8 %reduce-scatter.8.cloned.1.call-start = ((), (), s32[]{:S(2)}) async-start(), calls=%async_computation.7 | async-start | bytes 1179648 | tf_op jit(solution)/shard_map/reduce_scatter | solution.py:360
  (35 other events, 452.2 us)
Sparse Core Ops, SparseCore 0:
  9.5 51.9 all-gather.2
  63.6 60.3 all-gather.4
  257.9 88.8 reduce-scatter.3
  357.6 62.4 reduce-scatter.5
  423.8 62.4 reduce-scatter.7

commit v5 on v4

--- a/solution.py
+++ b/solution.py
@@ -45,11 +45,23 @@
     return lax.optimization_barrier((value, earlier))[0]
 
 
+def gather_tree(own, devices):
+    pieces = {0: own}
+    for k in sorted(range(1, devices), key=lambda k: (bin(k).count("1"), -k)):
+        low = k & -k
+        pieces[k] = exchange(pieces[k ^ low], low)
+    return [(pieces[k], 0) for k in range(devices)]
+
+
+def far_first(devices):
+    return sorted(range(devices), key=lambda k: (-(k & (devices // 2)), -(k & (devices // 4)), k & 1 == 0))
+
+
 def swap_direct(arrays):
-    out = list(arrays)
-    for k in range(1, len(arrays)):
-        out[k] = exchange(arrays[k], k)
-    return [(array, 0) for array in out]
+    out = {}
+    for k, array in zip(far_first(len(arrays)), arrays):
+        out[k] = (exchange(array, k) if k else array, 0)
+    return [out[k] for k in range(len(arrays))]
 
 
 def all_after(pieces, *earlier):
@@ -60,7 +72,7 @@
 
 def distinct(pieces):
     arrays = []
-    for array, _ in pieces:
+    for array, _ in [pieces[k] for k in far_first(len(pieces))]:
         if not any(other is array for other in arrays):
             arrays.append(array)
     index = {id(array): at for at, array in enumerate(arrays)}
@@ -103,18 +115,18 @@
     )(tokens, gain.reshape(1, width))
 
 
-def gate_up_kernel(devices, rows, depth, qblock, me_ref, rows_ref, *refs):
-    code_refs = refs[: 2 * SPLIT]
-    gate_scale_ref, up_scale_ref = refs[2 * SPLIT : 2 * SPLIT + 2]
-    out_refs = refs[2 * SPLIT + 2 : -1]
+def gate_up_kernel(places, devices, rows, depth, qblock, ins, *refs):
+    piece_refs = refs[:ins]
+    code_refs = refs[ins : ins + 2 * SPLIT]
+    gate_scale_ref, up_scale_ref = refs[ins + 2 * SPLIT : ins + 2 * SPLIT + 2]
+    out_refs = refs[ins + 2 * SPLIT + 2 : -1]
     held = refs[-1]
     span = code_refs[0].shape[0]
 
     @pl.when(pl.program_id(0) == 0)
     def _():
-        for k in range(devices):
-            start = pl.multiple_of((me_ref[0] ^ k) * rows, rows)
-            held[k * rows : (k + 1) * rows, :] = rows_ref[pl.ds(start, rows), :]
+        for k, (at, start) in enumerate(places):
+            held[k * rows : (k + 1) * rows, :] = piece_refs[at][start : start + rows, :]
 
     def weight(refs_of_codes, scales, at):
         parts = []
@@ -134,12 +146,13 @@
         term = jnp.dot(left, right, preferred_element_type=jnp.float32)
         up = term if up is None else up + term
     hidden = (gate / (1.0 + jnp.exp(-gate)) * up).astype(jnp.bfloat16)
-    for k, out_ref in enumerate(out_refs):
+    for k, out_ref in zip(far_first(devices), out_refs):
         out_ref[...] = hidden[k * rows : (k + 1) * rows]
 
 
-def gate_up(me, gathered, devices, gate_codes, gate_scales, up_codes, up_scales):
-    rows = gathered.shape[0] // devices
+def gate_up(pieces, rows, gate_codes, gate_scales, up_codes, up_scales):
+    devices = len(pieces)
+    arrays, places = distinct(pieces)
     width, local = gate_codes.shape
     blocks = gate_scales.shape[0]
     tile = 256
@@ -147,14 +160,10 @@
     scales = pl.BlockSpec((blocks, tile), lambda i: (0, i))
     return pl.pallas_call(
         functools.partial(
-            gate_up_kernel, devices, rows, 512, width // blocks
+            gate_up_kernel, places, devices, rows, 512, width // blocks, len(arrays)
         ),
         grid=(local // tile,),
-        in_specs=[pl.BlockSpec(memory_space=pltpu.SMEM)]
-        + whole_blocks([gathered])
-        + codes
-        + codes
-        + [scales, scales],
+        in_specs=whole_blocks(arrays) + codes + codes + [scales, scales],
         out_specs=[pl.BlockSpec((rows, tile), lambda i: (0, i))] * devices,
         out_shape=[jax.ShapeDtypeStruct((rows, local), jnp.bfloat16)] * devices,
         scratch_shapes=[pltpu.VMEM((devices * rows, width), jnp.bfloat16)],
@@ -167,14 +176,14 @@
             transcendentals=devices * rows * local,
         ),
         name="gate_up",
-    )(me, gathered, *[gate_codes] * SPLIT, *[up_codes] * SPLIT, gate_scales, up_scales)
+    )(*arrays, *[gate_codes] * SPLIT, *[up_codes] * SPLIT, gate_scales, up_scales)
 
 
 def rotate_kernel(places, rows, factor, ins, sign_ref, *refs):
     devices = len(places)
     piece_refs = refs[:ins]
     table_ref = refs[ins]
-    out_refs = refs[ins + 1 : -1]
+    out_refs = dict(zip(far_first(devices), refs[ins + 1 : -1]))
     held = refs[-1]
     local = piece_refs[0].shape[1]
     block = table_ref.shape[0]
@@ -234,18 +243,18 @@
     )(signs, *arrays, table)
 
 
-def down_kernel(places, rows, group, ins, me_ref, *refs):
+def down_kernel(places, rows, group, order, ins, *refs):
     devices = len(places)
     piece_refs = refs[:ins]
     code_refs = refs[ins : ins + SPLIT]
-    scale_ref, out_ref, held, weight = refs[ins + SPLIT :]
+    scale_ref, keep_ref, send_ref, held, weight = refs[ins + SPLIT :]
+    half = devices // 2
 
     @pl.when(pl.program_id(0) == 0)
     def _():
-        for k in range(devices):
+        for place, k in enumerate(order):
             at, start = places[k]
-            into = pl.multiple_of((me_ref[0] ^ k) * rows, rows)
-            held[pl.ds(into, rows), :] = piece_refs[at][start : start + rows, :]
+            held[place * rows : (place + 1) * rows, :] = piece_refs[at][start : start + rows, :]
 
     depth, tile = code_refs[0].shape
     repeat = math.lcm(group, 16)
@@ -272,25 +281,34 @@
             preferred_element_type=jnp.float32,
         )
         total = term if total is None else total + term
-    out_ref[...] = total.astype(jnp.bfloat16)
-
-
-def down(me, pieces, rows, first_column, columns, codes, scales):
+    keep_ref[...] = total[: half * rows]
+    send_ref[...] = total[half * rows :].astype(jnp.bfloat16)
+
+
+def down(pieces, rows, strides, first_column, columns, codes, scales):
     devices = len(pieces)
     arrays, places = distinct(pieces)
     local = codes.shape[0]
     blocks = scales.shape[0]
     tile = 512
     skip = first_column // tile
+    levels = len(strides)
+    order = sorted(
+        range(devices),
+        key=lambda k: sum(1 << (levels - 1 - i) for i, stride in enumerate(strides) if k & stride),
+    )
+    out_rows = devices // 2 * rows
     return pl.pallas_call(
-        functools.partial(down_kernel, places, rows, local // blocks, len(arrays)),
+        functools.partial(down_kernel, places, rows, local // blocks, order, len(arrays)),
         grid=(columns // tile,),
-        in_specs=[pl.BlockSpec(memory_space=pltpu.SMEM)]
-        + whole_blocks(arrays)
+        in_specs=whole_blocks(arrays)
         + split_blocks(local, tile, skip)
         + [pl.BlockSpec((blocks, tile), lambda i: (0, i + skip))],
-        out_specs=pl.BlockSpec((devices * rows, tile), lambda i: (0, i)),
-        out_shape=jax.ShapeDtypeStruct((devices * rows, columns), jnp.bfloat16),
+        out_specs=[pl.BlockSpec((out_rows, tile), lambda i: (0, i))] * 2,
+        out_shape=[
+            jax.ShapeDtypeStruct((out_rows, columns), jnp.float32),
+            jax.ShapeDtypeStruct((out_rows, columns), jnp.bfloat16),
+        ],
         scratch_shapes=[
             pltpu.VMEM((devices * rows, local), jnp.bfloat16),
             pltpu.VMEM((local, tile), jnp.bfloat16),
@@ -304,7 +322,17 @@
             transcendentals=0,
         ),
         name="down",
-    )(me, *arrays, *[codes] * SPLIT, scales)
+    )(*arrays, *[codes] * SPLIT, scales)
+
+
+def add_share(shares, stride, *earlier):
+    keep, send = shares
+    return keep + after(exchange(send, stride), *earlier).astype(jnp.float32)
+
+
+def split_share(total):
+    half = total.shape[0] // 2
+    return total[:half], total[half:].astype(jnp.bfloat16)
 
 
 def block_order(local, group):
@@ -334,45 +362,47 @@
     )
     weights = (gate_codes, gate_scales, up_codes, up_scales)
 
-    me = lax.axis_index(AXIS).reshape(1)
     half = width // 2
     own = norm(tokens, norm_gain, [(0, 0, rows, width), (rows, 0, rows, width)])
-    first = lax.all_gather(own[0], AXIS, axis=0, tiled=True)
-    second = lax.all_gather(after(own[1], first), AXIS, axis=0, tiled=True)
-
-    arrays = gate_up(me, first, devices, *weights)
+    first, second = [gather_tree(piece, devices) for piece in own]
+
+    arrays = gate_up(first, rows, *weights)
     hidden = swap_direct(arrays)
-    later_arrays = gate_up(me, after(second, arrays[1]), devices, *weights)
+    later_arrays = gate_up(all_after(second, arrays[0]), rows, *weights)
     later_hidden = swap_direct(later_arrays)
 
-    hidden = all_after(hidden, later_arrays[1])
-    arrays = rotate(hidden, rows, signs, table)
+    arrays = rotate(all_after(hidden, later_arrays[0]), rows, signs, table)
     rotated = swap_direct(arrays)
-    later_hidden = all_after(later_hidden, arrays[1])
-    later_arrays = rotate(later_hidden, rows, signs, table)
+    later_arrays = rotate(all_after(later_hidden, arrays[0]), rows, signs, table)
     later_rotated = swap_direct(later_arrays)
-    rotated = all_after(rotated, later_arrays[1])
-
-    def contract(pieces, first_column, columns):
-        return down(me, pieces, rows, first_column, columns, down_codes, down_scales)
-
-    def scatter(shares):
-        return lax.psum_scatter(shares, AXIS, scatter_dimension=0, tiled=True)
-
-    shares = contract(rotated, 0, width)
-    above = scatter(shares)
-    left = contract(all_after(later_rotated, above), 0, half)
-    right = contract(all_after(later_rotated, left), half, half)
-    residual = tokens.astype(jnp.float32)
-
-    def add(start, columns, sums):
-        base = residual[start : start + rows, columns : columns + sums.shape[1]]
-        return (base + sums.astype(jnp.float32)).astype(jnp.bfloat16)
-
-    above = add(0, 0, above)
-    left = add(rows, 0, scatter(left))
-    right = add(rows, half, after(scatter(right), left))
-    return jnp.concatenate([above, jnp.concatenate([left, right], axis=1)], axis=0)
+
+    def contract(pieces, strides, first_column, columns):
+        return down(pieces, rows, strides, first_column, columns, down_codes, down_scales)
+
+    order, other = [1, 2, 4], [2, 1, 4]
+    rotated = all_after(rotated, later_arrays[0])
+    top_left = contract(rotated, order, 0, half)
+    top_right = contract(all_after(rotated, top_left[1]), other, half, half)
+    left = contract(all_after(later_rotated, top_right[1]), order, 0, half)
+    top_left = split_share(add_share(top_left, order[0], left[1]))
+    top_right = split_share(add_share(top_right, other[0], left[1]))
+    right = contract(
+        all_after(later_rotated, left[1], top_left[1], top_right[1]), other, half, half
+    )
+    top_left = split_share(add_share(top_left, order[1], right[1]))
+    top_right = split_share(add_share(top_right, other[1], right[1]))
+    left = split_share(add_share(left, order[0], top_left[1], top_right[1]))
+    right = split_share(add_share(right, other[0], left[1]))
+    top_left = add_share(top_left, order[2], right[1])
+    top_right = add_share(top_right, other[2], right[1])
+    left = split_share(add_share(left, order[1], top_left, top_right))
+    right = split_share(add_share(right, other[1], left[1]))
+    left = add_share(left, order[2])
+    right = add_share(right, other[2], left)
+    above = jnp.concatenate([top_left, top_right], axis=1)
+    below = jnp.concatenate([left, right], axis=1)
+    total = jnp.concatenate([above, below], axis=0)
+    return (tokens.astype(jnp.float32) + total).astype(jnp.bfloat16)
 
 
 def dequantize(codes, scales):

time: 495 us -> 320 us (0.65)
  waiting for transfers between devices: 314 us -> 109 us
  starting transfers between devices: 49.4 us -> 100 us
  between operations: 13.3 us -> 0.33 us
  local copies, waits for them, and re-layouts: 19 us -> 12.6 us
    reduce_scatter x3 -> x0, waiting for transfers between devices: 147 us -> none  [scatter(): return lax.psum_scatter(shares, AXIS, scatter_dimension=0, tiled=True)]
    all_gather x2 -> x0, waiting for transfers between devices: 76 us -> none  [the longest x1 52.1 us: shards_piped(): first = lax.all_gather(own[0], AXIS, axis=0, tiled=True)]
    ppermute x28 -> x54, starting transfers between devices: 49 us -> 100 us  [exchange(): lax.ppermute(value, AXIS, [(i, i ^ stride) for i in range(lax.axis_size(A...]
    ppermute x28 -> x54, waiting for transfers between devices: 90.2 us -> 109 us  [exchange(): lax.ppermute(value, AXIS, [(i, i ^ stride) for i in range(lax.axis_size(A...]
    unnamed x52 -> x34, local copies, waits for them, and re-layouts: 18.3 us -> 11.7 us
    pallas_call x3 -> x4, Pallas kernels: 32.4 us -> 32.1 us  [down(): pl.pallas_call(functools.partial(down_kernel, places, rows, local // bloc...]
  transfers between devices with their start and end apart: 33 -> 54, of which waited for: 15 -> 21; matrix products, arithmetic and copies ran while one was open for 0% -> 0% of each run, Pallas kernels for 15% -> 30%
where the time goes in v5:
time: 320 us; the launch traced here: 319 us
  waiting for transfers between devices  109 us (34%)
  starting transfers between devices  100 us (31%)
  Pallas kernels  95.5 us (30%)
  local copies, waits for them, and re-layouts  12.6 us (4%)
    ppermute x54, waiting for transfers between devices, exchange(): lax.ppermute(value, AXIS, [(i, i ^ stride) for i in range(lax.axis_size(A...  109 us
    ppermute x54, starting transfers between devices, exchange(): lax.ppermute(value, AXIS, [(i, i ^ stride) for i in range(lax.axis_size(A...  100 us
    pallas_call x2, Pallas kernels, gate_up(): pl.pallas_call(functools.partial(gate_up_kernel, places, devices, rows, 5...  55.8 us
    pallas_call x4, Pallas kernels, down(): pl.pallas_call(functools.partial(down_kernel, places, rows, local // bloc...  32.1 us
    unnamed x34, local copies, waits for them, and re-layouts  11.7 us
    pallas_call x2, Pallas kernels, rotate(): pl.pallas_call(functools.partial(rotate_kernel, places, rows, (devices *...  7.34 us
  transfers between devices with their start and end apart: 54, of which 21 were waited for; matrix products, arithmetic and copies ran while one was open for 0% of the time, Pallas kernels for 30%

profile of v5, /device:TPU:0, one launch (start us, length us, event | category | flops | bytes accessed | tf_op | source)
XLA Modules:
  0.0 319.1 jit_solution(1687831555241782917)
XLA Ops:
  2.0 4.1 %collective-permute-start = (bf16[32,4096]{1,0:T(8,128)(2,1)S(1)}, bf16[32,4096]{1,0:T(8,128)(2,1)S(1)}, u32[]{:S(2)}, u32[]{:S(2)}) collective-permute-start(bf16[32,4096]{1,0:T(8,128)(2,1)S(1)} %get-tuple-element.114.refs_7_), channel_id=1, source_target_pairs={{0,8},{2,10},{4,12},{6,14},{8,0},{10,2},{12,4},{14,6},{1,9},{3,11}... | collective-permute-start | bytes 786440 | tf_op jit(solution)/shard_map/ppermute | solution.py:41
  9.5 10.3 %collective-permute-done.refs_3_ = bf16[32,4096]{1,0:T(8,128)(2,1)S(1)} collective-permute-done((bf16[32,4096]{1,0:T(8,128)(2,1)S(1)}, bf16[32,4096]{1,0:T(8,128)(2,1)S(1)}, u32[]{:S(2)}, u32[]{:S(2)}) %collective-permute-start) | collective-permute-done | bytes 262176 | tf_op jit(solution)/shard_map/ppermute | solution.py:41
  21.8 5.5 %collective-permute-start.5 = (bf16[32,4096]{1,0:T(8,128)(2,1)S(1)}, bf16[32,4096]{1,0:T(8,128)(2,1)S(1)}, u32[]{:S(2)}, u32[]{:S(2)}) collective-permute-start(bf16[32,4096]{1,0:T(8,128)(2,1)S(1)} %collective-permute-done.4.refs_5_), channel_id=1, source_target_pairs={{0,2},{2,0},{4,6},{6,4},{8,10},{10,8},{12,14},{14,12},{1,3},{3,1},... | collective-permute-start | bytes 786440 | tf_op jit(solution)/shard_map/ppermute | solution.py:41
  30.1 3.4 %collective-permute-done.1.refs_1_ = bf16[32,4096]{1,0:T(8,128)(2,1)S(1)} collective-permute-done((bf16[32,4096]{1,0:T(8,128)(2,1)S(1)}, bf16[32,4096]{1,0:T(8,128)(2,1)S(1)}, u32[]{:S(2)}, u32[]{:S(2)}) %collective-permute-start.1) | collective-permute-done | bytes 262176 | tf_op jit(solution)/shard_map/ppermute | solution.py:41
  45.9 27.9 %gate_up.2 = (bf16[32,3584]{1,0:T(8,128)(2,1)}, bf16[32,3584]{1,0:T(8,128)(2,1)S(1)}, bf16[32,3584]{1,0:T(8,128)(2,1)S(1)}, bf16[32,3584]{1,0:T(8,128)(2,1)S(1)}...) custom-call(bf16[32,4096]{1,0:T(8,128)(2,1)S(1)} %collective-permute, ...), custom_call_target="tpu_custom_call" | custom-call | flops 15032385536 | bytes 58720256 | tf_op jit(solution)/shard_map/gate_up/pallas_call | solution.py:161
  73.9 5.2 %collective-permute-start.8 = (bf16[32,3584]{1,0:T(8,128)(2,1)S(1)}, bf16[32,3584]{1,0:T(8,128)(2,1)S(1)}, u32[]{:S(2)}, u32[]{:S(2)}) collective-permute-start(bf16[32,3584]{1,0:T(8,128)(2,1)S(1)} %get-tuple-element.116), channel_id=1, source_target_pairs={{0,12},{2,14},{4,8},{6,10},{8,4},{10,6},{12,0},{14,2},{1,13},{3,15... | collective-permute-start | bytes 688136 | tf_op jit(solution)/shard_map/ppermute | solution.py:41
  85.6 15.4 %collective-permute-start.12 = (bf16[32,3584]{1,0:T(8,128)(2,1)}, bf16[32,3584]{1,0:T(8,128)(2,1)}, u32[]{:S(2)}, u32[]{:S(2)}) collective-permute-start(bf16[32,3584]{1,0:T(8,128)(2,1)} %get-tuple-element.120), channel_id=1, source_target_pairs={{0,4},{2,6},{4,0},{6,2},{8,12},{10,14},{12,8},{14,10},{1,5},{3,7},... | collective-permute-start | bytes 688136 | tf_op jit(solution)/shard_map/ppermute | solution.py:41
  101.0 7.2 %collective-permute-done.9.refs_2_ = bf16[32,3584]{1,0:T(8,128)(2,1)S(1)} collective-permute-done((bf16[32,3584]{1,0:T(8,128)(2,1)S(1)}, bf16[32,3584]{1,0:T(8,128)(2,1)S(1)}, u32[]{:S(2)}, u32[]{:S(2)}) %collective-permute-start.9) | collective-permute-done | bytes 229408 | tf_op jit(solution)/shard_map/ppermute | solution.py:41
  109.8 27.9 %gate_up.3 = (bf16[32,3584]{1,0:T(8,128)(2,1)S(1)}, bf16[32,3584]{1,0:T(8,128)(2,1)}, bf16[32,3584]{1,0:T(8,128)(2,1)S(1)}, bf16[32,3584]{1,0:T(8,128)(2,1)S(1)}...) custom-call(bf16[32,4096]{1,0:T(8,128)(2,1)S(1)} %collective-permute, ...), custom_call_target="tpu_custom_call" | custom-call | flops 15032385536 | bytes 58720256 | tf_op jit(solution)/shard_map/gate_up/pallas_call | solution.py:161
  155.4 4.0 %rotate.2 = (bf16[32,3584]{1,0:T(8,128)(2,1)S(1)}, bf16[32,3584]{1,0:T(8,128)(2,1)S(1)}, bf16[32,3584]{1,0:T(8,128)(2,1)S(1)}, bf16[32,3584]{1,0:T(8,128)(2,1)S(...) custom-call(f32[2,8]{1,0:T(2,128)S(1)} %dynamic-slice_bitcast_fusion, ...), custom_call_target="tpu_custom_call" | custom-call | flops 1644167168 | bytes 3670016 | tf_op jit(solution)/shard_map/rotate/pallas_call | solution.py:228
  159.4 7.8 %collective-permute-done.30.refs_2_ = bf16[32,3584]{1,0:T(8,128)(2,1)S(1)} collective-permute-done((bf16[32,3584]{1,0:T(8,128)(2,1)}, bf16[32,3584]{1,0:T(8,128)(2,1)S(1)}, u32[]{:S(2)}, u32[]{:S(2)}) %collective-permute-start.30) | collective-permute-done | bytes 229408 | tf_op jit(solution)/shard_map/ppermute | solution.py:41
  169.5 13.4 %collective-permute-done.31.refs_3_ = bf16[32,3584]{1,0:T(8,128)(2,1)S(1)} collective-permute-done((bf16[32,3584]{1,0:T(8,128)(2,1)}, bf16[32,3584]{1,0:T(8,128)(2,1)S(1)}, u32[]{:S(2)}, u32[]{:S(2)}) %collective-permute-start.31) | collective-permute-done | bytes 229408 | tf_op jit(solution)/shard_map/ppermute | solution.py:41
  183.4 3.5 %collective-permute-start.24 = (bf16[32,3584]{1,0:T(8,128)(2,1)S(1)}, bf16[32,3584]{1,0:T(8,128)(2,1)S(1)}, u32[]{:S(2)}, u32[]{:S(2)}) collective-permute-start(bf16[32,3584]{1,0:T(8,128)(2,1)S(1)} %get-tuple-element.144), channel_id=1, source_target_pairs={{0,8},{2,10},{4,12},{6,14},{8,0},{10,2},{12,4},{14,6},{1,9},{3,11}... | collective-permute-start | bytes 688136 | tf_op jit(solution)/shard_map/ppermute | solution.py:41
  191.3 13.6 %collective-permute-done.23.refs_2_ = bf16[32,3584]{1,0:T(8,128)(2,1)S(1)} collective-permute-done((bf16[32,3584]{1,0:T(8,128)(2,1)S(1)}, bf16[32,3584]{1,0:T(8,128)(2,1)S(1)}, u32[]{:S(2)}, u32[]{:S(2)}) %collective-permute-start.23) | collective-permute-done | bytes 229408 | tf_op jit(solution)/shard_map/ppermute | solution.py:41
  211.1 11.1 %collective-permute-done.24.refs_3_ = bf16[32,3584]{1,0:T(8,128)(2,1)S(1)} collective-permute-done((bf16[32,3584]{1,0:T(8,128)(2,1)S(1)}, bf16[32,3584]{1,0:T(8,128)(2,1)S(1)}, u32[]{:S(2)}, u32[]{:S(2)}) %collective-permute-start.24) | collective-permute-done | bytes 229408 | tf_op jit(solution)/shard_map/ppermute | solution.py:41
  222.7 3.5 %collective-permute-start.39 = (bf16[32,3584]{1,0:T(8,128)(2,1)S(1)}, bf16[32,3584]{1,0:T(8,128)(2,1)S(1)}, u32[]{:S(2)}, u32[]{:S(2)}) collective-permute-start(bf16[32,3584]{1,0:T(8,128)(2,1)S(1)} %get-tuple-element.177), channel_id=1, source_target_pairs={{0,8},{2,10},{4,12},{6,14},{8,0},{10,2},{12,4},{14,6},{1,9},{3,11}... | collective-permute-start | bytes 688136 | tf_op jit(solution)/shard_map/ppermute | solution.py:41
  230.0 8.0 %down.4 = (f32[128,2048]{1,0:T(8,128)S(1)}, bf16[128,2048]{1,0:T(8,128)(2,1)S(1)}) custom-call(bf16[32,3584]{1,0:T(8,128)(2,1)S(1)} %collective-permute-done.21.refs_0_, bf16[32,3584]{1,0:T(8,128)(2,1)S(1)} %collective-permute-done.22.refs_1_, bf16[32,3584]{1,0:T(8,128)(2,1)S(1)} %collective-permute-done.23.refs_2_, ...), custom_call_target="tpu_custom_call" | custom-call | flops 3758096384 | bytes 14680064 | tf_op jit(solution)/shard_map/down/pallas_call | solution.py:301
  238.0 8.6 %collective-permute-start.41 = (bf16[32,3584]{1,0:T(8,128)(2,1)S(1)}, bf16[32,3584]{1,0:T(8,128)(2,1)S(1)}, u32[]{:S(2)}, u32[]{:S(2)}) collective-permute-start(bf16[32,3584]{1,0:T(8,128)(2,1)S(1)} %get-tuple-element.179), channel_id=1, source_target_pairs={{0,4},{2,6},{4,0},{6,2},{8,12},{10,14},{12,8},{14,10},{1,5},{3,7},... | collective-permute-start | bytes 688136 | tf_op jit(solution)/shard_map/ppermute | solution.py:41
  250.7 8.0 %down.5 = (f32[128,2048]{1,0:T(8,128)S(1)}, bf16[128,2048]{1,0:T(8,128)(2,1)S(1)}) custom-call(bf16[32,3584]{1,0:T(8,128)(2,1)S(1)} %collective-permute-done.21.refs_0_, bf16[32,3584]{1,0:T(8,128)(2,1)S(1)} %collective-permute-done.22.refs_1_, bf16[32,3584]{1,0:T(8,128)(2,1)S(1)} %collective-permute-done.23.refs_2_, ...), custom_call_target="tpu_custom_call" | custom-call | flops 3758096384 | bytes 14680064 | tf_op jit(solution)/shard_map/down/pallas_call | solution.py:301
  259.6 8.0 %down.6 = (f32[128,2048]{1,0:T(8,128)S(1)}, bf16[128,2048]{1,0:T(8,128)(2,1)S(1)}) custom-call(bf16[32,3584]{1,0:T(8,128)(2,1)S(1)} %collective-permute-done.36.refs_0_, bf16[32,3584]{1,0:T(8,128)(2,1)S(1)} %collective-permute-done.37.refs_1_, bf16[32,3584]{1,0:T(8,128)(2,1)S(1)} %collective-permute-done.38.refs_2_, ...), custom_call_target="tpu_custom_call" | custom-call | flops 3758096384 | bytes 14680064 | tf_op jit(solution)/shard_map/down/pallas_call | solution.py:301
  274.5 8.0 %down.7 = (f32[128,2048]{1,0:T(8,128)S(1)}, bf16[128,2048]{1,0:T(8,128)(2,1)S(1)}) custom-call(bf16[32,3584]{1,0:T(8,128)(2,1)S(1)} %collective-permute-done.36.refs_0_, bf16[32,3584]{1,0:T(8,128)(2,1)S(1)} %collective-permute-done.37.refs_1_, bf16[32,3584]{1,0:T(8,128)(2,1)S(1)} %collective-permute-done.38.refs_2_, ...), custom_call_target="tpu_custom_call" | custom-call | flops 3758096384 | bytes 14680064 | tf_op jit(solution)/shard_map/down/pallas_call | solution.py:301
  290.3 8.7 %collective-permute-done.46 = bf16[128,2048]{1,0:T(8,128)(2,1)S(1)} collective-permute-done((bf16[128,2048]{1,0:T(8,128)(2,1)S(1)}, bf16[128,2048]{1,0:T(8,128)(2,1)S(1)}, u32[]{:S(2)}, u32[]{:S(2)}) %collective-permute-start.46) | collective-permute-done | bytes 524320 | tf_op jit(solution)/shard_map/ppermute | solution.py:41
  304.5 7.0 %collective-permute-done.51 = bf16[32,2048]{1,0:T(8,128)(2,1)S(1)} collective-permute-done((bf16[32,2048]{1,0:T(8,128)(2,1)S(1)}, bf16[32,2048]{1,0:T(8,128)(2,1)S(1)}, u32[]{:S(2)}, u32[]{:S(2)}) %collective-permute-start.51) | collective-permute-done | bytes 131104 | tf_op jit(solution)/shard_map/ppermute | solution.py:41
  311.7 6.5 %collective-permute-done.53 = bf16[32,2048]{1,0:T(8,128)(2,1)S(1)} collective-permute-done((bf16[32,2048]{1,0:T(8,128)(2,1)S(1)}, bf16[32,2048]{1,0:T(8,128)(2,1)S(1)}, u32[]{:S(2)}, u32[]{:S(2)}) %collective-permute-start.53) | collective-permute-done | bytes 131104 | tf_op jit(solution)/shard_map/ppermute | solution.py:41
  (148 shorter events, 91.9 us)
Async XLA Ops:
  38.8 40.2 %collective-permute-start.20 = (bf16[32,4096]{1,0:T(8,128)(2,1)S(1)}, bf16[32,4096]{1,0:T(8,128)(2,1)S(1)}, u32[]{:S(2)}, u32[]{:S(2)}) collective-permute-start(bf16[32,4096]{1,0:T(8,128)(2,1)S(1)} %get-tuple-element.131.refs_7_), channel_id=1, source_target_pairs={{0,2},{2,0},{4,6},{6,4},{8,10},{10,8},{12,14},{14,12},{1,3},{3,1},... | collective-permute-start | bytes 786440 | tf_op jit(solution)/shard_map/ppermute | solution.py:41
  40.4 41.6 %collective-permute-start.17 = (bf16[32,4096]{1,0:T(8,128)(2,1)S(1)}, bf16[32,4096]{1,0:T(8,128)(2,1)S(1)}, u32[]{:S(2)}, u32[]{:S(2)}) collective-permute-start(bf16[32,4096]{1,0:T(8,128)(2,1)S(1)} %collective-permute-done.14.refs_3_), channel_id=1, source_target_pairs={{0,2},{2,0},{4,6},{6,4},{8,10},{10,8},{12,14},{14,12},{1,3},{3,1},... | collective-permute-start | bytes 786440 | tf_op jit(solution)/shard_map/ppermute | solution.py:41
  40.9 38.2 %collective-permute-start.19 = (bf16[32,4096]{1,0:T(8,128)(2,1)S(1)}, bf16[32,4096]{1,0:T(8,128)(2,1)S(1)}, u32[]{:S(2)}, u32[]{:S(2)}) collective-permute-start(bf16[32,4096]{1,0:T(8,128)(2,1)S(1)} %collective-permute-done.18.refs_5_), channel_id=1, source_target_pairs={{0,2},{2,0},{4,6},{6,4},{8,10},{10,8},{12,14},{14,12},{1,3},{3,1},... | collective-permute-start | bytes 786440 | tf_op jit(solution)/shard_map/ppermute | solution.py:41
  42.4 39.6 %collective-permute-start.16 = (bf16[32,4096]{1,0:T(8,128)(2,1)S(1)}, bf16[32,4096]{1,0:T(8,128)(2,1)S(1)}, u32[]{:S(2)}, u32[]{:S(2)}) collective-permute-start(bf16[32,4096]{1,0:T(8,128)(2,1)S(1)} %collective-permute-done.15.refs_1_), channel_id=1, source_target_pairs={{0,2},{2,0},{4,6},{6,4},{8,10},{10,8},{12,14},{14,12},{1,3},{3,1},... | collective-permute-start | bytes 786440 | tf_op jit(solution)/shard_map/ppermute | solution.py:41
  79.1 29.2 %collective-permute-start.9 = (bf16[32,3584]{1,0:T(8,128)(2,1)S(1)}, bf16[32,3584]{1,0:T(8,128)(2,1)S(1)}, u32[]{:S(2)}, u32[]{:S(2)}) collective-permute-start(bf16[32,3584]{1,0:T(8,128)(2,1)S(1)} %get-tuple-element.117), channel_id=1, source_target_pairs={{0,10},{2,8},{4,14},{6,12},{8,2},{10,0},{12,6},{14,4},{1,11},{3,9}... | collective-permute-start | bytes 688136 | tf_op jit(solution)/shard_map/ppermute | solution.py:41
  79.1 62.0 %collective-permute-start.10 = (bf16[32,3584]{1,0:T(8,128)(2,1)S(1)}, bf16[32,3584]{1,0:T(8,128)(2,1)S(1)}, u32[]{:S(2)}, u32[]{:S(2)}) collective-permute-start(bf16[32,3584]{1,0:T(8,128)(2,1)S(1)} %get-tuple-element.118), channel_id=1, source_target_pairs={{0,8},{2,10},{4,12},{6,14},{8,0},{10,2},{12,4},{14,6},{1,9},{3,11}... | collective-permute-start | bytes 688136 | tf_op jit(solution)/shard_map/ppermute | solution.py:41
  82.0 62.8 %collective-permute-start.11 = (bf16[32,3584]{1,0:T(8,128)(2,1)}, bf16[32,3584]{1,0:T(8,128)(2,1)}, u32[]{:S(2)}, u32[]{:S(2)}) collective-permute-start(bf16[32,3584]{1,0:T(8,128)(2,1)} %get-tuple-element.119), channel_id=1, source_target_pairs={{0,6},{2,4},{4,2},{6,0},{8,14},{10,12},{12,10},{14,8},{1,7},{3,5},... | collective-permute-start | bytes 688136 | tf_op jit(solution)/shard_map/ppermute | solution.py:41
  82.0 66.2 %collective-permute-start.7 = (bf16[32,3584]{1,0:T(8,128)(2,1)}, bf16[32,3584]{1,0:T(8,128)(2,1)}, u32[]{:S(2)}, u32[]{:S(2)}) collective-permute-start(bf16[32,3584]{1,0:T(8,128)(2,1)} %get-tuple-element.115), channel_id=1, source_target_pairs={{0,14},{2,12},{4,10},{6,8},{8,6},{10,4},{12,2},{14,0},{1,15},{3,13... | collective-permute-start | bytes 688136 | tf_op jit(solution)/shard_map/ppermute | solution.py:41
  85.6 59.1 %collective-permute-start.12 = (bf16[32,3584]{1,0:T(8,128)(2,1)}, bf16[32,3584]{1,0:T(8,128)(2,1)}, u32[]{:S(2)}, u32[]{:S(2)}) collective-permute-start(bf16[32,3584]{1,0:T(8,128)(2,1)} %get-tuple-element.120), channel_id=1, source_target_pairs={{0,4},{2,6},{4,0},{6,2},{8,12},{10,14},{12,8},{14,10},{1,5},{3,7},... | collective-permute-start | bytes 688136 | tf_op jit(solution)/shard_map/ppermute | solution.py:41
  108.3 39.3 %collective-permute-start.13 = (bf16[32,3584]{1,0:T(8,128)(2,1)}, bf16[32,3584]{1,0:T(8,128)(2,1)}, u32[]{:S(2)}, u32[]{:S(2)}) collective-permute-start(bf16[32,3584]{1,0:T(8,128)(2,1)} %get-tuple-element.121), channel_id=1, source_target_pairs={{0,2},{2,0},{4,6},{6,4},{8,10},{10,8},{12,14},{14,12},{1,3},{3,1},... | collective-permute-start | bytes 688136 | tf_op jit(solution)/shard_map/ppermute | solution.py:41
  144.8 22.4 %collective-permute-start.30 = (bf16[32,3584]{1,0:T(8,128)(2,1)}, bf16[32,3584]{1,0:T(8,128)(2,1)S(1)}, u32[]{:S(2)}, u32[]{:S(2)}) collective-permute-start(bf16[32,3584]{1,0:T(8,128)(2,1)} %copy-done.14), channel_id=1, source_target_pairs={{0,10},{2,8},{4,14},{6,12},{8,2},{10,0},{12,6},{14,4},{1,11},{3,9}... | collective-permute-start | bytes 688136 | tf_op jit(solution)/shard_map/ppermute | solution.py:41
  144.8 38.1 %collective-permute-start.31 = (bf16[32,3584]{1,0:T(8,128)(2,1)}, bf16[32,3584]{1,0:T(8,128)(2,1)S(1)}, u32[]{:S(2)}, u32[]{:S(2)}) collective-permute-start(bf16[32,3584]{1,0:T(8,128)(2,1)} %copy-done.13), channel_id=1, source_target_pairs={{0,8},{2,10},{4,12},{6,14},{8,0},{10,2},{12,4},{14,6},{1,9},{3,11}... | collective-permute-start | bytes 688136 | tf_op jit(solution)/shard_map/ppermute | solution.py:41
  147.5 35.9 %collective-permute-start.32 = (bf16[32,3584]{1,0:T(8,128)(2,1)}, bf16[32,3584]{1,0:T(8,128)(2,1)S(1)}, u32[]{:S(2)}, u32[]{:S(2)}) collective-permute-start(bf16[32,3584]{1,0:T(8,128)(2,1)} %copy-done.12), channel_id=1, source_target_pairs={{0,6},{2,4},{4,2},{6,0},{8,14},{10,12},{12,10},{14,8},{1,7},{3,5},... | collective-permute-start | bytes 688136 | tf_op jit(solution)/shard_map/ppermute | solution.py:41
  148.2 35.2 %collective-permute-start.33 = (bf16[32,3584]{1,0:T(8,128)(2,1)}, bf16[32,3584]{1,0:T(8,128)(2,1)S(1)}, u32[]{:S(2)}, u32[]{:S(2)}) collective-permute-start(bf16[32,3584]{1,0:T(8,128)(2,1)} %copy-done.11), channel_id=1, source_target_pairs={{0,4},{2,6},{4,0},{6,2},{8,12},{10,14},{12,8},{14,10},{1,5},{3,7},... | collective-permute-start | bytes 688136 | tf_op jit(solution)/shard_map/ppermute | solution.py:41
  152.4 34.5 %collective-permute-start.34 = (bf16[32,3584]{1,0:T(8,128)(2,1)}, bf16[32,3584]{1,0:T(8,128)(2,1)S(1)}, u32[]{:S(2)}, u32[]{:S(2)}) collective-permute-start(bf16[32,3584]{1,0:T(8,128)(2,1)} %copy-done.8), channel_id=1, source_target_pairs={{0,2},{2,0},{4,6},{6,4},{8,10},{10,8},{12,14},{14,12},{1,3},{3,1},... | collective-permute-start | bytes 688136 | tf_op jit(solution)/shard_map/ppermute | solution.py:41
  183.4 38.8 %collective-permute-start.24 = (bf16[32,3584]{1,0:T(8,128)(2,1)S(1)}, bf16[32,3584]{1,0:T(8,128)(2,1)S(1)}, u32[]{:S(2)}, u32[]{:S(2)}) collective-permute-start(bf16[32,3584]{1,0:T(8,128)(2,1)S(1)} %get-tuple-element.144), channel_id=1, source_target_pairs={{0,8},{2,10},{4,12},{6,14},{8,0},{10,2},{12,4},{14,6},{1,9},{3,11}... | collective-permute-start | bytes 688136 | tf_op jit(solution)/shard_map/ppermute | solution.py:41
  186.9 35.8 %collective-permute-start.25 = (bf16[32,3584]{1,0:T(8,128)(2,1)S(1)}, bf16[32,3584]{1,0:T(8,128)(2,1)S(1)}, u32[]{:S(2)}, u32[]{:S(2)}) collective-permute-start(bf16[32,3584]{1,0:T(8,128)(2,1)S(1)} %get-tuple-element.145), channel_id=1, source_target_pairs={{0,6},{2,4},{4,2},{6,0},{8,14},{10,12},{12,10},{14,8},{1,7},{3,5},... | collective-permute-start | bytes 688136 | tf_op jit(solution)/shard_map/ppermute | solution.py:41
  188.3 34.5 %collective-permute-start.26 = (bf16[32,3584]{1,0:T(8,128)(2,1)S(1)}, bf16[32,3584]{1,0:T(8,128)(2,1)S(1)}, u32[]{:S(2)}, u32[]{:S(2)}) collective-permute-start(bf16[32,3584]{1,0:T(8,128)(2,1)S(1)} %get-tuple-element.146), channel_id=1, source_target_pairs={{0,4},{2,6},{4,0},{6,2},{8,12},{10,14},{12,8},{14,10},{1,5},{3,7},... | collective-permute-start | bytes 688136 | tf_op jit(solution)/shard_map/ppermute | solution.py:41
  190.8 35.4 %collective-permute-start.27 = (bf16[32,3584]{1,0:T(8,128)(2,1)S(1)}, bf16[32,3584]{1,0:T(8,128)(2,1)S(1)}, u32[]{:S(2)}, u32[]{:S(2)}) collective-permute-start(bf16[32,3584]{1,0:T(8,128)(2,1)S(1)} %get-tuple-element.147), channel_id=1, source_target_pairs={{0,2},{2,0},{4,6},{6,4},{8,10},{10,8},{12,14},{14,12},{1,3},{3,1},... | collective-permute-start | bytes 688136 | tf_op jit(solution)/shard_map/ppermute | solution.py:41
  205.0 22.6 %collective-permute-start.21 = (bf16[32,3584]{1,0:T(8,128)(2,1)S(1)}, bf16[32,3584]{1,0:T(8,128)(2,1)S(1)}, u32[]{:S(2)}, u32[]{:S(2)}) collective-permute-start(bf16[32,3584]{1,0:T(8,128)(2,1)S(1)} %get-tuple-element.141), channel_id=1, source_target_pairs={{0,14},{2,12},{4,10},{6,8},{8,6},{10,4},{12,2},{14,0},{1,15},{3,13... | collective-permute-start | bytes 688136 | tf_op jit(solution)/shard_map/ppermute | solution.py:41
  222.7 26.6 %collective-permute-start.38 = (bf16[32,3584]{1,0:T(8,128)(2,1)S(1)}, bf16[32,3584]{1,0:T(8,128)(2,1)S(1)}, u32[]{:S(2)}, u32[]{:S(2)}) collective-permute-start(bf16[32,3584]{1,0:T(8,128)(2,1)S(1)} %get-tuple-element.176), channel_id=1, source_target_pairs={{0,10},{2,8},{4,14},{6,12},{8,2},{10,0},{12,6},{14,4},{1,11},{3,9}... | collective-permute-start | bytes 688136 | tf_op jit(solution)/shard_map/ppermute | solution.py:41
  222.7 36.0 %collective-permute-start.39 = (bf16[32,3584]{1,0:T(8,128)(2,1)S(1)}, bf16[32,3584]{1,0:T(8,128)(2,1)S(1)}, u32[]{:S(2)}, u32[]{:S(2)}) collective-permute-start(bf16[32,3584]{1,0:T(8,128)(2,1)S(1)} %get-tuple-element.177), channel_id=1, source_target_pairs={{0,8},{2,10},{4,12},{6,14},{8,0},{10,2},{12,4},{14,6},{1,9},{3,11}... | collective-permute-start | bytes 688136 | tf_op jit(solution)/shard_map/ppermute | solution.py:41
  226.2 32.6 %collective-permute-start.40 = (bf16[32,3584]{1,0:T(8,128)(2,1)S(1)}, bf16[32,3584]{1,0:T(8,128)(2,1)S(1)}, u32[]{:S(2)}, u32[]{:S(2)}) collective-permute-start(bf16[32,3584]{1,0:T(8,128)(2,1)S(1)} %get-tuple-element.178), channel_id=1, source_target_pairs={{0,6},{2,4},{4,2},{6,0},{8,14},{10,12},{12,10},{14,8},{1,7},{3,5},... | collective-permute-start | bytes 688136 | tf_op jit(solution)/shard_map/ppermute | solution.py:41
  227.6 32.0 %collective-permute-start.36 = (bf16[32,3584]{1,0:T(8,128)(2,1)S(1)}, bf16[32,3584]{1,0:T(8,128)(2,1)S(1)}, u32[]{:S(2)}, u32[]{:S(2)}) collective-permute-start(bf16[32,3584]{1,0:T(8,128)(2,1)S(1)} %get-tuple-element.164), channel_id=1, source_target_pairs={{0,14},{2,12},{4,10},{6,8},{8,6},{10,4},{12,2},{14,0},{1,15},{3,13... | collective-permute-start | bytes 688136 | tf_op jit(solution)/shard_map/ppermute | solution.py:41
  (47 other events, 792.0 us)

commit v6 on v5

--- a/solution.py
+++ b/solution.py
@@ -53,13 +53,14 @@
     return [(pieces[k], 0) for k in range(devices)]
 
 
-def far_first(devices):
-    return sorted(range(devices), key=lambda k: (-(k & (devices // 2)), -(k & (devices // 4)), k & 1 == 0))
+def departure(devices):
+    half = devices // 2
+    return [1, 2] + list(range(devices - 1, half - 1, -1)) + list(range(3, half)) + [0]
 
 
 def swap_direct(arrays):
     out = {}
-    for k, array in zip(far_first(len(arrays)), arrays):
+    for k, array in zip(departure(len(arrays)), arrays):
         out[k] = (exchange(array, k) if k else array, 0)
     return [out[k] for k in range(len(arrays))]
 
@@ -72,7 +73,7 @@
 
 def distinct(pieces):
     arrays = []
-    for array, _ in [pieces[k] for k in far_first(len(pieces))]:
+    for array, _ in [pieces[k] for k in departure(len(pieces))]:
         if not any(other is array for other in arrays):
             arrays.append(array)
     index = {id(array): at for at, array in enumerate(arrays)}
@@ -146,7 +147,7 @@
         term = jnp.dot(left, right, preferred_element_type=jnp.float32)
         up = term if up is None else up + term
     hidden = (gate / (1.0 + jnp.exp(-gate)) * up).astype(jnp.bfloat16)
-    for k, out_ref in zip(far_first(devices), out_refs):
+    for k, out_ref in zip(departure(devices), out_refs):
         out_ref[...] = hidden[k * rows : (k + 1) * rows]
 
 
@@ -183,7 +184,7 @@
     devices = len(places)
     piece_refs = refs[:ins]
     table_ref = refs[ins]
-    out_refs = dict(zip(far_first(devices), refs[ins + 1 : -1]))
+    out_refs = dict(zip(departure(devices), refs[ins + 1 : -1]))
     held = refs[-1]
     local = piece_refs[0].shape[1]
     block = table_ref.shape[0]
@@ -363,31 +364,32 @@
     weights = (gate_codes, gate_scales, up_codes, up_scales)
 
     half = width // 2
+    most = max(half, width // 512 * 5 // 8 * 512)
     own = norm(tokens, norm_gain, [(0, 0, rows, width), (rows, 0, rows, width)])
     first, second = [gather_tree(piece, devices) for piece in own]
 
     arrays = gate_up(first, rows, *weights)
     hidden = swap_direct(arrays)
-    later_arrays = gate_up(all_after(second, arrays[0]), rows, *weights)
+    later_arrays = gate_up(all_after(second, arrays[-1]), rows, *weights)
     later_hidden = swap_direct(later_arrays)
 
-    arrays = rotate(all_after(hidden, later_arrays[0]), rows, signs, table)
+    arrays = rotate(all_after(hidden, later_arrays[-1]), rows, signs, table)
     rotated = swap_direct(arrays)
-    later_arrays = rotate(all_after(later_hidden, arrays[0]), rows, signs, table)
+    later_arrays = rotate(all_after(later_hidden, arrays[-1]), rows, signs, table)
     later_rotated = swap_direct(later_arrays)
 
     def contract(pieces, strides, first_column, columns):
         return down(pieces, rows, strides, first_column, columns, down_codes, down_scales)
 
     order, other = [1, 2, 4], [2, 1, 4]
-    rotated = all_after(rotated, later_arrays[0])
+    rotated = all_after(rotated, later_arrays[-1])
     top_left = contract(rotated, order, 0, half)
     top_right = contract(all_after(rotated, top_left[1]), other, half, half)
-    left = contract(all_after(later_rotated, top_right[1]), order, 0, half)
+    left = contract(all_after(later_rotated, top_right[1]), order, 0, most)
     top_left = split_share(add_share(top_left, order[0], left[1]))
     top_right = split_share(add_share(top_right, other[0], left[1]))
     right = contract(
-        all_after(later_rotated, left[1], top_left[1], top_right[1]), other, half, half
+        all_after(later_rotated, left[1], top_left[1], top_right[1]), other, most, width - most
     )
     top_left = split_share(add_share(top_left, order[1], right[1]))
     top_right = split_share(add_share(top_right, other[1], right[1]))

time: 320 us -> 302 us (0.944)
  waiting for transfers between devices: 109 us -> 82.6 us
  starting transfers between devices: 100 us -> 113 us
  local copies, waits for them, and re-layouts: 12.6 us -> 8.15 us
    ppermute x54, waiting for transfers between devices: 109 us -> 82.6 us  [exchange(): lax.ppermute(value, AXIS, [(i, i ^ stride) for i in range(lax.axis_size(A...]
    ppermute x54, starting transfers between devices: 100 us -> 113 us  [exchange(): lax.ppermute(value, AXIS, [(i, i ^ stride) for i in range(lax.axis_size(A...]
    unnamed x34 -> x28, local copies, waits for them, and re-layouts: 11.7 us -> 7.29 us
  transfers between devices with their start and end apart: 54 -> 54, of which waited for: 21 -> 19; matrix products, arithmetic and copies ran while one was open for 0% -> 1% of each run, Pallas kernels for 30% -> 32%
where the time goes in v6:
time: 302 us; the launch traced here: 301 us
  starting transfers between devices  113 us (37%)
  Pallas kernels  95.2 us (32%)
  waiting for transfers between devices  82.6 us (27%)
  local copies, waits for them, and re-layouts  8.15 us (3%)
    ppermute x54, starting transfers between devices, exchange(): lax.ppermute(value, AXIS, [(i, i ^ stride) for i in range(lax.axis_size(A...  113 us
    ppermute x54, waiting for transfers between devices, exchange(): lax.ppermute(value, AXIS, [(i, i ^ stride) for i in range(lax.axis_size(A...  82.6 us
    pallas_call x2, Pallas kernels, gate_up(): pl.pallas_call(functools.partial(gate_up_kernel, places, devices, rows, 5...  55.2 us
    pallas_call x4, Pallas kernels, down(): pl.pallas_call(functools.partial(down_kernel, places, rows, local // bloc...  32.8 us
    unnamed x28, local copies, waits for them, and re-layouts  7.29 us
    pallas_call x2, Pallas kernels, rotate(): pl.pallas_call(functools.partial(rotate_kernel, places, rows, (devices *...  7 us
  transfers between devices with their start and end apart: 54, of which 19 were waited for; matrix products, arithmetic and copies ran while one was open for 1% of the time, Pallas kernels for 32%

profile of v6, /device:TPU:0, one launch (start us, length us, event | category | flops | bytes accessed | tf_op | source)
XLA Modules:
  0.0 300.8 jit_solution(2071793086856438071)
XLA Ops:
  2.0 4.1 %collective-permute-start.2 = (bf16[32,4096]{1,0:T(8,128)(2,1)S(1)}, bf16[32,4096]{1,0:T(8,128)(2,1)S(1)}, u32[]{:S(2)}, u32[]{:S(2)}) collective-permute-start(bf16[32,4096]{1,0:T(8,128)(2,1)S(1)} %get-tuple-element.114.refs_7_), channel_id=1, source_target_pairs={{0,8},{2,10},{4,12},{6,14},{8,0},{10,2},{12,4},{14,6},{1,9},{3,11}... | collective-permute-start | bytes 786440 | tf_op jit(solution)/shard_map/ppermute | solution.py:41
  9.5 10.3 %collective-permute-done.2.refs_5_ = bf16[32,4096]{1,0:T(8,128)(2,1)S(1)} collective-permute-done((bf16[32,4096]{1,0:T(8,128)(2,1)S(1)}, bf16[32,4096]{1,0:T(8,128)(2,1)S(1)}, u32[]{:S(2)}, u32[]{:S(2)}) %collective-permute-start.2) | collective-permute-done | bytes 262176 | tf_op jit(solution)/shard_map/ppermute | solution.py:41
  21.8 5.5 %collective-permute-start.5 = (bf16[32,4096]{1,0:T(8,128)(2,1)S(1)}, bf16[32,4096]{1,0:T(8,128)(2,1)S(1)}, u32[]{:S(2)}, u32[]{:S(2)}) collective-permute-start(bf16[32,4096]{1,0:T(8,128)(2,1)S(1)} %collective-permute-done.2.refs_5_), channel_id=1, source_target_pairs={{0,2},{2,0},{4,6},{6,4},{8,10},{10,8},{12,14},{14,12},{1,3},{3,1},... | collective-permute-start | bytes 786440 | tf_op jit(solution)/shard_map/ppermute | solution.py:41
  45.9 27.9 %gate_up.2 = (bf16[32,3584]{1,0:T(8,128)(2,1)}, bf16[32,3584]{1,0:T(8,128)(2,1)}, bf16[32,3584]{1,0:T(8,128)(2,1)S(1)}, bf16[32,3584]{1,0:T(8,128)(2,1)S(1)}, bf...) custom-call(bf16[32,4096]{1,0:T(8,128)(2,1)S(1)} %collective-permute, ...), custom_call_target="tpu_custom_call" | custom-call | flops 15032385536 | bytes 58720256 | tf_op jit(solution)/shard_map/gate_up/pallas_call | solution.py:162
  79.3 4.7 %collective-permute-start.9 = (bf16[32,3584]{1,0:T(8,128)(2,1)}, bf16[32,3584]{1,0:T(8,128)(2,1)S(1)}, u32[]{:S(2)}, u32[]{:S(2)}) collective-permute-start(bf16[32,3584]{1,0:T(8,128)(2,1)} %copy-done.12), channel_id=1, source_target_pairs={{0,14},{2,12},{4,10},{6,8},{8,6},{10,4},{12,2},{14,0},{1,15},{3,13... | collective-permute-start | bytes 688136 | tf_op jit(solution)/shard_map/ppermute | solution.py:41
  87.7 4.8 %collective-permute-start.13 = (bf16[32,3584]{1,0:T(8,128)(2,1)}, bf16[32,3584]{1,0:T(8,128)(2,1)S(1)}, u32[]{:S(2)}, u32[]{:S(2)}) collective-permute-start(bf16[32,3584]{1,0:T(8,128)(2,1)} %copy-done.8), channel_id=1, source_target_pairs={{0,6},{2,4},{4,2},{6,0},{8,14},{10,12},{12,10},{14,8},{1,7},{3,5},... | collective-permute-start | bytes 688136 | tf_op jit(solution)/shard_map/ppermute | solution.py:41
  92.5 27.3 %gate_up.3 = (bf16[32,3584]{1,0:T(8,128)(2,1)S(1)}, bf16[32,3584]{1,0:T(8,128)(2,1)S(1)}, bf16[32,3584]{1,0:T(8,128)(2,1)S(1)}, bf16[32,3584]{1,0:T(8,128)(2,1)S...) custom-call(bf16[32,4096]{1,0:T(8,128)(2,1)S(1)} %collective-permute, ...), custom_call_target="tpu_custom_call" | custom-call | flops 15032385536 | bytes 58720256 | tf_op jit(solution)/shard_map/gate_up/pallas_call | solution.py:162
  122.3 10.4 %collective-permute-start.30 = (bf16[32,3584]{1,0:T(8,128)(2,1)S(1)}, bf16[32,3584]{1,0:T(8,128)(2,1)S(1)}, u32[]{:S(2)}, u32[]{:S(2)}) collective-permute-start(bf16[32,3584]{1,0:T(8,128)(2,1)S(1)} %get-tuple-element.151), channel_id=1, source_target_pairs={{0,14},{2,12},{4,10},{6,8},{8,6},{10,4},{12,2},{14,0},{1,15},{3,13... | collective-permute-start | bytes 688136 | tf_op jit(solution)/shard_map/ppermute | solution.py:41
  134.1 3.7 %rotate.2 = (bf16[32,3584]{1,0:T(8,128)(2,1)S(1)}, bf16[32,3584]{1,0:T(8,128)(2,1)S(1)}, bf16[32,3584]{1,0:T(8,128)(2,1)S(1)}, bf16[32,3584]{1,0:T(8,128)(2,1)S(...) custom-call(f32[2,8]{1,0:T(2,128)S(1)} %dynamic-slice_bitcast_fusion, ...), custom_call_target="tpu_custom_call" | custom-call | flops 1644167168 | bytes 3670016 | tf_op jit(solution)/shard_map/rotate/pallas_call | solution.py:229
  144.2 3.4 %collective-permute-done.31.refs_3_ = bf16[32,3584]{1,0:T(8,128)(2,1)S(1)} collective-permute-done((bf16[32,3584]{1,0:T(8,128)(2,1)S(1)}, bf16[32,3584]{1,0:T(8,128)(2,1)S(1)}, u32[]{:S(2)}, u32[]{:S(2)}) %collective-permute-start.31) | collective-permute-done | bytes 229408 | tf_op jit(solution)/shard_map/ppermute | solution.py:41
  147.7 11.1 %collective-permute-start.22 = (bf16[32,3584]{1,0:T(8,128)(2,1)S(1)}, bf16[32,3584]{1,0:T(8,128)(2,1)S(1)}, u32[]{:S(2)}, u32[]{:S(2)}) collective-permute-start(bf16[32,3584]{1,0:T(8,128)(2,1)S(1)} %get-tuple-element.142), channel_id=1, source_target_pairs={{0,4},{2,6},{4,0},{6,2},{8,12},{10,14},{12,8},{14,10},{1,5},{3,7},... | collective-permute-start | bytes 688136 | tf_op jit(solution)/shard_map/ppermute | solution.py:41
  158.8 5.9 %collective-permute-done.32.refs_4_ = bf16[32,3584]{1,0:T(8,128)(2,1)S(1)} collective-permute-done((bf16[32,3584]{1,0:T(8,128)(2,1)S(1)}, bf16[32,3584]{1,0:T(8,128)(2,1)S(1)}, u32[]{:S(2)}, u32[]{:S(2)}) %collective-permute-start.32) | collective-permute-done | bytes 229408 | tf_op jit(solution)/shard_map/ppermute | solution.py:41
  167.2 12.7 %collective-permute-done.33.refs_5_ = bf16[32,3584]{1,0:T(8,128)(2,1)S(1)} collective-permute-done((bf16[32,3584]{1,0:T(8,128)(2,1)S(1)}, bf16[32,3584]{1,0:T(8,128)(2,1)S(1)}, u32[]{:S(2)}, u32[]{:S(2)}) %collective-permute-start.33) | collective-permute-done | bytes 229408 | tf_op jit(solution)/shard_map/ppermute | solution.py:41
  179.9 3.6 %collective-permute-start.24 = (bf16[32,3584]{1,0:T(8,128)(2,1)S(1)}, bf16[32,3584]{1,0:T(8,128)(2,1)S(1)}, u32[]{:S(2)}, u32[]{:S(2)}) collective-permute-start(bf16[32,3584]{1,0:T(8,128)(2,1)S(1)} %get-tuple-element.144), channel_id=1, source_target_pairs={{0,12},{2,14},{4,8},{6,10},{8,4},{10,6},{12,0},{14,2},{1,13},{3,15... | collective-permute-start | bytes 688136 | tf_op jit(solution)/shard_map/ppermute | solution.py:41
  191.2 6.6 %collective-permute-start.37 = (bf16[32,3584]{1,0:T(8,128)(2,1)S(1)}, bf16[32,3584]{1,0:T(8,128)(2,1)S(1)}, u32[]{:S(2)}, u32[]{:S(2)}) collective-permute-start(bf16[32,3584]{1,0:T(8,128)(2,1)S(1)} %get-tuple-element.176), channel_id=1, source_target_pairs={{0,4},{2,6},{4,0},{6,2},{8,12},{10,14},{12,8},{14,10},{1,5},{3,7},... | collective-permute-start | bytes 688136 | tf_op jit(solution)/shard_map/ppermute | solution.py:41
  197.9 6.3 %collective-permute-done.25.refs_4_ = bf16[32,3584]{1,0:T(8,128)(2,1)S(1)} collective-permute-done((bf16[32,3584]{1,0:T(8,128)(2,1)S(1)}, bf16[32,3584]{1,0:T(8,128)(2,1)S(1)}, u32[]{:S(2)}, u32[]{:S(2)}) %collective-permute-start.25) | collective-permute-done | bytes 229408 | tf_op jit(solution)/shard_map/ppermute | solution.py:41
  206.6 9.6 %collective-permute-done.26.refs_5_ = bf16[32,3584]{1,0:T(8,128)(2,1)S(1)} collective-permute-done((bf16[32,3584]{1,0:T(8,128)(2,1)S(1)}, bf16[32,3584]{1,0:T(8,128)(2,1)S(1)}, u32[]{:S(2)}, u32[]{:S(2)}) %collective-permute-start.26) | collective-permute-done | bytes 229408 | tf_op jit(solution)/shard_map/ppermute | solution.py:41
  216.2 4.2 %collective-permute-start.39 = (bf16[32,3584]{1,0:T(8,128)(2,1)S(1)}, bf16[32,3584]{1,0:T(8,128)(2,1)S(1)}, u32[]{:S(2)}, u32[]{:S(2)}) collective-permute-start(bf16[32,3584]{1,0:T(8,128)(2,1)S(1)} %get-tuple-element.178), channel_id=1, source_target_pairs={{0,12},{2,14},{4,8},{6,10},{8,4},{10,6},{12,0},{14,2},{1,13},{3,15... | collective-permute-start | bytes 688136 | tf_op jit(solution)/shard_map/ppermute | solution.py:41
  220.4 8.0 %down.4 = (f32[128,2048]{1,0:T(8,128)S(1)}, bf16[128,2048]{1,0:T(8,128)(2,1)S(1)}) custom-call(bf16[32,3584]{1,0:T(8,128)(2,1)S(1)} %collective-permute-done.21.refs_0_, bf16[32,3584]{1,0:T(8,128)(2,1)S(1)} %collective-permute-done.22.refs_1_, bf16[32,3584]{1,0:T(8,128)(2,1)S(1)} %collective-permute-done.23.refs_2_, ...), custom_call_target="tpu_custom_call" | custom-call | flops 3758096384 | bytes 14680064 | tf_op jit(solution)/shard_map/down/pallas_call | solution.py:302
  231.8 8.2 %down.5 = (f32[128,2048]{1,0:T(8,128)S(1)}, bf16[128,2048]{1,0:T(8,128)(2,1)S(1)}) custom-call(bf16[32,3584]{1,0:T(8,128)(2,1)S(1)} %collective-permute-done.21.refs_0_, bf16[32,3584]{1,0:T(8,128)(2,1)S(1)} %collective-permute-done.22.refs_1_, bf16[32,3584]{1,0:T(8,128)(2,1)S(1)} %collective-permute-done.23.refs_2_, ...), custom_call_target="tpu_custom_call" | custom-call | flops 3758096384 | bytes 14680064 | tf_op jit(solution)/shard_map/down/pallas_call | solution.py:302
  246.8 9.9 %down.6 = (f32[128,2560]{1,0:T(8,128)S(1)}, bf16[128,2560]{1,0:T(8,128)(2,1)S(1)}) custom-call(bf16[32,3584]{1,0:T(8,128)(2,1)S(1)} %collective-permute-done.36.refs_0_, bf16[32,3584]{1,0:T(8,128)(2,1)S(1)} %collective-permute-done.37.refs_1_, bf16[32,3584]{1,0:T(8,128)(2,1)S(1)} %collective-permute-done.38.refs_2_, ...), custom_call_target="tpu_custom_call" | custom-call | flops 4697620480 | bytes 18350080 | tf_op jit(solution)/shard_map/down/pallas_call | solution.py:302
  259.2 6.6 %down.7 = (f32[128,1536]{1,0:T(8,128)S(1)}, bf16[128,1536]{1,0:T(8,128)(2,1)S(1)}) custom-call(bf16[32,3584]{1,0:T(8,128)(2,1)S(1)} %collective-permute-done.36.refs_0_, bf16[32,3584]{1,0:T(8,128)(2,1)S(1)} %collective-permute-done.37.refs_1_, bf16[32,3584]{1,0:T(8,128)(2,1)S(1)} %collective-permute-done.38.refs_2_, ...), custom_call_target="tpu_custom_call" | custom-call | flops 2818572288 | bytes 11010048 | tf_op jit(solution)/shard_map/down/pallas_call | solution.py:302
  267.9 5.6 %collective-permute-done.48 = bf16[64,2048]{1,0:T(8,128)(2,1)S(1)} collective-permute-done((bf16[64,2048]{1,0:T(8,128)(2,1)S(1)}, bf16[64,2048]{1,0:T(8,128)(2,1)S(1)}, u32[]{:S(2)}, u32[]{:S(2)}) %collective-permute-start.48) | collective-permute-done | bytes 262176 | tf_op jit(solution)/shard_map/ppermute | solution.py:41
  290.0 8.8 %collective-permute-done.51 = bf16[32,2560]{1,0:T(8,128)(2,1)S(1)} collective-permute-done((bf16[32,2560]{1,0:T(8,128)(2,1)S(1)}, bf16[32,2560]{1,0:T(8,128)(2,1)S(1)}, u32[]{:S(2)}, u32[]{:S(2)}) %collective-permute-start.51) | collective-permute-done | bytes 163872 | tf_op jit(solution)/shard_map/ppermute | solution.py:41
  (142 shorter events, 91.3 us)
Async XLA Ops:
  38.8 40.5 %collective-permute-start.14 = (bf16[32,4096]{1,0:T(8,128)(2,1)S(1)}, bf16[32,4096]{1,0:T(8,128)(2,1)S(1)}, u32[]{:S(2)}, u32[]{:S(2)}) collective-permute-start(bf16[32,4096]{1,0:T(8,128)(2,1)S(1)} %get-tuple-element.131.refs_7_), channel_id=1, source_target_pairs={{0,2},{2,0},{4,6},{6,4},{8,10},{10,8},{12,14},{14,12},{1,3},{3,1},... | collective-permute-start | bytes 786440 | tf_op jit(solution)/shard_map/ppermute | solution.py:41
  40.4 38.9 %collective-permute-start.19 = (bf16[32,4096]{1,0:T(8,128)(2,1)S(1)}, bf16[32,4096]{1,0:T(8,128)(2,1)S(1)}, u32[]{:S(2)}, u32[]{:S(2)}) collective-permute-start(bf16[32,4096]{1,0:T(8,128)(2,1)S(1)} %collective-permute-done.16.refs_5_), channel_id=1, source_target_pairs={{0,2},{2,0},{4,6},{6,4},{8,10},{10,8},{12,14},{14,12},{1,3},{3,1},... | collective-permute-start | bytes 786440 | tf_op jit(solution)/shard_map/ppermute | solution.py:41
  40.9 43.1 %collective-permute-start.20 = (bf16[32,4096]{1,0:T(8,128)(2,1)S(1)}, bf16[32,4096]{1,0:T(8,128)(2,1)S(1)}, u32[]{:S(2)}, u32[]{:S(2)}) collective-permute-start(bf16[32,4096]{1,0:T(8,128)(2,1)S(1)} %collective-permute-done.15.refs_1_), channel_id=1, source_target_pairs={{0,2},{2,0},{4,6},{6,4},{8,10},{10,8},{12,14},{14,12},{1,3},{3,1},... | collective-permute-start | bytes 786440 | tf_op jit(solution)/shard_map/ppermute | solution.py:41
  42.4 41.6 %collective-permute-start.18 = (bf16[32,4096]{1,0:T(8,128)(2,1)S(1)}, bf16[32,4096]{1,0:T(8,128)(2,1)S(1)}, u32[]{:S(2)}, u32[]{:S(2)}) collective-permute-start(bf16[32,4096]{1,0:T(8,128)(2,1)S(1)} %collective-permute-done.17.refs_3_), channel_id=1, source_target_pairs={{0,2},{2,0},{4,6},{6,4},{8,10},{10,8},{12,14},{14,12},{1,3},{3,1},... | collective-permute-start | bytes 786440 | tf_op jit(solution)/shard_map/ppermute | solution.py:41
  79.3 40.5 %collective-permute-start.9 = (bf16[32,3584]{1,0:T(8,128)(2,1)}, bf16[32,3584]{1,0:T(8,128)(2,1)S(1)}, u32[]{:S(2)}, u32[]{:S(2)}) collective-permute-start(bf16[32,3584]{1,0:T(8,128)(2,1)} %copy-done.12), channel_id=1, source_target_pairs={{0,14},{2,12},{4,10},{6,8},{8,6},{10,4},{12,2},{14,0},{1,15},{3,13... | collective-permute-start | bytes 688136 | tf_op jit(solution)/shard_map/ppermute | solution.py:41
  84.0 38.4 %collective-permute-start.10 = (bf16[32,3584]{1,0:T(8,128)(2,1)}, bf16[32,3584]{1,0:T(8,128)(2,1)S(1)}, u32[]{:S(2)}, u32[]{:S(2)}) collective-permute-start(bf16[32,3584]{1,0:T(8,128)(2,1)} %copy-done.11), channel_id=1, source_target_pairs={{0,12},{2,14},{4,8},{6,10},{8,4},{10,6},{12,0},{14,2},{1,13},{3,15... | collective-permute-start | bytes 688136 | tf_op jit(solution)/shard_map/ppermute | solution.py:41
  84.0 38.4 %collective-permute-start.11 = (bf16[32,3584]{1,0:T(8,128)(2,1)}, bf16[32,3584]{1,0:T(8,128)(2,1)S(1)}, u32[]{:S(2)}, u32[]{:S(2)}) collective-permute-start(bf16[32,3584]{1,0:T(8,128)(2,1)} %copy-done.10), channel_id=1, source_target_pairs={{0,10},{2,8},{4,14},{6,12},{8,2},{10,0},{12,6},{14,4},{1,11},{3,9}... | collective-permute-start | bytes 688136 | tf_op jit(solution)/shard_map/ppermute | solution.py:41
  86.5 46.2 %collective-permute-start.12 = (bf16[32,3584]{1,0:T(8,128)(2,1)}, bf16[32,3584]{1,0:T(8,128)(2,1)S(1)}, u32[]{:S(2)}, u32[]{:S(2)}) collective-permute-start(bf16[32,3584]{1,0:T(8,128)(2,1)} %copy-done.9), channel_id=1, source_target_pairs={{0,8},{2,10},{4,12},{6,14},{8,0},{10,2},{12,4},{14,6},{1,9},{3,11}... | collective-permute-start | bytes 688136 | tf_op jit(solution)/shard_map/ppermute | solution.py:41
  87.7 45.7 %collective-permute-start.13 = (bf16[32,3584]{1,0:T(8,128)(2,1)}, bf16[32,3584]{1,0:T(8,128)(2,1)S(1)}, u32[]{:S(2)}, u32[]{:S(2)}) collective-permute-start(bf16[32,3584]{1,0:T(8,128)(2,1)} %copy-done.8), channel_id=1, source_target_pairs={{0,6},{2,4},{4,2},{6,0},{8,14},{10,12},{12,10},{14,8},{1,7},{3,5},... | collective-permute-start | bytes 688136 | tf_op jit(solution)/shard_map/ppermute | solution.py:41
  122.3 21.8 %collective-permute-start.30 = (bf16[32,3584]{1,0:T(8,128)(2,1)S(1)}, bf16[32,3584]{1,0:T(8,128)(2,1)S(1)}, u32[]{:S(2)}, u32[]{:S(2)}) collective-permute-start(bf16[32,3584]{1,0:T(8,128)(2,1)S(1)} %get-tuple-element.151), channel_id=1, source_target_pairs={{0,14},{2,12},{4,10},{6,8},{8,6},{10,4},{12,2},{14,0},{1,15},{3,13... | collective-permute-start | bytes 688136 | tf_op jit(solution)/shard_map/ppermute | solution.py:41
  133.4 31.3 %collective-permute-start.32 = (bf16[32,3584]{1,0:T(8,128)(2,1)S(1)}, bf16[32,3584]{1,0:T(8,128)(2,1)S(1)}, u32[]{:S(2)}, u32[]{:S(2)}) collective-permute-start(bf16[32,3584]{1,0:T(8,128)(2,1)S(1)} %get-tuple-element.153), channel_id=1, source_target_pairs={{0,10},{2,8},{4,14},{6,12},{8,2},{10,0},{12,6},{14,4},{1,11},{3,9}... | collective-permute-start | bytes 688136 | tf_op jit(solution)/shard_map/ppermute | solution.py:41
  137.8 42.0 %collective-permute-start.33 = (bf16[32,3584]{1,0:T(8,128)(2,1)S(1)}, bf16[32,3584]{1,0:T(8,128)(2,1)S(1)}, u32[]{:S(2)}, u32[]{:S(2)}) collective-permute-start(bf16[32,3584]{1,0:T(8,128)(2,1)S(1)} %get-tuple-element.154), channel_id=1, source_target_pairs={{0,8},{2,10},{4,12},{6,14},{8,0},{10,2},{12,4},{14,6},{1,9},{3,11}... | collective-permute-start | bytes 688136 | tf_op jit(solution)/shard_map/ppermute | solution.py:41
  140.2 43.3 %collective-permute-start.34 = (bf16[32,3584]{1,0:T(8,128)(2,1)S(1)}, bf16[32,3584]{1,0:T(8,128)(2,1)S(1)}, u32[]{:S(2)}, u32[]{:S(2)}) collective-permute-start(bf16[32,3584]{1,0:T(8,128)(2,1)S(1)} %get-tuple-element.155), channel_id=1, source_target_pairs={{0,6},{2,4},{4,2},{6,0},{8,14},{10,12},{12,10},{14,8},{1,7},{3,5},... | collective-permute-start | bytes 688136 | tf_op jit(solution)/shard_map/ppermute | solution.py:41
  144.1 39.3 %collective-permute-start.21 = (bf16[32,3584]{1,0:T(8,128)(2,1)S(1)}, bf16[32,3584]{1,0:T(8,128)(2,1)S(1)}, u32[]{:S(2)}, u32[]{:S(2)}) collective-permute-start(bf16[32,3584]{1,0:T(8,128)(2,1)S(1)} %get-tuple-element.141), channel_id=1, source_target_pairs={{0,2},{2,0},{4,6},{6,4},{8,10},{10,8},{12,14},{14,12},{1,3},{3,1},... | collective-permute-start | bytes 688136 | tf_op jit(solution)/shard_map/ppermute | solution.py:41
  147.7 38.6 %collective-permute-start.22 = (bf16[32,3584]{1,0:T(8,128)(2,1)S(1)}, bf16[32,3584]{1,0:T(8,128)(2,1)S(1)}, u32[]{:S(2)}, u32[]{:S(2)}) collective-permute-start(bf16[32,3584]{1,0:T(8,128)(2,1)S(1)} %get-tuple-element.142), channel_id=1, source_target_pairs={{0,4},{2,6},{4,0},{6,2},{8,12},{10,14},{12,8},{14,10},{1,5},{3,7},... | collective-permute-start | bytes 688136 | tf_op jit(solution)/shard_map/ppermute | solution.py:41
  164.7 24.8 %collective-permute-start.23 = (bf16[32,3584]{1,0:T(8,128)(2,1)S(1)}, bf16[32,3584]{1,0:T(8,128)(2,1)S(1)}, u32[]{:S(2)}, u32[]{:S(2)}) collective-permute-start(bf16[32,3584]{1,0:T(8,128)(2,1)S(1)} %get-tuple-element.143), channel_id=1, source_target_pairs={{0,14},{2,12},{4,10},{6,8},{8,6},{10,4},{12,2},{14,0},{1,15},{3,13... | collective-permute-start | bytes 688136 | tf_op jit(solution)/shard_map/ppermute | solution.py:41
  183.4 20.7 %collective-permute-start.25 = (bf16[32,3584]{1,0:T(8,128)(2,1)S(1)}, bf16[32,3584]{1,0:T(8,128)(2,1)S(1)}, u32[]{:S(2)}, u32[]{:S(2)}) collective-permute-start(bf16[32,3584]{1,0:T(8,128)(2,1)S(1)} %get-tuple-element.145), channel_id=1, source_target_pairs={{0,10},{2,8},{4,14},{6,12},{8,2},{10,0},{12,6},{14,4},{1,11},{3,9}... | collective-permute-start | bytes 688136 | tf_op jit(solution)/shard_map/ppermute | solution.py:41
  183.4 32.7 %collective-permute-start.26 = (bf16[32,3584]{1,0:T(8,128)(2,1)S(1)}, bf16[32,3584]{1,0:T(8,128)(2,1)S(1)}, u32[]{:S(2)}, u32[]{:S(2)}) collective-permute-start(bf16[32,3584]{1,0:T(8,128)(2,1)S(1)} %get-tuple-element.146), channel_id=1, source_target_pairs={{0,8},{2,10},{4,12},{6,14},{8,0},{10,2},{12,4},{14,6},{1,9},{3,11}... | collective-permute-start | bytes 688136 | tf_op jit(solution)/shard_map/ppermute | solution.py:41
  186.2 34.2 %collective-permute-start.27 = (bf16[32,3584]{1,0:T(8,128)(2,1)S(1)}, bf16[32,3584]{1,0:T(8,128)(2,1)S(1)}, u32[]{:S(2)}, u32[]{:S(2)}) collective-permute-start(bf16[32,3584]{1,0:T(8,128)(2,1)S(1)} %get-tuple-element.147), channel_id=1, source_target_pairs={{0,6},{2,4},{4,2},{6,0},{8,14},{10,12},{12,10},{14,8},{1,7},{3,5},... | collective-permute-start | bytes 688136 | tf_op jit(solution)/shard_map/ppermute | solution.py:41
  189.6 38.9 %collective-permute-start.36 = (bf16[32,3584]{1,0:T(8,128)(2,1)S(1)}, bf16[32,3584]{1,0:T(8,128)(2,1)S(1)}, u32[]{:S(2)}, u32[]{:S(2)}) collective-permute-start(bf16[32,3584]{1,0:T(8,128)(2,1)S(1)} %get-tuple-element.175), channel_id=1, source_target_pairs={{0,2},{2,0},{4,6},{6,4},{8,10},{10,8},{12,14},{14,12},{1,3},{3,1},... | collective-permute-start | bytes 688136 | tf_op jit(solution)/shard_map/ppermute | solution.py:41
  191.2 40.6 %collective-permute-start.37 = (bf16[32,3584]{1,0:T(8,128)(2,1)S(1)}, bf16[32,3584]{1,0:T(8,128)(2,1)S(1)}, u32[]{:S(2)}, u32[]{:S(2)}) collective-permute-start(bf16[32,3584]{1,0:T(8,128)(2,1)S(1)} %get-tuple-element.176), channel_id=1, source_target_pairs={{0,4},{2,6},{4,0},{6,2},{8,12},{10,14},{12,8},{14,10},{1,5},{3,7},... | collective-permute-start | bytes 688136 | tf_op jit(solution)/shard_map/ppermute | solution.py:41
  204.1 35.9 %collective-permute-start.38 = (bf16[32,3584]{1,0:T(8,128)(2,1)S(1)}, bf16[32,3584]{1,0:T(8,128)(2,1)S(1)}, u32[]{:S(2)}, u32[]{:S(2)}) collective-permute-start(bf16[32,3584]{1,0:T(8,128)(2,1)S(1)} %get-tuple-element.177), channel_id=1, source_target_pairs={{0,14},{2,12},{4,10},{6,8},{8,6},{10,4},{12,2},{14,0},{1,15},{3,13... | collective-permute-start | bytes 688136 | tf_op jit(solution)/shard_map/ppermute | solution.py:41
  216.2 26.3 %collective-permute-start.39 = (bf16[32,3584]{1,0:T(8,128)(2,1)S(1)}, bf16[32,3584]{1,0:T(8,128)(2,1)S(1)}, u32[]{:S(2)}, u32[]{:S(2)}) collective-permute-start(bf16[32,3584]{1,0:T(8,128)(2,1)S(1)} %get-tuple-element.178), channel_id=1, source_target_pairs={{0,12},{2,14},{4,8},{6,10},{8,4},{10,6},{12,0},{14,2},{1,13},{3,15... | collective-permute-start | bytes 688136 | tf_op jit(solution)/shard_map/ppermute | solution.py:41
  220.4 23.0 %collective-permute-start.40 = (bf16[32,3584]{1,0:T(8,128)(2,1)S(1)}, bf16[32,3584]{1,0:T(8,128)(2,1)S(1)}, u32[]{:S(2)}, u32[]{:S(2)}) collective-permute-start(bf16[32,3584]{1,0:T(8,128)(2,1)S(1)} %get-tuple-element.179), channel_id=1, source_target_pairs={{0,10},{2,8},{4,14},{6,12},{8,2},{10,0},{12,6},{14,4},{1,11},{3,9}... | collective-permute-start | bytes 688136 | tf_op jit(solution)/shard_map/ppermute | solution.py:41
  (44 other events, 667.0 us)

commit v7 on v6

--- a/solution.py
+++ b/solution.py
@@ -169,7 +169,7 @@
         out_shape=[jax.ShapeDtypeStruct((rows, local), jnp.bfloat16)] * devices,
         scratch_shapes=[pltpu.VMEM((devices * rows, width), jnp.bfloat16)],
         compiler_params=pltpu.CompilerParams(
-            dimension_semantics=("arbitrary",), vmem_limit_bytes=40 * MIB
+            dimension_semantics=("arbitrary",), vmem_limit_bytes=28 * MIB
         ),
         cost_estimate=pl.CostEstimate(
             flops=4 * devices * rows * width * local,
@@ -234,7 +234,7 @@
         out_specs=[vmem] * devices,
         out_shape=[jax.ShapeDtypeStruct((rows, local), jnp.bfloat16)] * devices,
         scratch_shapes=[pltpu.VMEM((devices * rows * local // block, block), jnp.bfloat16)],
-        compiler_params=pltpu.CompilerParams(vmem_limit_bytes=40 * MIB),
+        compiler_params=pltpu.CompilerParams(vmem_limit_bytes=20 * MIB),
         cost_estimate=pl.CostEstimate(
             flops=2 * devices * rows * local * block,
             bytes_accessed=4 * devices * rows * local,
@@ -315,7 +315,7 @@
             pltpu.VMEM((local, tile), jnp.bfloat16),
         ],
         compiler_params=pltpu.CompilerParams(
-            dimension_semantics=("arbitrary",), vmem_limit_bytes=40 * MIB
+            dimension_semantics=("arbitrary",), vmem_limit_bytes=24 * MIB
         ),
         cost_estimate=pl.CostEstimate(
             flops=2 * devices * rows * columns * local,
@@ -391,15 +391,15 @@
     right = contract(
         all_after(later_rotated, left[1], top_left[1], top_right[1]), other, most, width - most
     )
-    top_left = split_share(add_share(top_left, order[1], right[1]))
-    top_right = split_share(add_share(top_right, other[1], right[1]))
-    left = split_share(add_share(left, order[0], top_left[1], top_right[1]))
-    right = split_share(add_share(right, other[0], left[1]))
+    left = split_share(add_share(left, order[0], right[1]))
+    top_left = split_share(add_share(top_left, order[1], left[1]))
+    top_right = split_share(add_share(top_right, other[1], left[1]))
+    right = split_share(add_share(right, other[0], top_left[1], top_right[1]))
+    left = split_share(add_share(left, order[1], right[1]))
+    right = split_share(add_share(right, other[1], left[1]))
     top_left = add_share(top_left, order[2], right[1])
     top_right = add_share(top_right, other[2], right[1])
-    left = split_share(add_share(left, order[1], top_left, top_right))
-    right = split_share(add_share(right, other[1], left[1]))
-    left = add_share(left, order[2])
+    left = add_share(left, order[2], top_left, top_right)
     right = add_share(right, other[2], left)
     above = jnp.concatenate([top_left, top_right], axis=1)
     below = jnp.concatenate([left, right], axis=1)

time: 302 us -> 299 us (0.990)
  transfers between devices with their start and end apart: 54 -> 54, of which waited for: 19 -> 20; matrix products, arithmetic and copies ran while one was open for 1% -> 1% of each run, Pallas kernels for 32% -> 32%
where the time goes in v7:
time: 299 us
  starting transfers between devices  112 us (37%)
  Pallas kernels  95.2 us (32%)
  waiting for transfers between devices  81.7 us (27%)
  local copies, waits for them, and re-layouts  8.15 us (3%)
    ppermute x54, starting transfers between devices, exchange(): lax.ppermute(value, AXIS, [(i, i ^ stride) for i in range(lax.axis_size(A...  112 us
    ppermute x54, waiting for transfers between devices, exchange(): lax.ppermute(value, AXIS, [(i, i ^ stride) for i in range(lax.axis_size(A...  81.7 us
    pallas_call x2, Pallas kernels, gate_up(): pl.pallas_call(functools.partial(gate_up_kernel, places, devices, rows, 5...  55.2 us
    pallas_call x4, Pallas kernels, down(): pl.pallas_call(functools.partial(down_kernel, places, rows, local // bloc...  32.8 us
    unnamed x28, local copies, waits for them, and re-layouts  7.29 us
    pallas_call x2, Pallas kernels, rotate(): pl.pallas_call(functools.partial(rotate_kernel, places, rows, (devices *...  6.98 us
  transfers between devices with their start and end apart: 54, of which 20 were waited for; matrix products, arithmetic and copies ran while one was open for 1% of the time, Pallas kernels for 32%

profile of v7, /device:TPU:0, one launch (start us, length us, event | category | flops | bytes accessed | tf_op | source)
XLA Modules:
  0.0 299.0 jit_solution(9402056421342587032)
XLA Ops:
  2.0 4.1 %collective-permute-start.2 = (bf16[32,4096]{1,0:T(8,128)(2,1)S(1)}, bf16[32,4096]{1,0:T(8,128)(2,1)S(1)}, u32[]{:S(2)}, u32[]{:S(2)}) collective-permute-start(bf16[32,4096]{1,0:T(8,128)(2,1)S(1)} %get-tuple-element.115.refs_7_), channel_id=1, source_target_pairs={{0,8},{2,10},{4,12},{6,14},{8,0},{10,2},{12,4},{14,6},{1,9},{3,11}... | collective-permute-start | bytes 786440 | tf_op jit(solution)/shard_map/ppermute | solution.py:41
  9.5 10.3 %collective-permute-done.2.refs_5_ = bf16[32,4096]{1,0:T(8,128)(2,1)S(1)} collective-permute-done((bf16[32,4096]{1,0:T(8,128)(2,1)S(1)}, bf16[32,4096]{1,0:T(8,128)(2,1)S(1)}, u32[]{:S(2)}, u32[]{:S(2)}) %collective-permute-start.2) | collective-permute-done | bytes 262176 | tf_op jit(solution)/shard_map/ppermute | solution.py:41
  21.8 5.5 %collective-permute-start.5 = (bf16[32,4096]{1,0:T(8,128)(2,1)S(1)}, bf16[32,4096]{1,0:T(8,128)(2,1)S(1)}, u32[]{:S(2)}, u32[]{:S(2)}) collective-permute-start(bf16[32,4096]{1,0:T(8,128)(2,1)S(1)} %collective-permute-done.2.refs_5_), channel_id=1, source_target_pairs={{0,2},{2,0},{4,6},{6,4},{8,10},{10,8},{12,14},{14,12},{1,3},{3,1},... | collective-permute-start | bytes 786440 | tf_op jit(solution)/shard_map/ppermute | solution.py:41
  45.9 27.9 %gate_up.2 = (bf16[32,3584]{1,0:T(8,128)(2,1)}, bf16[32,3584]{1,0:T(8,128)(2,1)}, bf16[32,3584]{1,0:T(8,128)(2,1)S(1)}, bf16[32,3584]{1,0:T(8,128)(2,1)S(1)}, bf...) custom-call(bf16[32,4096]{1,0:T(8,128)(2,1)S(1)} %collective-permute, ...), custom_call_target="tpu_custom_call" | custom-call | flops 15032385536 | bytes 58720256 | tf_op jit(solution)/shard_map/gate_up/pallas_call | solution.py:162
  79.3 4.7 %collective-permute-start.9 = (bf16[32,3584]{1,0:T(8,128)(2,1)}, bf16[32,3584]{1,0:T(8,128)(2,1)S(1)}, u32[]{:S(2)}, u32[]{:S(2)}) collective-permute-start(bf16[32,3584]{1,0:T(8,128)(2,1)} %copy-done.12), channel_id=1, source_target_pairs={{0,14},{2,12},{4,10},{6,8},{8,6},{10,4},{12,2},{14,0},{1,15},{3,13... | collective-permute-start | bytes 688136 | tf_op jit(solution)/shard_map/ppermute | solution.py:41
  87.7 4.8 %collective-permute-start.13 = (bf16[32,3584]{1,0:T(8,128)(2,1)}, bf16[32,3584]{1,0:T(8,128)(2,1)S(1)}, u32[]{:S(2)}, u32[]{:S(2)}) collective-permute-start(bf16[32,3584]{1,0:T(8,128)(2,1)} %copy-done.8), channel_id=1, source_target_pairs={{0,6},{2,4},{4,2},{6,0},{8,14},{10,12},{12,10},{14,8},{1,7},{3,5},... | collective-permute-start | bytes 688136 | tf_op jit(solution)/shard_map/ppermute | solution.py:41
  92.5 27.3 %gate_up.3 = (bf16[32,3584]{1,0:T(8,128)(2,1)S(1)}, bf16[32,3584]{1,0:T(8,128)(2,1)S(1)}, bf16[32,3584]{1,0:T(8,128)(2,1)S(1)}, bf16[32,3584]{1,0:T(8,128)(2,1)S...) custom-call(bf16[32,4096]{1,0:T(8,128)(2,1)S(1)} %collective-permute, ...), custom_call_target="tpu_custom_call" | custom-call | flops 15032385536 | bytes 58720256 | tf_op jit(solution)/shard_map/gate_up/pallas_call | solution.py:162
  122.3 10.4 %collective-permute-start.30 = (bf16[32,3584]{1,0:T(8,128)(2,1)S(1)}, bf16[32,3584]{1,0:T(8,128)(2,1)S(1)}, u32[]{:S(2)}, u32[]{:S(2)}) collective-permute-start(bf16[32,3584]{1,0:T(8,128)(2,1)S(1)} %get-tuple-element.152), channel_id=1, source_target_pairs={{0,14},{2,12},{4,10},{6,8},{8,6},{10,4},{12,2},{14,0},{1,15},{3,13... | collective-permute-start | bytes 688136 | tf_op jit(solution)/shard_map/ppermute | solution.py:41
  134.1 3.7 %rotate.2 = (bf16[32,3584]{1,0:T(8,128)(2,1)S(1)}, bf16[32,3584]{1,0:T(8,128)(2,1)S(1)}, bf16[32,3584]{1,0:T(8,128)(2,1)S(1)}, bf16[32,3584]{1,0:T(8,128)(2,1)S(...) custom-call(f32[2,8]{1,0:T(2,128)S(1)} %dynamic-slice_bitcast_fusion, ...), custom_call_target="tpu_custom_call" | custom-call | flops 1644167168 | bytes 3670016 | tf_op jit(solution)/shard_map/rotate/pallas_call | solution.py:229
  147.7 11.1 %collective-permute-start.22 = (bf16[32,3584]{1,0:T(8,128)(2,1)S(1)}, bf16[32,3584]{1,0:T(8,128)(2,1)S(1)}, u32[]{:S(2)}, u32[]{:S(2)}) collective-permute-start(bf16[32,3584]{1,0:T(8,128)(2,1)S(1)} %get-tuple-element.143), channel_id=1, source_target_pairs={{0,4},{2,6},{4,0},{6,2},{8,12},{10,14},{12,8},{14,10},{1,5},{3,7},... | collective-permute-start | bytes 688136 | tf_op jit(solution)/shard_map/ppermute | solution.py:41
  158.8 5.9 %collective-permute-done.32.refs_4_ = bf16[32,3584]{1,0:T(8,128)(2,1)S(1)} collective-permute-done((bf16[32,3584]{1,0:T(8,128)(2,1)S(1)}, bf16[32,3584]{1,0:T(8,128)(2,1)S(1)}, u32[]{:S(2)}, u32[]{:S(2)}) %collective-permute-start.32) | collective-permute-done | bytes 229408 | tf_op jit(solution)/shard_map/ppermute | solution.py:41
  167.2 12.7 %collective-permute-done.33.refs_5_ = bf16[32,3584]{1,0:T(8,128)(2,1)S(1)} collective-permute-done((bf16[32,3584]{1,0:T(8,128)(2,1)S(1)}, bf16[32,3584]{1,0:T(8,128)(2,1)S(1)}, u32[]{:S(2)}, u32[]{:S(2)}) %collective-permute-start.33) | collective-permute-done | bytes 229408 | tf_op jit(solution)/shard_map/ppermute | solution.py:41
  179.8 3.6 %collective-permute-start.24 = (bf16[32,3584]{1,0:T(8,128)(2,1)S(1)}, bf16[32,3584]{1,0:T(8,128)(2,1)S(1)}, u32[]{:S(2)}, u32[]{:S(2)}) collective-permute-start(bf16[32,3584]{1,0:T(8,128)(2,1)S(1)} %get-tuple-element.145), channel_id=1, source_target_pairs={{0,12},{2,14},{4,8},{6,10},{8,4},{10,6},{12,0},{14,2},{1,13},{3,15... | collective-permute-start | bytes 688136 | tf_op jit(solution)/shard_map/ppermute | solution.py:41
  191.2 6.6 %collective-permute-start.37 = (bf16[32,3584]{1,0:T(8,128)(2,1)S(1)}, bf16[32,3584]{1,0:T(8,128)(2,1)S(1)}, u32[]{:S(2)}, u32[]{:S(2)}) collective-permute-start(bf16[32,3584]{1,0:T(8,128)(2,1)S(1)} %get-tuple-element.177), channel_id=1, source_target_pairs={{0,4},{2,6},{4,0},{6,2},{8,12},{10,14},{12,8},{14,10},{1,5},{3,7},... | collective-permute-start | bytes 688136 | tf_op jit(solution)/shard_map/ppermute | solution.py:41
  197.9 6.2 %collective-permute-done.25.refs_4_ = bf16[32,3584]{1,0:T(8,128)(2,1)S(1)} collective-permute-done((bf16[32,3584]{1,0:T(8,128)(2,1)S(1)}, bf16[32,3584]{1,0:T(8,128)(2,1)S(1)}, u32[]{:S(2)}, u32[]{:S(2)}) %collective-permute-start.25) | collective-permute-done | bytes 229408 | tf_op jit(solution)/shard_map/ppermute | solution.py:41
  206.6 9.6 %collective-permute-done.26.refs_5_ = bf16[32,3584]{1,0:T(8,128)(2,1)S(1)} collective-permute-done((bf16[32,3584]{1,0:T(8,128)(2,1)S(1)}, bf16[32,3584]{1,0:T(8,128)(2,1)S(1)}, u32[]{:S(2)}, u32[]{:S(2)}) %collective-permute-start.26) | collective-permute-done | bytes 229408 | tf_op jit(solution)/shard_map/ppermute | solution.py:41
  216.2 4.2 %collective-permute-start.39 = (bf16[32,3584]{1,0:T(8,128)(2,1)S(1)}, bf16[32,3584]{1,0:T(8,128)(2,1)S(1)}, u32[]{:S(2)}, u32[]{:S(2)}) collective-permute-start(bf16[32,3584]{1,0:T(8,128)(2,1)S(1)} %get-tuple-element.179), channel_id=1, source_target_pairs={{0,12},{2,14},{4,8},{6,10},{8,4},{10,6},{12,0},{14,2},{1,13},{3,15... | collective-permute-start | bytes 688136 | tf_op jit(solution)/shard_map/ppermute | solution.py:41
  220.4 8.0 %down.4 = (f32[128,2048]{1,0:T(8,128)S(1)}, bf16[128,2048]{1,0:T(8,128)(2,1)S(1)}) custom-call(bf16[32,3584]{1,0:T(8,128)(2,1)S(1)} %collective-permute-done.21.refs_0_, bf16[32,3584]{1,0:T(8,128)(2,1)S(1)} %collective-permute-done.22.refs_1_, bf16[32,3584]{1,0:T(8,128)(2,1)S(1)} %collective-permute-done.23.refs_2_, ...), custom_call_target="tpu_custom_call" | custom-call | flops 3758096384 | bytes 14680064 | tf_op jit(solution)/shard_map/down/pallas_call | solution.py:302
  231.8 8.2 %down.5 = (f32[128,2048]{1,0:T(8,128)S(1)}, bf16[128,2048]{1,0:T(8,128)(2,1)S(1)}) custom-call(bf16[32,3584]{1,0:T(8,128)(2,1)S(1)} %collective-permute-done.21.refs_0_, bf16[32,3584]{1,0:T(8,128)(2,1)S(1)} %collective-permute-done.22.refs_1_, bf16[32,3584]{1,0:T(8,128)(2,1)S(1)} %collective-permute-done.23.refs_2_, ...), custom_call_target="tpu_custom_call" | custom-call | flops 3758096384 | bytes 14680064 | tf_op jit(solution)/shard_map/down/pallas_call | solution.py:302
  246.8 9.9 %down.6 = (f32[128,2560]{1,0:T(8,128)S(1)}, bf16[128,2560]{1,0:T(8,128)(2,1)S(1)}) custom-call(bf16[32,3584]{1,0:T(8,128)(2,1)S(1)} %collective-permute-done.36.refs_0_, bf16[32,3584]{1,0:T(8,128)(2,1)S(1)} %collective-permute-done.37.refs_1_, bf16[32,3584]{1,0:T(8,128)(2,1)S(1)} %collective-permute-done.38.refs_2_, ...), custom_call_target="tpu_custom_call" | custom-call | flops 4697620480 | bytes 18350080 | tf_op jit(solution)/shard_map/down/pallas_call | solution.py:302
  259.2 6.6 %down.7 = (f32[128,1536]{1,0:T(8,128)S(1)}, bf16[128,1536]{1,0:T(8,128)(2,1)S(1)}) custom-call(bf16[32,3584]{1,0:T(8,128)(2,1)S(1)} %collective-permute-done.36.refs_0_, bf16[32,3584]{1,0:T(8,128)(2,1)S(1)} %collective-permute-done.37.refs_1_, bf16[32,3584]{1,0:T(8,128)(2,1)S(1)} %collective-permute-done.38.refs_2_, ...), custom_call_target="tpu_custom_call" | custom-call | flops 2818572288 | bytes 11010048 | tf_op jit(solution)/shard_map/down/pallas_call | solution.py:302
  277.2 4.7 %collective-permute-done.47 = bf16[128,1536]{1,0:T(8,128)(2,1)S(1)} collective-permute-done((bf16[128,1536]{1,0:T(8,128)(2,1)S(1)}, bf16[128,1536]{1,0:T(8,128)(2,1)S(1)}, u32[]{:S(2)}, u32[]{:S(2)}) %collective-permute-start.47) | collective-permute-done | bytes 393248 | tf_op jit(solution)/shard_map/ppermute | solution.py:41
  283.6 3.8 %collective-permute-done.50 = bf16[64,2560]{1,0:T(8,128)(2,1)S(1)} collective-permute-done((bf16[64,2560]{1,0:T(8,128)(2,1)S(1)}, bf16[64,2560]{1,0:T(8,128)(2,1)S(1)}, u32[]{:S(2)}, u32[]{:S(2)}) %collective-permute-start.50) | collective-permute-done | bytes 327712 | tf_op jit(solution)/shard_map/ppermute | solution.py:41
  290.7 6.3 %collective-permute-done.52 = bf16[32,2560]{1,0:T(8,128)(2,1)S(1)} collective-permute-done((bf16[32,2560]{1,0:T(8,128)(2,1)S(1)}, bf16[32,2560]{1,0:T(8,128)(2,1)S(1)}, u32[]{:S(2)}, u32[]{:S(2)}) %collective-permute-start.52) | collective-permute-done | bytes 163872 | tf_op jit(solution)/shard_map/ppermute | solution.py:41
  (142 shorter events, 92.6 us)
Async XLA Ops:
  38.8 40.5 %collective-permute-start.14 = (bf16[32,4096]{1,0:T(8,128)(2,1)S(1)}, bf16[32,4096]{1,0:T(8,128)(2,1)S(1)}, u32[]{:S(2)}, u32[]{:S(2)}) collective-permute-start(bf16[32,4096]{1,0:T(8,128)(2,1)S(1)} %get-tuple-element.132.refs_7_), channel_id=1, source_target_pairs={{0,2},{2,0},{4,6},{6,4},{8,10},{10,8},{12,14},{14,12},{1,3},{3,1},... | collective-permute-start | bytes 786440 | tf_op jit(solution)/shard_map/ppermute | solution.py:41
  40.4 38.9 %collective-permute-start.19 = (bf16[32,4096]{1,0:T(8,128)(2,1)S(1)}, bf16[32,4096]{1,0:T(8,128)(2,1)S(1)}, u32[]{:S(2)}, u32[]{:S(2)}) collective-permute-start(bf16[32,4096]{1,0:T(8,128)(2,1)S(1)} %collective-permute-done.16.refs_5_), channel_id=1, source_target_pairs={{0,2},{2,0},{4,6},{6,4},{8,10},{10,8},{12,14},{14,12},{1,3},{3,1},... | collective-permute-start | bytes 786440 | tf_op jit(solution)/shard_map/ppermute | solution.py:41
  40.9 43.1 %collective-permute-start.20 = (bf16[32,4096]{1,0:T(8,128)(2,1)S(1)}, bf16[32,4096]{1,0:T(8,128)(2,1)S(1)}, u32[]{:S(2)}, u32[]{:S(2)}) collective-permute-start(bf16[32,4096]{1,0:T(8,128)(2,1)S(1)} %collective-permute-done.15.refs_1_), channel_id=1, source_target_pairs={{0,2},{2,0},{4,6},{6,4},{8,10},{10,8},{12,14},{14,12},{1,3},{3,1},... | collective-permute-start | bytes 786440 | tf_op jit(solution)/shard_map/ppermute | solution.py:41
  42.4 41.6 %collective-permute-start.18 = (bf16[32,4096]{1,0:T(8,128)(2,1)S(1)}, bf16[32,4096]{1,0:T(8,128)(2,1)S(1)}, u32[]{:S(2)}, u32[]{:S(2)}) collective-permute-start(bf16[32,4096]{1,0:T(8,128)(2,1)S(1)} %collective-permute-done.17.refs_3_), channel_id=1, source_target_pairs={{0,2},{2,0},{4,6},{6,4},{8,10},{10,8},{12,14},{14,12},{1,3},{3,1},... | collective-permute-start | bytes 786440 | tf_op jit(solution)/shard_map/ppermute | solution.py:41
  79.3 40.5 %collective-permute-start.9 = (bf16[32,3584]{1,0:T(8,128)(2,1)}, bf16[32,3584]{1,0:T(8,128)(2,1)S(1)}, u32[]{:S(2)}, u32[]{:S(2)}) collective-permute-start(bf16[32,3584]{1,0:T(8,128)(2,1)} %copy-done.12), channel_id=1, source_target_pairs={{0,14},{2,12},{4,10},{6,8},{8,6},{10,4},{12,2},{14,0},{1,15},{3,13... | collective-permute-start | bytes 688136 | tf_op jit(solution)/shard_map/ppermute | solution.py:41
  84.0 38.4 %collective-permute-start.10 = (bf16[32,3584]{1,0:T(8,128)(2,1)}, bf16[32,3584]{1,0:T(8,128)(2,1)S(1)}, u32[]{:S(2)}, u32[]{:S(2)}) collective-permute-start(bf16[32,3584]{1,0:T(8,128)(2,1)} %copy-done.11), channel_id=1, source_target_pairs={{0,12},{2,14},{4,8},{6,10},{8,4},{10,6},{12,0},{14,2},{1,13},{3,15... | collective-permute-start | bytes 688136 | tf_op jit(solution)/shard_map/ppermute | solution.py:41
  84.0 38.4 %collective-permute-start.11 = (bf16[32,3584]{1,0:T(8,128)(2,1)}, bf16[32,3584]{1,0:T(8,128)(2,1)S(1)}, u32[]{:S(2)}, u32[]{:S(2)}) collective-permute-start(bf16[32,3584]{1,0:T(8,128)(2,1)} %copy-done.10), channel_id=1, source_target_pairs={{0,10},{2,8},{4,14},{6,12},{8,2},{10,0},{12,6},{14,4},{1,11},{3,9}... | collective-permute-start | bytes 688136 | tf_op jit(solution)/shard_map/ppermute | solution.py:41
  86.5 46.2 %collective-permute-start.12 = (bf16[32,3584]{1,0:T(8,128)(2,1)}, bf16[32,3584]{1,0:T(8,128)(2,1)S(1)}, u32[]{:S(2)}, u32[]{:S(2)}) collective-permute-start(bf16[32,3584]{1,0:T(8,128)(2,1)} %copy-done.9), channel_id=1, source_target_pairs={{0,8},{2,10},{4,12},{6,14},{8,0},{10,2},{12,4},{14,6},{1,9},{3,11}... | collective-permute-start | bytes 688136 | tf_op jit(solution)/shard_map/ppermute | solution.py:41
  87.7 45.7 %collective-permute-start.13 = (bf16[32,3584]{1,0:T(8,128)(2,1)}, bf16[32,3584]{1,0:T(8,128)(2,1)S(1)}, u32[]{:S(2)}, u32[]{:S(2)}) collective-permute-start(bf16[32,3584]{1,0:T(8,128)(2,1)} %copy-done.8), channel_id=1, source_target_pairs={{0,6},{2,4},{4,2},{6,0},{8,14},{10,12},{12,10},{14,8},{1,7},{3,5},... | collective-permute-start | bytes 688136 | tf_op jit(solution)/shard_map/ppermute | solution.py:41
  122.3 21.8 %collective-permute-start.30 = (bf16[32,3584]{1,0:T(8,128)(2,1)S(1)}, bf16[32,3584]{1,0:T(8,128)(2,1)S(1)}, u32[]{:S(2)}, u32[]{:S(2)}) collective-permute-start(bf16[32,3584]{1,0:T(8,128)(2,1)S(1)} %get-tuple-element.152), channel_id=1, source_target_pairs={{0,14},{2,12},{4,10},{6,8},{8,6},{10,4},{12,2},{14,0},{1,15},{3,13... | collective-permute-start | bytes 688136 | tf_op jit(solution)/shard_map/ppermute | solution.py:41
  133.4 31.3 %collective-permute-start.32 = (bf16[32,3584]{1,0:T(8,128)(2,1)S(1)}, bf16[32,3584]{1,0:T(8,128)(2,1)S(1)}, u32[]{:S(2)}, u32[]{:S(2)}) collective-permute-start(bf16[32,3584]{1,0:T(8,128)(2,1)S(1)} %get-tuple-element.154), channel_id=1, source_target_pairs={{0,10},{2,8},{4,14},{6,12},{8,2},{10,0},{12,6},{14,4},{1,11},{3,9}... | collective-permute-start | bytes 688136 | tf_op jit(solution)/shard_map/ppermute | solution.py:41
  137.8 42.0 %collective-permute-start.33 = (bf16[32,3584]{1,0:T(8,128)(2,1)S(1)}, bf16[32,3584]{1,0:T(8,128)(2,1)S(1)}, u32[]{:S(2)}, u32[]{:S(2)}) collective-permute-start(bf16[32,3584]{1,0:T(8,128)(2,1)S(1)} %get-tuple-element.155), channel_id=1, source_target_pairs={{0,8},{2,10},{4,12},{6,14},{8,0},{10,2},{12,4},{14,6},{1,9},{3,11}... | collective-permute-start | bytes 688136 | tf_op jit(solution)/shard_map/ppermute | solution.py:41
  140.1 43.3 %collective-permute-start.34 = (bf16[32,3584]{1,0:T(8,128)(2,1)S(1)}, bf16[32,3584]{1,0:T(8,128)(2,1)S(1)}, u32[]{:S(2)}, u32[]{:S(2)}) collective-permute-start(bf16[32,3584]{1,0:T(8,128)(2,1)S(1)} %get-tuple-element.156), channel_id=1, source_target_pairs={{0,6},{2,4},{4,2},{6,0},{8,14},{10,12},{12,10},{14,8},{1,7},{3,5},... | collective-permute-start | bytes 688136 | tf_op jit(solution)/shard_map/ppermute | solution.py:41
  144.1 39.3 %collective-permute-start.21 = (bf16[32,3584]{1,0:T(8,128)(2,1)S(1)}, bf16[32,3584]{1,0:T(8,128)(2,1)S(1)}, u32[]{:S(2)}, u32[]{:S(2)}) collective-permute-start(bf16[32,3584]{1,0:T(8,128)(2,1)S(1)} %get-tuple-element.142), channel_id=1, source_target_pairs={{0,2},{2,0},{4,6},{6,4},{8,10},{10,8},{12,14},{14,12},{1,3},{3,1},... | collective-permute-start | bytes 688136 | tf_op jit(solution)/shard_map/ppermute | solution.py:41
  147.7 38.6 %collective-permute-start.22 = (bf16[32,3584]{1,0:T(8,128)(2,1)S(1)}, bf16[32,3584]{1,0:T(8,128)(2,1)S(1)}, u32[]{:S(2)}, u32[]{:S(2)}) collective-permute-start(bf16[32,3584]{1,0:T(8,128)(2,1)S(1)} %get-tuple-element.143), channel_id=1, source_target_pairs={{0,4},{2,6},{4,0},{6,2},{8,12},{10,14},{12,8},{14,10},{1,5},{3,7},... | collective-permute-start | bytes 688136 | tf_op jit(solution)/shard_map/ppermute | solution.py:41
  164.7 24.8 %collective-permute-start.23 = (bf16[32,3584]{1,0:T(8,128)(2,1)S(1)}, bf16[32,3584]{1,0:T(8,128)(2,1)S(1)}, u32[]{:S(2)}, u32[]{:S(2)}) collective-permute-start(bf16[32,3584]{1,0:T(8,128)(2,1)S(1)} %get-tuple-element.144), channel_id=1, source_target_pairs={{0,14},{2,12},{4,10},{6,8},{8,6},{10,4},{12,2},{14,0},{1,15},{3,13... | collective-permute-start | bytes 688136 | tf_op jit(solution)/shard_map/ppermute | solution.py:41
  183.4 20.7 %collective-permute-start.25 = (bf16[32,3584]{1,0:T(8,128)(2,1)S(1)}, bf16[32,3584]{1,0:T(8,128)(2,1)S(1)}, u32[]{:S(2)}, u32[]{:S(2)}) collective-permute-start(bf16[32,3584]{1,0:T(8,128)(2,1)S(1)} %get-tuple-element.146), channel_id=1, source_target_pairs={{0,10},{2,8},{4,14},{6,12},{8,2},{10,0},{12,6},{14,4},{1,11},{3,9}... | collective-permute-start | bytes 688136 | tf_op jit(solution)/shard_map/ppermute | solution.py:41
  183.4 32.7 %collective-permute-start.26 = (bf16[32,3584]{1,0:T(8,128)(2,1)S(1)}, bf16[32,3584]{1,0:T(8,128)(2,1)S(1)}, u32[]{:S(2)}, u32[]{:S(2)}) collective-permute-start(bf16[32,3584]{1,0:T(8,128)(2,1)S(1)} %get-tuple-element.147), channel_id=1, source_target_pairs={{0,8},{2,10},{4,12},{6,14},{8,0},{10,2},{12,4},{14,6},{1,9},{3,11}... | collective-permute-start | bytes 688136 | tf_op jit(solution)/shard_map/ppermute | solution.py:41
  186.2 34.2 %collective-permute-start.27 = (bf16[32,3584]{1,0:T(8,128)(2,1)S(1)}, bf16[32,3584]{1,0:T(8,128)(2,1)S(1)}, u32[]{:S(2)}, u32[]{:S(2)}) collective-permute-start(bf16[32,3584]{1,0:T(8,128)(2,1)S(1)} %get-tuple-element.148), channel_id=1, source_target_pairs={{0,6},{2,4},{4,2},{6,0},{8,14},{10,12},{12,10},{14,8},{1,7},{3,5},... | collective-permute-start | bytes 688136 | tf_op jit(solution)/shard_map/ppermute | solution.py:41
  189.6 38.9 %collective-permute-start.36 = (bf16[32,3584]{1,0:T(8,128)(2,1)S(1)}, bf16[32,3584]{1,0:T(8,128)(2,1)S(1)}, u32[]{:S(2)}, u32[]{:S(2)}) collective-permute-start(bf16[32,3584]{1,0:T(8,128)(2,1)S(1)} %get-tuple-element.176), channel_id=1, source_target_pairs={{0,2},{2,0},{4,6},{6,4},{8,10},{10,8},{12,14},{14,12},{1,3},{3,1},... | collective-permute-start | bytes 688136 | tf_op jit(solution)/shard_map/ppermute | solution.py:41
  191.2 40.6 %collective-permute-start.37 = (bf16[32,3584]{1,0:T(8,128)(2,1)S(1)}, bf16[32,3584]{1,0:T(8,128)(2,1)S(1)}, u32[]{:S(2)}, u32[]{:S(2)}) collective-permute-start(bf16[32,3584]{1,0:T(8,128)(2,1)S(1)} %get-tuple-element.177), channel_id=1, source_target_pairs={{0,4},{2,6},{4,0},{6,2},{8,12},{10,14},{12,8},{14,10},{1,5},{3,7},... | collective-permute-start | bytes 688136 | tf_op jit(solution)/shard_map/ppermute | solution.py:41
  204.1 35.9 %collective-permute-start.38 = (bf16[32,3584]{1,0:T(8,128)(2,1)S(1)}, bf16[32,3584]{1,0:T(8,128)(2,1)S(1)}, u32[]{:S(2)}, u32[]{:S(2)}) collective-permute-start(bf16[32,3584]{1,0:T(8,128)(2,1)S(1)} %get-tuple-element.178), channel_id=1, source_target_pairs={{0,14},{2,12},{4,10},{6,8},{8,6},{10,4},{12,2},{14,0},{1,15},{3,13... | collective-permute-start | bytes 688136 | tf_op jit(solution)/shard_map/ppermute | solution.py:41
  216.2 26.3 %collective-permute-start.39 = (bf16[32,3584]{1,0:T(8,128)(2,1)S(1)}, bf16[32,3584]{1,0:T(8,128)(2,1)S(1)}, u32[]{:S(2)}, u32[]{:S(2)}) collective-permute-start(bf16[32,3584]{1,0:T(8,128)(2,1)S(1)} %get-tuple-element.179), channel_id=1, source_target_pairs={{0,12},{2,14},{4,8},{6,10},{8,4},{10,6},{12,0},{14,2},{1,13},{3,15... | collective-permute-start | bytes 688136 | tf_op jit(solution)/shard_map/ppermute | solution.py:41
  220.4 23.0 %collective-permute-start.40 = (bf16[32,3584]{1,0:T(8,128)(2,1)S(1)}, bf16[32,3584]{1,0:T(8,128)(2,1)S(1)}, u32[]{:S(2)}, u32[]{:S(2)}) collective-permute-start(bf16[32,3584]{1,0:T(8,128)(2,1)S(1)} %get-tuple-element.180), channel_id=1, source_target_pairs={{0,10},{2,8},{4,14},{6,12},{8,2},{10,0},{12,6},{14,4},{1,11},{3,9}... | collective-permute-start | bytes 688136 | tf_op jit(solution)/shard_map/ppermute | solution.py:41
  (44 other events, 673.8 us)

commit v8 on v7

--- a/solution.py
+++ b/solution.py
@@ -53,6 +53,18 @@
     return [(pieces[k], 0) for k in range(devices)]
 
 
+def gather_doubling(own, strides):
+    rows = own.shape[0]
+    held, places = own, {0: 0}
+    for stride in strides[:-1]:
+        places.update({k ^ stride: place + len(places) for k, place in places.items()})
+        held = jnp.concatenate([held, exchange(held, stride)], axis=0)
+    came = exchange(held, strides[-1])
+    pieces = {k: (held, place * rows) for k, place in places.items()}
+    pieces.update({k ^ strides[-1]: (came, place * rows) for k, place in places.items()})
+    return [pieces[k] for k in range(len(pieces))]
+
+
 def departure(devices):
     half = devices // 2
     return [1, 2] + list(range(devices - 1, half - 1, -1)) + list(range(3, half)) + [0]
@@ -156,7 +168,7 @@
     arrays, places = distinct(pieces)
     width, local = gate_codes.shape
     blocks = gate_scales.shape[0]
-    tile = 256
+    tile = 512
     codes = split_blocks(width, tile, 0)
     scales = pl.BlockSpec((blocks, tile), lambda i: (0, i))
     return pl.pallas_call(
@@ -169,7 +181,7 @@
         out_shape=[jax.ShapeDtypeStruct((rows, local), jnp.bfloat16)] * devices,
         scratch_shapes=[pltpu.VMEM((devices * rows, width), jnp.bfloat16)],
         compiler_params=pltpu.CompilerParams(
-            dimension_semantics=("arbitrary",), vmem_limit_bytes=28 * MIB
+            dimension_semantics=("arbitrary",), vmem_limit_bytes=36 * MIB
         ),
         cost_estimate=pl.CostEstimate(
             flops=4 * devices * rows * width * local,
@@ -366,7 +378,8 @@
     half = width // 2
     most = max(half, width // 512 * 5 // 8 * 512)
     own = norm(tokens, norm_gain, [(0, 0, rows, width), (rows, 0, rows, width)])
-    first, second = [gather_tree(piece, devices) for piece in own]
+    first = gather_tree(own[0], devices)
+    second = gather_doubling(own[1], [4, 2, 1])
 
     arrays = gate_up(first, rows, *weights)
     hidden = swap_direct(arrays)

time: 299 us -> 311 us (1.040)
  waiting for transfers between devices: 81.7 us -> 129 us
  starting transfers between devices: 112 us -> 85.4 us
  Pallas kernels: 95.2 us -> 88.2 us
    ppermute x54 -> x50, waiting for transfers between devices: 81.7 us -> 129 us  [exchange(): lax.ppermute(value, AXIS, [(i, i ^ stride) for i in range(lax.axis_size(A...]
    ppermute x54 -> x50, starting transfers between devices: 112 us -> 85.4 us  [exchange(): lax.ppermute(value, AXIS, [(i, i ^ stride) for i in range(lax.axis_size(A...]
    pallas_call x2, Pallas kernels: 55.2 us -> 48.4 us  [gate_up(): pl.pallas_call(functools.partial(gate_up_kernel, places, devices, rows, 5...]
    unnamed x28 -> x26, local copies, waits for them, and re-layouts: 7.29 us -> 5.25 us
  transfers between devices with their start and end apart: 54 -> 50, of which waited for: 20 -> 22; matrix products, arithmetic and copies ran while one was open for 1% -> 1% of each run, Pallas kernels for 32% -> 27%
where the time goes in v8:
time: 311 us
  waiting for transfers between devices  129 us (41%)
  Pallas kernels  88.2 us (28%)
  starting transfers between devices  85.4 us (27%)
  local copies, waits for them, and re-layouts  6.15 us (2%)
    ppermute x50, waiting for transfers between devices, exchange(): lax.ppermute(value, AXIS, [(i, i ^ stride) for i in range(lax.axis_size(A...  129 us
    ppermute x50, starting transfers between devices, exchange(): lax.ppermute(value, AXIS, [(i, i ^ stride) for i in range(lax.axis_size(A...  85.4 us
    pallas_call x2, Pallas kernels, gate_up(): pl.pallas_call(functools.partial(gate_up_kernel, places, devices, rows, 5...  48.4 us
    pallas_call x4, Pallas kernels, down(): pl.pallas_call(functools.partial(down_kernel, places, rows, local // bloc...  32.6 us
    pallas_call x2, Pallas kernels, rotate(): pl.pallas_call(functools.partial(rotate_kernel, places, rows, (devices *...  6.99 us
  transfers between devices with their start and end apart: 50, of which 22 were waited for; matrix products, arithmetic and copies ran while one was open for 1% of the time, Pallas kernels for 27%

profile of v8, /device:TPU:0, one launch (start us, length us, event | category | flops | bytes accessed | tf_op | source)
XLA Modules:
  0.0 310.5 jit_solution(15712832517779058208)
XLA Ops:
  2.0 4.1 %collective-permute-start.14 = (bf16[32,4096]{1,0:T(8,128)(2,1)S(1)}, bf16[32,4096]{1,0:T(8,128)(2,1)S(1)}, u32[]{:S(2)}, u32[]{:S(2)}) collective-permute-start(bf16[32,4096]{1,0:T(8,128)(2,1)S(1)} %get-tuple-element.118), channel_id=1, source_target_pairs={{0,8},{2,10},{4,12},{6,14},{8,0},{10,2},{12,4},{14,6},{1,9},{3,11}... | collective-permute-start | bytes 786440 | tf_op jit(solution)/shard_map/ppermute | solution.py:41
  9.6 15.0 %collective-permute-done.14 = bf16[32,4096]{1,0:T(8,128)(2,1)S(1)} collective-permute-done((bf16[32,4096]{1,0:T(8,128)(2,1)S(1)}, bf16[32,4096]{1,0:T(8,128)(2,1)S(1)}, u32[]{:S(2)}, u32[]{:S(2)}) %collective-permute-start.14) | collective-permute-done | bytes 262176 | tf_op jit(solution)/shard_map/ppermute | solution.py:41
  24.7 4.7 %collective-permute-done.2.refs_5_ = bf16[32,4096]{1,0:T(8,128)(2,1)S(1)} collective-permute-done((bf16[32,4096]{1,0:T(8,128)(2,1)S(1)}, bf16[32,4096]{1,0:T(8,128)(2,1)S(1)}, u32[]{:S(2)}, u32[]{:S(2)}) %collective-permute-start.2) | collective-permute-done | bytes 262176 | tf_op jit(solution)/shard_map/ppermute | solution.py:41
  32.1 14.0 %collective-permute-done.3.refs_3_ = bf16[32,4096]{1,0:T(8,128)(2,1)S(1)} collective-permute-done((bf16[32,4096]{1,0:T(8,128)(2,1)S(1)}, bf16[32,4096]{1,0:T(8,128)(2,1)S(1)}, u32[]{:S(2)}, u32[]{:S(2)}) %collective-permute-start.3) | collective-permute-done | bytes 262176 | tf_op jit(solution)/shard_map/ppermute | solution.py:41
  48.3 7.0 %collective-permute-done.4.refs_2_ = bf16[32,4096]{1,0:T(8,128)(2,1)S(1)} collective-permute-done((bf16[32,4096]{1,0:T(8,128)(2,1)S(1)}, bf16[32,4096]{1,0:T(8,128)(2,1)S(1)}, u32[]{:S(2)}, u32[]{:S(2)}) %collective-permute-start.4) | collective-permute-done | bytes 262176 | tf_op jit(solution)/shard_map/ppermute | solution.py:41
  55.3 24.5 %gate_up.2 = (bf16[32,3584]{1,0:T(8,128)(2,1)}, bf16[32,3584]{1,0:T(8,128)(2,1)}, bf16[32,3584]{1,0:T(8,128)(2,1)S(1)}, bf16[32,3584]{1,0:T(8,128)(2,1)S(1)}, bf...) custom-call(bf16[32,4096]{1,0:T(8,128)(2,1)S(1)} %collective-permute, ...), custom_call_target="tpu_custom_call" | custom-call | flops 15032385536 | bytes 58720256 | tf_op jit(solution)/shard_map/gate_up/pallas_call | solution.py:174
  93.1 4.7 %collective-permute-start.13 = (bf16[32,3584]{1,0:T(8,128)(2,1)}, bf16[32,3584]{1,0:T(8,128)(2,1)S(1)}, u32[]{:S(2)}, u32[]{:S(2)}) collective-permute-start(bf16[32,3584]{1,0:T(8,128)(2,1)} %copy-done.6), channel_id=1, source_target_pairs={{0,6},{2,4},{4,2},{6,0},{8,14},{10,12},{12,10},{14,8},{1,7},{3,5},... | collective-permute-start | bytes 688136 | tf_op jit(solution)/shard_map/ppermute | solution.py:41
  97.8 23.9 %gate_up.3 = (bf16[32,3584]{1,0:T(8,128)(2,1)S(1)}, bf16[32,3584]{1,0:T(8,128)(2,1)S(1)}, bf16[32,3584]{1,0:T(8,128)(2,1)S(1)}, bf16[32,3584]{1,0:T(8,128)(2,1)S...) custom-call(bf16[128,4096]{1,0:T(8,128)(2,1)S(1)} %collective-permut, ...), custom_call_target="tpu_custom_call" | custom-call | flops 15032385536 | bytes 58720256 | tf_op jit(solution)/shard_map/gate_up/pallas_call | solution.py:174
  127.6 3.7 %rotate.2 = (bf16[32,3584]{1,0:T(8,128)(2,1)S(1)}, bf16[32,3584]{1,0:T(8,128)(2,1)S(1)}, bf16[32,3584]{1,0:T(8,128)(2,1)S(1)}, bf16[32,3584]{1,0:T(8,128)(2,1)S(...) custom-call(f32[2,8]{1,0:T(2,128)S(1)} %dynamic-slice_bitcast_fusion, ...), custom_call_target="tpu_custom_call" | custom-call | flops 1644167168 | bytes 3670016 | tf_op jit(solution)/shard_map/rotate/pallas_call | solution.py:241
  149.9 3.7 %collective-permute-done.26.refs_2_ = bf16[32,3584]{1,0:T(8,128)(2,1)S(1)} collective-permute-done((bf16[32,3584]{1,0:T(8,128)(2,1)S(1)}, bf16[32,3584]{1,0:T(8,128)(2,1)S(1)}, u32[]{:S(2)}, u32[]{:S(2)}) %collective-permute-start.26) | collective-permute-done | bytes 229408 | tf_op jit(solution)/shard_map/ppermute | solution.py:41
  153.6 4.3 %collective-permute-start.19 = (bf16[32,3584]{1,0:T(8,128)(2,1)S(1)}, bf16[32,3584]{1,0:T(8,128)(2,1)S(1)}, u32[]{:S(2)}, u32[]{:S(2)}) collective-permute-start(bf16[32,3584]{1,0:T(8,128)(2,1)S(1)} %get-tuple-element.132), channel_id=1, source_target_pairs={{0,14},{2,12},{4,10},{6,8},{8,6},{10,4},{12,2},{14,0},{1,15},{3,13... | collective-permute-start | bytes 688136 | tf_op jit(solution)/shard_map/ppermute | solution.py:41
  158.0 29.0 %collective-permute-done.28.refs_4_ = bf16[32,3584]{1,0:T(8,128)(2,1)S(1)} collective-permute-done((bf16[32,3584]{1,0:T(8,128)(2,1)S(1)}, bf16[32,3584]{1,0:T(8,128)(2,1)S(1)}, u32[]{:S(2)}, u32[]{:S(2)}) %collective-permute-start.28) | collective-permute-done | bytes 229408 | tf_op jit(solution)/shard_map/ppermute | solution.py:41
  187.0 7.0 %collective-permute-done.29.refs_5_ = bf16[32,3584]{1,0:T(8,128)(2,1)S(1)} collective-permute-done((bf16[32,3584]{1,0:T(8,128)(2,1)S(1)}, bf16[32,3584]{1,0:T(8,128)(2,1)S(1)}, u32[]{:S(2)}, u32[]{:S(2)}) %collective-permute-start.29) | collective-permute-done | bytes 229408 | tf_op jit(solution)/shard_map/ppermute | solution.py:41
  194.0 10.0 %collective-permute-start.23 = (bf16[32,3584]{1,0:T(8,128)(2,1)S(1)}, bf16[32,3584]{1,0:T(8,128)(2,1)S(1)}, u32[]{:S(2)}, u32[]{:S(2)}) collective-permute-start(bf16[32,3584]{1,0:T(8,128)(2,1)S(1)} %get-tuple-element.136), channel_id=1, source_target_pairs={{0,6},{2,4},{4,2},{6,0},{8,14},{10,12},{12,10},{14,8},{1,7},{3,5},... | collective-permute-start | bytes 688136 | tf_op jit(solution)/shard_map/ppermute | solution.py:41
  207.3 5.4 %collective-permute-done.21.refs_4_ = bf16[32,3584]{1,0:T(8,128)(2,1)S(1)} collective-permute-done((bf16[32,3584]{1,0:T(8,128)(2,1)S(1)}, bf16[32,3584]{1,0:T(8,128)(2,1)S(1)}, u32[]{:S(2)}, u32[]{:S(2)}) %collective-permute-start.21) | collective-permute-done | bytes 229408 | tf_op jit(solution)/shard_map/ppermute | solution.py:41
  216.6 4.4 %collective-permute-start.34 = (bf16[32,3584]{1,0:T(8,128)(2,1)S(1)}, bf16[32,3584]{1,0:T(8,128)(2,1)S(1)}, u32[]{:S(2)}, u32[]{:S(2)}) collective-permute-start(bf16[32,3584]{1,0:T(8,128)(2,1)S(1)} %get-tuple-element.166), channel_id=1, source_target_pairs={{0,14},{2,12},{4,10},{6,8},{8,6},{10,4},{12,2},{14,0},{1,15},{3,13... | collective-permute-start | bytes 688136 | tf_op jit(solution)/shard_map/ppermute | solution.py:41
  223.0 8.0 %down.4 = (f32[128,2048]{1,0:T(8,128)S(1)}, bf16[128,2048]{1,0:T(8,128)(2,1)S(1)}) custom-call(bf16[32,3584]{1,0:T(8,128)(2,1)S(1)} %collective-permute-done.17.refs_0_, bf16[32,3584]{1,0:T(8,128)(2,1)S(1)} %collective-permute-done.18.refs_1_, bf16[32,3584]{1,0:T(8,128)(2,1)S(1)} %collective-permute-done.19.refs_2_, ...), custom_call_target="tpu_custom_call" | custom-call | flops 3758096384 | bytes 14680064 | tf_op jit(solution)/shard_map/down/pallas_call | solution.py:314
  234.4 8.0 %down.5 = (f32[128,2048]{1,0:T(8,128)S(1)}, bf16[128,2048]{1,0:T(8,128)(2,1)S(1)}) custom-call(bf16[32,3584]{1,0:T(8,128)(2,1)S(1)} %collective-permute-done.17.refs_0_, bf16[32,3584]{1,0:T(8,128)(2,1)S(1)} %collective-permute-done.18.refs_1_, bf16[32,3584]{1,0:T(8,128)(2,1)S(1)} %collective-permute-done.19.refs_2_, ...), custom_call_target="tpu_custom_call" | custom-call | flops 3758096384 | bytes 14680064 | tf_op jit(solution)/shard_map/down/pallas_call | solution.py:314
  244.8 10.6 %collective-permute-done.36.refs_4_ = bf16[32,3584]{1,0:T(8,128)(2,1)S(1)} collective-permute-done((bf16[32,3584]{1,0:T(8,128)(2,1)S(1)}, bf16[32,3584]{1,0:T(8,128)(2,1)S(1)}, u32[]{:S(2)}, u32[]{:S(2)}) %collective-permute-start.36) | collective-permute-done | bytes 229408 | tf_op jit(solution)/shard_map/ppermute | solution.py:41
  256.2 9.9 %down.6 = (f32[128,2560]{1,0:T(8,128)S(1)}, bf16[128,2560]{1,0:T(8,128)(2,1)S(1)}) custom-call(bf16[32,3584]{1,0:T(8,128)(2,1)S(1)} %collective-permute-done.32.refs_0_, bf16[32,3584]{1,0:T(8,128)(2,1)S(1)} %collective-permute-done.33.refs_1_, bf16[32,3584]{1,0:T(8,128)(2,1)S(1)} %collective-permute-done.34.refs_2_, ...), custom_call_target="tpu_custom_call" | custom-call | flops 4697620480 | bytes 18350080 | tf_op jit(solution)/shard_map/down/pallas_call | solution.py:314
  269.3 6.6 %down.7 = (f32[128,1536]{1,0:T(8,128)S(1)}, bf16[128,1536]{1,0:T(8,128)(2,1)S(1)}) custom-call(bf16[32,3584]{1,0:T(8,128)(2,1)S(1)} %collective-permute-done.32.refs_0_, bf16[32,3584]{1,0:T(8,128)(2,1)S(1)} %collective-permute-done.33.refs_1_, bf16[32,3584]{1,0:T(8,128)(2,1)S(1)} %collective-permute-done.34.refs_2_, ...), custom_call_target="tpu_custom_call" | custom-call | flops 2818572288 | bytes 11010048 | tf_op jit(solution)/shard_map/down/pallas_call | solution.py:314
  277.5 5.8 %collective-permute-done.40 = bf16[128,2560]{1,0:T(8,128)(2,1)S(1)} collective-permute-done((bf16[128,2560]{1,0:T(8,128)(2,1)S(1)}, bf16[128,2560]{1,0:T(8,128)(2,1)S(1)}, u32[]{:S(2)}, u32[]{:S(2)}) %collective-permute-start.40) | collective-permute-done | bytes 655392 | tf_op jit(solution)/shard_map/ppermute | solution.py:41
  292.0 4.5 %collective-permute-done.46 = bf16[64,2560]{1,0:T(8,128)(2,1)S(1)} collective-permute-done((bf16[64,2560]{1,0:T(8,128)(2,1)S(1)}, bf16[64,2560]{1,0:T(8,128)(2,1)S(1)}, u32[]{:S(2)}, u32[]{:S(2)}) %collective-permute-start.46) | collective-permute-done | bytes 327712 | tf_op jit(solution)/shard_map/ppermute | solution.py:41
  299.7 5.7 %collective-permute-done.42 = bf16[32,2048]{1,0:T(8,128)(2,1)S(1)} collective-permute-done((bf16[32,2048]{1,0:T(8,128)(2,1)S(1)}, bf16[32,2048]{1,0:T(8,128)(2,1)S(1)}, u32[]{:S(2)}, u32[]{:S(2)}) %collective-permute-start.42) | collective-permute-done | bytes 131104 | tf_op jit(solution)/shard_map/ppermute | solution.py:41
  (134 shorter events, 85.8 us)
Async XLA Ops:
  2.0 22.5 %collective-permute-start.14 = (bf16[32,4096]{1,0:T(8,128)(2,1)S(1)}, bf16[32,4096]{1,0:T(8,128)(2,1)S(1)}, u32[]{:S(2)}, u32[]{:S(2)}) collective-permute-start(bf16[32,4096]{1,0:T(8,128)(2,1)S(1)} %get-tuple-element.118), channel_id=1, source_target_pairs={{0,8},{2,10},{4,12},{6,14},{8,0},{10,2},{12,4},{14,6},{1,9},{3,11}... | collective-permute-start | bytes 786440 | tf_op jit(solution)/shard_map/ppermute | solution.py:41
  6.1 23.3 %collective-permute-start.2 = (bf16[32,4096]{1,0:T(8,128)(2,1)S(1)}, bf16[32,4096]{1,0:T(8,128)(2,1)S(1)}, u32[]{:S(2)}, u32[]{:S(2)}) collective-permute-start(bf16[32,4096]{1,0:T(8,128)(2,1)S(1)} %get-tuple-element.109.refs_7_), channel_id=1, source_target_pairs={{0,8},{2,10},{4,12},{6,14},{8,0},{10,2},{12,4},{14,6},{1,9},{3,11}... | collective-permute-start | bytes 786440 | tf_op jit(solution)/shard_map/ppermute | solution.py:41
  6.2 25.3 %collective-permute-start.1 = (bf16[32,4096]{1,0:T(8,128)(2,1)S(1)}, bf16[32,4096]{1,0:T(8,128)(2,1)S(1)}, u32[]{:S(2)}, u32[]{:S(2)}) collective-permute-start(bf16[32,4096]{1,0:T(8,128)(2,1)S(1)} %get-tuple-element.109.refs_7_), channel_id=1, source_target_pairs={{0,4},{2,6},{4,0},{6,2},{8,12},{10,14},{12,8},{14,10},{1,5},{3,7},... | collective-permute-start | bytes 786440 | tf_op jit(solution)/shard_map/ppermute | solution.py:41
  8.1 40.2 %collective-permute-start = (bf16[32,4096]{1,0:T(8,128)(2,1)S(1)}, bf16[32,4096]{1,0:T(8,128)(2,1)S(1)}, u32[]{:S(2)}, u32[]{:S(2)}) collective-permute-start(bf16[32,4096]{1,0:T(8,128)(2,1)S(1)} %get-tuple-element.109.refs_7_), channel_id=1, source_target_pairs={{0,2},{2,0},{4,6},{6,4},{8,10},{10,8},{12,14},{14,12},{1,3},{3,1},... | collective-permute-start | bytes 786440 | tf_op jit(solution)/shard_map/ppermute | solution.py:41
  24.6 23.1 %collective-permute-start.15 = (bf16[64,4096]{1,0:T(8,128)(2,1)S(1)}, bf16[64,4096]{1,0:T(8,128)(2,1)S(1)}, u32[]{:S(2)}, u32[]{:S(2)}) collective-permute-start(bf16[64,4096]{1,0:T(8,128)(2,1)S(1)} %pad_maximum_fusion), channel_id=1, source_target_pairs={{0,4},{2,6},{4,0},{6,2},{8,12},{10,14},{12,8},{14,10},{1,5},{3,7},... | collective-permute-start | bytes 1572872 | tf_op jit(solution)/shard_map/ppermute | solution.py:41
  47.7 41.5 %collective-permute-start.16 = (bf16[128,4096]{1,0:T(8,128)(2,1)S(1)}, bf16[128,4096]{1,0:T(8,128)(2,1)S(1)}, u32[]{:S(2)}, u32[]{:S(2)}) collective-permute-start(bf16[128,4096]{1,0:T(8,128)(2,1)S(1)} %constant_dynamic-update-slice_fusion.refs_1_), channel_id=1, source_target_pairs={{0,2},{2,0},{4,6},{6,4},{8,10},{10,8},{12,14},{14,12},{1,3},{3,1},... | collective-permute-start | bytes 3145736 | tf_op jit(solution)/shard_map/ppermute | solution.py:41
  85.5 36.3 %collective-permute-start.9 = (bf16[32,3584]{1,0:T(8,128)(2,1)}, bf16[32,3584]{1,0:T(8,128)(2,1)S(1)}, u32[]{:S(2)}, u32[]{:S(2)}) collective-permute-start(bf16[32,3584]{1,0:T(8,128)(2,1)} %copy-done.10), channel_id=1, source_target_pairs={{0,14},{2,12},{4,10},{6,8},{8,6},{10,4},{12,2},{14,0},{1,15},{3,13... | collective-permute-start | bytes 688136 | tf_op jit(solution)/shard_map/ppermute | solution.py:41
  88.9 32.8 %collective-permute-start.10 = (bf16[32,3584]{1,0:T(8,128)(2,1)}, bf16[32,3584]{1,0:T(8,128)(2,1)S(1)}, u32[]{:S(2)}, u32[]{:S(2)}) collective-permute-start(bf16[32,3584]{1,0:T(8,128)(2,1)} %copy-done.9), channel_id=1, source_target_pairs={{0,12},{2,14},{4,8},{6,10},{8,4},{10,6},{12,0},{14,2},{1,13},{3,15... | collective-permute-start | bytes 688136 | tf_op jit(solution)/shard_map/ppermute | solution.py:41
  89.2 35.7 %collective-permute-start.11 = (bf16[32,3584]{1,0:T(8,128)(2,1)}, bf16[32,3584]{1,0:T(8,128)(2,1)S(1)}, u32[]{:S(2)}, u32[]{:S(2)}) collective-permute-start(bf16[32,3584]{1,0:T(8,128)(2,1)} %copy-done.8), channel_id=1, source_target_pairs={{0,10},{2,8},{4,14},{6,12},{8,2},{10,0},{12,6},{14,4},{1,11},{3,9}... | collective-permute-start | bytes 688136 | tf_op jit(solution)/shard_map/ppermute | solution.py:41
  92.5 35.1 %collective-permute-start.12 = (bf16[32,3584]{1,0:T(8,128)(2,1)}, bf16[32,3584]{1,0:T(8,128)(2,1)S(1)}, u32[]{:S(2)}, u32[]{:S(2)}) collective-permute-start(bf16[32,3584]{1,0:T(8,128)(2,1)} %copy-done.7), channel_id=1, source_target_pairs={{0,8},{2,10},{4,12},{6,14},{8,0},{10,2},{12,4},{14,6},{1,9},{3,11}... | collective-permute-start | bytes 688136 | tf_op jit(solution)/shard_map/ppermute | solution.py:41
  93.1 34.5 %collective-permute-start.13 = (bf16[32,3584]{1,0:T(8,128)(2,1)}, bf16[32,3584]{1,0:T(8,128)(2,1)S(1)}, u32[]{:S(2)}, u32[]{:S(2)}) collective-permute-start(bf16[32,3584]{1,0:T(8,128)(2,1)} %copy-done.6), channel_id=1, source_target_pairs={{0,6},{2,4},{4,2},{6,0},{8,14},{10,12},{12,10},{14,8},{1,7},{3,5},... | collective-permute-start | bytes 688136 | tf_op jit(solution)/shard_map/ppermute | solution.py:41
  142.5 44.5 %collective-permute-start.28 = (bf16[32,3584]{1,0:T(8,128)(2,1)S(1)}, bf16[32,3584]{1,0:T(8,128)(2,1)S(1)}, u32[]{:S(2)}, u32[]{:S(2)}) collective-permute-start(bf16[32,3584]{1,0:T(8,128)(2,1)S(1)} %get-tuple-element.142), channel_id=1, source_target_pairs={{0,10},{2,8},{4,14},{6,12},{8,2},{10,0},{12,6},{14,4},{1,11},{3,9}... | collective-permute-start | bytes 688136 | tf_op jit(solution)/shard_map/ppermute | solution.py:41
  145.7 48.3 %collective-permute-start.29 = (bf16[32,3584]{1,0:T(8,128)(2,1)S(1)}, bf16[32,3584]{1,0:T(8,128)(2,1)S(1)}, u32[]{:S(2)}, u32[]{:S(2)}) collective-permute-start(bf16[32,3584]{1,0:T(8,128)(2,1)S(1)} %get-tuple-element.143), channel_id=1, source_target_pairs={{0,8},{2,10},{4,12},{6,14},{8,0},{10,2},{12,4},{14,6},{1,9},{3,11}... | collective-permute-start | bytes 688136 | tf_op jit(solution)/shard_map/ppermute | solution.py:41
  147.9 46.1 %collective-permute-start.30 = (bf16[32,3584]{1,0:T(8,128)(2,1)S(1)}, bf16[32,3584]{1,0:T(8,128)(2,1)S(1)}, u32[]{:S(2)}, u32[]{:S(2)}) collective-permute-start(bf16[32,3584]{1,0:T(8,128)(2,1)S(1)} %get-tuple-element.144), channel_id=1, source_target_pairs={{0,6},{2,4},{4,2},{6,0},{8,14},{10,12},{12,10},{14,8},{1,7},{3,5},... | collective-permute-start | bytes 688136 | tf_op jit(solution)/shard_map/ppermute | solution.py:41
  153.6 53.7 %collective-permute-start.19 = (bf16[32,3584]{1,0:T(8,128)(2,1)S(1)}, bf16[32,3584]{1,0:T(8,128)(2,1)S(1)}, u32[]{:S(2)}, u32[]{:S(2)}) collective-permute-start(bf16[32,3584]{1,0:T(8,128)(2,1)S(1)} %get-tuple-element.132), channel_id=1, source_target_pairs={{0,14},{2,12},{4,10},{6,8},{8,6},{10,4},{12,2},{14,0},{1,15},{3,13... | collective-permute-start | bytes 688136 | tf_op jit(solution)/shard_map/ppermute | solution.py:41
  158.0 49.3 %collective-permute-start.20 = (bf16[32,3584]{1,0:T(8,128)(2,1)S(1)}, bf16[32,3584]{1,0:T(8,128)(2,1)S(1)}, u32[]{:S(2)}, u32[]{:S(2)}) collective-permute-start(bf16[32,3584]{1,0:T(8,128)(2,1)S(1)} %get-tuple-element.133), channel_id=1, source_target_pairs={{0,12},{2,14},{4,8},{6,10},{8,4},{10,6},{12,0},{14,2},{1,13},{3,15... | collective-permute-start | bytes 688136 | tf_op jit(solution)/shard_map/ppermute | solution.py:41
  187.0 25.7 %collective-permute-start.21 = (bf16[32,3584]{1,0:T(8,128)(2,1)S(1)}, bf16[32,3584]{1,0:T(8,128)(2,1)S(1)}, u32[]{:S(2)}, u32[]{:S(2)}) collective-permute-start(bf16[32,3584]{1,0:T(8,128)(2,1)S(1)} %get-tuple-element.134), channel_id=1, source_target_pairs={{0,10},{2,8},{4,14},{6,12},{8,2},{10,0},{12,6},{14,4},{1,11},{3,9}... | collective-permute-start | bytes 688136 | tf_op jit(solution)/shard_map/ppermute | solution.py:41
  216.6 25.9 %collective-permute-start.34 = (bf16[32,3584]{1,0:T(8,128)(2,1)S(1)}, bf16[32,3584]{1,0:T(8,128)(2,1)S(1)}, u32[]{:S(2)}, u32[]{:S(2)}) collective-permute-start(bf16[32,3584]{1,0:T(8,128)(2,1)S(1)} %get-tuple-element.166), channel_id=1, source_target_pairs={{0,14},{2,12},{4,10},{6,8},{8,6},{10,4},{12,2},{14,0},{1,15},{3,13... | collective-permute-start | bytes 688136 | tf_op jit(solution)/shard_map/ppermute | solution.py:41
  221.0 23.9 %collective-permute-start.35 = (bf16[32,3584]{1,0:T(8,128)(2,1)S(1)}, bf16[32,3584]{1,0:T(8,128)(2,1)S(1)}, u32[]{:S(2)}, u32[]{:S(2)}) collective-permute-start(bf16[32,3584]{1,0:T(8,128)(2,1)S(1)} %get-tuple-element.167), channel_id=1, source_target_pairs={{0,12},{2,14},{4,8},{6,10},{8,4},{10,6},{12,0},{14,2},{1,13},{3,15... | collective-permute-start | bytes 688136 | tf_op jit(solution)/shard_map/ppermute | solution.py:41
  221.9 33.5 %collective-permute-start.36 = (bf16[32,3584]{1,0:T(8,128)(2,1)S(1)}, bf16[32,3584]{1,0:T(8,128)(2,1)S(1)}, u32[]{:S(2)}, u32[]{:S(2)}) collective-permute-start(bf16[32,3584]{1,0:T(8,128)(2,1)S(1)} %get-tuple-element.168), channel_id=1, source_target_pairs={{0,10},{2,8},{4,14},{6,12},{8,2},{10,0},{12,6},{14,4},{1,11},{3,9}... | collective-permute-start | bytes 688136 | tf_op jit(solution)/shard_map/ppermute | solution.py:41
  231.0 25.1 %collective-permute-start.37 = (bf16[32,3584]{1,0:T(8,128)(2,1)S(1)}, bf16[32,3584]{1,0:T(8,128)(2,1)S(1)}, u32[]{:S(2)}, u32[]{:S(2)}) collective-permute-start(bf16[32,3584]{1,0:T(8,128)(2,1)S(1)} %get-tuple-element.169), channel_id=1, source_target_pairs={{0,8},{2,10},{4,12},{6,14},{8,0},{10,2},{12,4},{14,6},{1,9},{3,11}... | collective-permute-start | bytes 688136 | tf_op jit(solution)/shard_map/ppermute | solution.py:41
  232.3 23.8 %collective-permute-start.38 = (bf16[32,3584]{1,0:T(8,128)(2,1)S(1)}, bf16[32,3584]{1,0:T(8,128)(2,1)S(1)}, u32[]{:S(2)}, u32[]{:S(2)}) collective-permute-start(bf16[32,3584]{1,0:T(8,128)(2,1)S(1)} %get-tuple-element.170), channel_id=1, source_target_pairs={{0,6},{2,4},{4,2},{6,0},{8,14},{10,12},{12,10},{14,8},{1,7},{3,5},... | collective-permute-start | bytes 688136 | tf_op jit(solution)/shard_map/ppermute | solution.py:41
  242.5 25.8 %collective-permute-start.41 = (bf16[128,2048]{1,0:T(8,128)(2,1)S(1)}, bf16[128,2048]{1,0:T(8,128)(2,1)S(1)}, u32[]{:S(2)}, u32[]{:S(2)}) collective-permute-start(bf16[128,2048]{1,0:T(8,128)(2,1)S(1)} %get-tuple-element.179), channel_id=1, source_target_pairs={{0,4},{2,6},{4,0},{6,2},{8,12},{10,14},{12,8},{14,10},{1,5},{3,7},... | collective-permute-start | bytes 1572872 | tf_op jit(solution)/shard_map/ppermute | solution.py:41
  244.8 23.5 %collective-permute-start.31 = (bf16[128,2048]{1,0:T(8,128)(2,1)S(1)}, bf16[128,2048]{1,0:T(8,128)(2,1)S(1)}, u32[]{:S(2)}, u32[]{:S(2)}) collective-permute-start(bf16[128,2048]{1,0:T(8,128)(2,1)S(1)} %get-tuple-element.163), channel_id=1, source_target_pairs={{0,2},{2,0},{4,6},{6,4},{8,10},{10,8},{12,14},{14,12},{1,3},{3,1},... | collective-permute-start | bytes 1572872 | tf_op jit(solution)/shard_map/ppermute | solution.py:41
  (38 other events, 544.5 us)

commit v9 on v7

--- a/solution.py
+++ b/solution.py
@@ -156,7 +156,7 @@
     arrays, places = distinct(pieces)
     width, local = gate_codes.shape
     blocks = gate_scales.shape[0]
-    tile = 256
+    tile = 512 if local % 512 == 0 else 128
     codes = split_blocks(width, tile, 0)
     scales = pl.BlockSpec((blocks, tile), lambda i: (0, i))
     return pl.pallas_call(
@@ -169,7 +169,7 @@
         out_shape=[jax.ShapeDtypeStruct((rows, local), jnp.bfloat16)] * devices,
         scratch_shapes=[pltpu.VMEM((devices * rows, width), jnp.bfloat16)],
         compiler_params=pltpu.CompilerParams(
-            dimension_semantics=("arbitrary",), vmem_limit_bytes=28 * MIB
+            dimension_semantics=("arbitrary",), vmem_limit_bytes=36 * MIB
         ),
         cost_estimate=pl.CostEstimate(
             flops=4 * devices * rows * width * local,

time: 299 us -> 294 us (0.983)
  starting transfers between devices: 112 us -> 121 us
  waiting for transfers between devices: 81.7 us -> 73.9 us
  Pallas kernels: 95.2 us -> 88.5 us
    ppermute x54, starting transfers between devices: 112 us -> 121 us  [exchange(): lax.ppermute(value, AXIS, [(i, i ^ stride) for i in range(lax.axis_size(A...]
    ppermute x54, waiting for transfers between devices: 81.7 us -> 73.9 us  [exchange(): lax.ppermute(value, AXIS, [(i, i ^ stride) for i in range(lax.axis_size(A...]
    pallas_call x2, Pallas kernels: 55.2 us -> 48.5 us  [gate_up(): pl.pallas_call(functools.partial(gate_up_kernel, places, devices, rows, 5...]
  transfers between devices with their start and end apart: 54 -> 54, of which waited for: 20 -> 19; matrix products, arithmetic and copies ran while one was open for 1% -> 1% of each run, Pallas kernels for 32% -> 30%
where the time goes in v9:
time: 294 us
  starting transfers between devices  121 us (41%)
  Pallas kernels  88.5 us (30%)
  waiting for transfers between devices  73.9 us (25%)
  local copies, waits for them, and re-layouts  8.15 us (3%)
    ppermute x54, starting transfers between devices, exchange(): lax.ppermute(value, AXIS, [(i, i ^ stride) for i in range(lax.axis_size(A...  121 us
    ppermute x54, waiting for transfers between devices, exchange(): lax.ppermute(value, AXIS, [(i, i ^ stride) for i in range(lax.axis_size(A...  73.9 us
    pallas_call x2, Pallas kernels, gate_up(): pl.pallas_call(functools.partial(gate_up_kernel, places, devices, rows, 5...  48.5 us
    pallas_call x4, Pallas kernels, down(): pl.pallas_call(functools.partial(down_kernel, places, rows, local // bloc...  32.8 us
    unnamed x28, local copies, waits for them, and re-layouts  7.29 us
    pallas_call x2, Pallas kernels, rotate(): pl.pallas_call(functools.partial(rotate_kernel, places, rows, (devices *...  7 us
  transfers between devices with their start and end apart: 54, of which 19 were waited for; matrix products, arithmetic and copies ran while one was open for 1% of the time, Pallas kernels for 30%

profile of v9, /device:TPU:0, one launch (start us, length us, event | category | flops | bytes accessed | tf_op | source)
XLA Modules:
  0.0 293.7 jit_solution(5074669085617850137)
XLA Ops:
  2.0 4.1 %collective-permute-start.2 = (bf16[32,4096]{1,0:T(8,128)(2,1)S(1)}, bf16[32,4096]{1,0:T(8,128)(2,1)S(1)}, u32[]{:S(2)}, u32[]{:S(2)}) collective-permute-start(bf16[32,4096]{1,0:T(8,128)(2,1)S(1)} %get-tuple-element.115.refs_7_), channel_id=1, source_target_pairs={{0,8},{2,10},{4,12},{6,14},{8,0},{10,2},{12,4},{14,6},{1,9},{3,11}... | collective-permute-start | bytes 786440 | tf_op jit(solution)/shard_map/ppermute | solution.py:41
  9.5 10.3 %collective-permute-done.2.refs_5_ = bf16[32,4096]{1,0:T(8,128)(2,1)S(1)} collective-permute-done((bf16[32,4096]{1,0:T(8,128)(2,1)S(1)}, bf16[32,4096]{1,0:T(8,128)(2,1)S(1)}, u32[]{:S(2)}, u32[]{:S(2)}) %collective-permute-start.2) | collective-permute-done | bytes 262176 | tf_op jit(solution)/shard_map/ppermute | solution.py:41
  21.8 5.5 %collective-permute-start.5 = (bf16[32,4096]{1,0:T(8,128)(2,1)S(1)}, bf16[32,4096]{1,0:T(8,128)(2,1)S(1)}, u32[]{:S(2)}, u32[]{:S(2)}) collective-permute-start(bf16[32,4096]{1,0:T(8,128)(2,1)S(1)} %collective-permute-done.2.refs_5_), channel_id=1, source_target_pairs={{0,2},{2,0},{4,6},{6,4},{8,10},{10,8},{12,14},{14,12},{1,3},{3,1},... | collective-permute-start | bytes 786440 | tf_op jit(solution)/shard_map/ppermute | solution.py:41
  45.9 24.5 %gate_up.2 = (bf16[32,3584]{1,0:T(8,128)(2,1)}, bf16[32,3584]{1,0:T(8,128)(2,1)}, bf16[32,3584]{1,0:T(8,128)(2,1)S(1)}, bf16[32,3584]{1,0:T(8,128)(2,1)S(1)}, bf...) custom-call(bf16[32,4096]{1,0:T(8,128)(2,1)S(1)} %collective-permute, ...), custom_call_target="tpu_custom_call" | custom-call | flops 15032385536 | bytes 58720256 | tf_op jit(solution)/shard_map/gate_up/pallas_call | solution.py:162
  76.0 4.7 %collective-permute-start.9 = (bf16[32,3584]{1,0:T(8,128)(2,1)}, bf16[32,3584]{1,0:T(8,128)(2,1)S(1)}, u32[]{:S(2)}, u32[]{:S(2)}) collective-permute-start(bf16[32,3584]{1,0:T(8,128)(2,1)} %copy-done.12), channel_id=1, source_target_pairs={{0,14},{2,12},{4,10},{6,8},{8,6},{10,4},{12,2},{14,0},{1,15},{3,13... | collective-permute-start | bytes 688136 | tf_op jit(solution)/shard_map/ppermute | solution.py:41
  84.4 4.8 %collective-permute-start.13 = (bf16[32,3584]{1,0:T(8,128)(2,1)}, bf16[32,3584]{1,0:T(8,128)(2,1)S(1)}, u32[]{:S(2)}, u32[]{:S(2)}) collective-permute-start(bf16[32,3584]{1,0:T(8,128)(2,1)} %copy-done.8), channel_id=1, source_target_pairs={{0,6},{2,4},{4,2},{6,0},{8,14},{10,12},{12,10},{14,8},{1,7},{3,5},... | collective-permute-start | bytes 688136 | tf_op jit(solution)/shard_map/ppermute | solution.py:41
  89.1 23.9 %gate_up.3 = (bf16[32,3584]{1,0:T(8,128)(2,1)S(1)}, bf16[32,3584]{1,0:T(8,128)(2,1)S(1)}, bf16[32,3584]{1,0:T(8,128)(2,1)S(1)}, bf16[32,3584]{1,0:T(8,128)(2,1)S...) custom-call(bf16[32,4096]{1,0:T(8,128)(2,1)S(1)} %collective-permute, ...), custom_call_target="tpu_custom_call" | custom-call | flops 15032385536 | bytes 58720256 | tf_op jit(solution)/shard_map/gate_up/pallas_call | solution.py:162
  117.4 8.6 %collective-permute-start.30 = (bf16[32,3584]{1,0:T(8,128)(2,1)S(1)}, bf16[32,3584]{1,0:T(8,128)(2,1)S(1)}, u32[]{:S(2)}, u32[]{:S(2)}) collective-permute-start(bf16[32,3584]{1,0:T(8,128)(2,1)S(1)} %get-tuple-element.152), channel_id=1, source_target_pairs={{0,14},{2,12},{4,10},{6,8},{8,6},{10,4},{12,2},{14,0},{1,15},{3,13... | collective-permute-start | bytes 688136 | tf_op jit(solution)/shard_map/ppermute | solution.py:41
  140.9 11.1 %collective-permute-start.22 = (bf16[32,3584]{1,0:T(8,128)(2,1)S(1)}, bf16[32,3584]{1,0:T(8,128)(2,1)S(1)}, u32[]{:S(2)}, u32[]{:S(2)}) collective-permute-start(bf16[32,3584]{1,0:T(8,128)(2,1)S(1)} %get-tuple-element.143), channel_id=1, source_target_pairs={{0,4},{2,6},{4,0},{6,2},{8,12},{10,14},{12,8},{14,10},{1,5},{3,7},... | collective-permute-start | bytes 688136 | tf_op jit(solution)/shard_map/ppermute | solution.py:41
  152.1 5.9 %collective-permute-done.32.refs_4_ = bf16[32,3584]{1,0:T(8,128)(2,1)S(1)} collective-permute-done((bf16[32,3584]{1,0:T(8,128)(2,1)S(1)}, bf16[32,3584]{1,0:T(8,128)(2,1)S(1)}, u32[]{:S(2)}, u32[]{:S(2)}) %collective-permute-start.32) | collective-permute-done | bytes 229408 | tf_op jit(solution)/shard_map/ppermute | solution.py:41
  160.4 12.5 %collective-permute-done.33.refs_5_ = bf16[32,3584]{1,0:T(8,128)(2,1)S(1)} collective-permute-done((bf16[32,3584]{1,0:T(8,128)(2,1)S(1)}, bf16[32,3584]{1,0:T(8,128)(2,1)S(1)}, u32[]{:S(2)}, u32[]{:S(2)}) %collective-permute-start.33) | collective-permute-done | bytes 229408 | tf_op jit(solution)/shard_map/ppermute | solution.py:41
  172.8 3.8 %collective-permute-start.24 = (bf16[32,3584]{1,0:T(8,128)(2,1)S(1)}, bf16[32,3584]{1,0:T(8,128)(2,1)S(1)}, u32[]{:S(2)}, u32[]{:S(2)}) collective-permute-start(bf16[32,3584]{1,0:T(8,128)(2,1)S(1)} %get-tuple-element.145), channel_id=1, source_target_pairs={{0,12},{2,14},{4,8},{6,10},{8,4},{10,6},{12,0},{14,2},{1,13},{3,15... | collective-permute-start | bytes 688136 | tf_op jit(solution)/shard_map/ppermute | solution.py:41
  184.4 7.3 %collective-permute-start.37 = (bf16[32,3584]{1,0:T(8,128)(2,1)S(1)}, bf16[32,3584]{1,0:T(8,128)(2,1)S(1)}, u32[]{:S(2)}, u32[]{:S(2)}) collective-permute-start(bf16[32,3584]{1,0:T(8,128)(2,1)S(1)} %get-tuple-element.177), channel_id=1, source_target_pairs={{0,4},{2,6},{4,0},{6,2},{8,12},{10,14},{12,8},{14,10},{1,5},{3,7},... | collective-permute-start | bytes 688136 | tf_op jit(solution)/shard_map/ppermute | solution.py:41
  191.7 4.7 %collective-permute-done.25.refs_4_ = bf16[32,3584]{1,0:T(8,128)(2,1)S(1)} collective-permute-done((bf16[32,3584]{1,0:T(8,128)(2,1)S(1)}, bf16[32,3584]{1,0:T(8,128)(2,1)S(1)}, u32[]{:S(2)}, u32[]{:S(2)}) %collective-permute-start.25) | collective-permute-done | bytes 229408 | tf_op jit(solution)/shard_map/ppermute | solution.py:41
  196.3 4.1 %collective-permute-start.38 = (bf16[32,3584]{1,0:T(8,128)(2,1)S(1)}, bf16[32,3584]{1,0:T(8,128)(2,1)S(1)}, u32[]{:S(2)}, u32[]{:S(2)}) collective-permute-start(bf16[32,3584]{1,0:T(8,128)(2,1)S(1)} %get-tuple-element.178), channel_id=1, source_target_pairs={{0,14},{2,12},{4,10},{6,8},{8,6},{10,4},{12,2},{14,0},{1,15},{3,13... | collective-permute-start | bytes 688136 | tf_op jit(solution)/shard_map/ppermute | solution.py:41
  200.4 13.8 %collective-permute-start.39 = (bf16[32,3584]{1,0:T(8,128)(2,1)S(1)}, bf16[32,3584]{1,0:T(8,128)(2,1)S(1)}, u32[]{:S(2)}, u32[]{:S(2)}) collective-permute-start(bf16[32,3584]{1,0:T(8,128)(2,1)S(1)} %get-tuple-element.179), channel_id=1, source_target_pairs={{0,12},{2,14},{4,8},{6,10},{8,4},{10,6},{12,0},{14,2},{1,13},{3,15... | collective-permute-start | bytes 688136 | tf_op jit(solution)/shard_map/ppermute | solution.py:41
  214.2 8.2 %down.4 = (f32[128,2048]{1,0:T(8,128)S(1)}, bf16[128,2048]{1,0:T(8,128)(2,1)S(1)}) custom-call(bf16[32,3584]{1,0:T(8,128)(2,1)S(1)} %collective-permute-done.21.refs_0_, bf16[32,3584]{1,0:T(8,128)(2,1)S(1)} %collective-permute-done.22.refs_1_, bf16[32,3584]{1,0:T(8,128)(2,1)S(1)} %collective-permute-done.23.refs_2_, ...), custom_call_target="tpu_custom_call" | custom-call | flops 3758096384 | bytes 14680064 | tf_op jit(solution)/shard_map/down/pallas_call | solution.py:302
  225.9 8.0 %down.5 = (f32[128,2048]{1,0:T(8,128)S(1)}, bf16[128,2048]{1,0:T(8,128)(2,1)S(1)}) custom-call(bf16[32,3584]{1,0:T(8,128)(2,1)S(1)} %collective-permute-done.21.refs_0_, bf16[32,3584]{1,0:T(8,128)(2,1)S(1)} %collective-permute-done.22.refs_1_, bf16[32,3584]{1,0:T(8,128)(2,1)S(1)} %collective-permute-done.23.refs_2_, ...), custom_call_target="tpu_custom_call" | custom-call | flops 3758096384 | bytes 14680064 | tf_op jit(solution)/shard_map/down/pallas_call | solution.py:302
  237.5 3.8 %collective-permute-done.42.refs_6_ = bf16[32,3584]{1,0:T(8,128)(2,1)S(1)} collective-permute-done((bf16[32,3584]{1,0:T(8,128)(2,1)S(1)}, bf16[32,3584]{1,0:T(8,128)(2,1)S(1)}, u32[]{:S(2)}, u32[]{:S(2)}) %collective-permute-start.42) | collective-permute-done | bytes 229408 | tf_op jit(solution)/shard_map/ppermute | solution.py:41
  241.2 9.9 %down.6 = (f32[128,2560]{1,0:T(8,128)S(1)}, bf16[128,2560]{1,0:T(8,128)(2,1)S(1)}) custom-call(bf16[32,3584]{1,0:T(8,128)(2,1)S(1)} %collective-permute-done.36.refs_0_, bf16[32,3584]{1,0:T(8,128)(2,1)S(1)} %collective-permute-done.37.refs_1_, bf16[32,3584]{1,0:T(8,128)(2,1)S(1)} %collective-permute-done.38.refs_2_, ...), custom_call_target="tpu_custom_call" | custom-call | flops 4697620480 | bytes 18350080 | tf_op jit(solution)/shard_map/down/pallas_call | solution.py:302
  253.6 6.6 %down.7 = (f32[128,1536]{1,0:T(8,128)S(1)}, bf16[128,1536]{1,0:T(8,128)(2,1)S(1)}) custom-call(bf16[32,3584]{1,0:T(8,128)(2,1)S(1)} %collective-permute-done.36.refs_0_, bf16[32,3584]{1,0:T(8,128)(2,1)S(1)} %collective-permute-done.37.refs_1_, bf16[32,3584]{1,0:T(8,128)(2,1)S(1)} %collective-permute-done.38.refs_2_, ...), custom_call_target="tpu_custom_call" | custom-call | flops 2818572288 | bytes 11010048 | tf_op jit(solution)/shard_map/down/pallas_call | solution.py:302
  271.4 5.2 %collective-permute-done.47 = bf16[128,1536]{1,0:T(8,128)(2,1)S(1)} collective-permute-done((bf16[128,1536]{1,0:T(8,128)(2,1)S(1)}, bf16[128,1536]{1,0:T(8,128)(2,1)S(1)}, u32[]{:S(2)}, u32[]{:S(2)}) %collective-permute-start.47) | collective-permute-done | bytes 393248 | tf_op jit(solution)/shard_map/ppermute | solution.py:41
  277.5 4.1 %collective-permute-done.50 = bf16[64,2560]{1,0:T(8,128)(2,1)S(1)} collective-permute-done((bf16[64,2560]{1,0:T(8,128)(2,1)S(1)}, bf16[64,2560]{1,0:T(8,128)(2,1)S(1)}, u32[]{:S(2)}, u32[]{:S(2)}) %collective-permute-start.50) | collective-permute-done | bytes 327712 | tf_op jit(solution)/shard_map/ppermute | solution.py:41
  284.9 6.7 %collective-permute-done.52 = bf16[32,2560]{1,0:T(8,128)(2,1)S(1)} collective-permute-done((bf16[32,2560]{1,0:T(8,128)(2,1)S(1)}, bf16[32,2560]{1,0:T(8,128)(2,1)S(1)}, u32[]{:S(2)}, u32[]{:S(2)}) %collective-permute-start.52) | collective-permute-done | bytes 163872 | tf_op jit(solution)/shard_map/ppermute | solution.py:41
  (142 shorter events, 91.4 us)
Async XLA Ops:
  9.2 20.2 %collective-permute-start.16 = (bf16[32,4096]{1,0:T(8,128)(2,1)S(1)}, bf16[32,4096]{1,0:T(8,128)(2,1)S(1)}, u32[]{:S(2)}, u32[]{:S(2)}) collective-permute-start(bf16[32,4096]{1,0:T(8,128)(2,1)S(1)} %get-tuple-element.132.refs_7_), channel_id=1, source_target_pairs={{0,8},{2,10},{4,12},{6,14},{8,0},{10,2},{12,4},{14,6},{1,9},{3,11}... | collective-permute-start | bytes 786440 | tf_op jit(solution)/shard_map/ppermute | solution.py:41
  38.8 37.1 %collective-permute-start.14 = (bf16[32,4096]{1,0:T(8,128)(2,1)S(1)}, bf16[32,4096]{1,0:T(8,128)(2,1)S(1)}, u32[]{:S(2)}, u32[]{:S(2)}) collective-permute-start(bf16[32,4096]{1,0:T(8,128)(2,1)S(1)} %get-tuple-element.132.refs_7_), channel_id=1, source_target_pairs={{0,2},{2,0},{4,6},{6,4},{8,10},{10,8},{12,14},{14,12},{1,3},{3,1},... | collective-permute-start | bytes 786440 | tf_op jit(solution)/shard_map/ppermute | solution.py:41
  40.4 35.6 %collective-permute-start.19 = (bf16[32,4096]{1,0:T(8,128)(2,1)S(1)}, bf16[32,4096]{1,0:T(8,128)(2,1)S(1)}, u32[]{:S(2)}, u32[]{:S(2)}) collective-permute-start(bf16[32,4096]{1,0:T(8,128)(2,1)S(1)} %collective-permute-done.16.refs_5_), channel_id=1, source_target_pairs={{0,2},{2,0},{4,6},{6,4},{8,10},{10,8},{12,14},{14,12},{1,3},{3,1},... | collective-permute-start | bytes 786440 | tf_op jit(solution)/shard_map/ppermute | solution.py:41
  40.9 39.8 %collective-permute-start.20 = (bf16[32,4096]{1,0:T(8,128)(2,1)S(1)}, bf16[32,4096]{1,0:T(8,128)(2,1)S(1)}, u32[]{:S(2)}, u32[]{:S(2)}) collective-permute-start(bf16[32,4096]{1,0:T(8,128)(2,1)S(1)} %collective-permute-done.15.refs_1_), channel_id=1, source_target_pairs={{0,2},{2,0},{4,6},{6,4},{8,10},{10,8},{12,14},{14,12},{1,3},{3,1},... | collective-permute-start | bytes 786440 | tf_op jit(solution)/shard_map/ppermute | solution.py:41
  42.4 38.2 %collective-permute-start.18 = (bf16[32,4096]{1,0:T(8,128)(2,1)S(1)}, bf16[32,4096]{1,0:T(8,128)(2,1)S(1)}, u32[]{:S(2)}, u32[]{:S(2)}) collective-permute-start(bf16[32,4096]{1,0:T(8,128)(2,1)S(1)} %collective-permute-done.17.refs_3_), channel_id=1, source_target_pairs={{0,2},{2,0},{4,6},{6,4},{8,10},{10,8},{12,14},{14,12},{1,3},{3,1},... | collective-permute-start | bytes 786440 | tf_op jit(solution)/shard_map/ppermute | solution.py:41
  76.0 37.1 %collective-permute-start.9 = (bf16[32,3584]{1,0:T(8,128)(2,1)}, bf16[32,3584]{1,0:T(8,128)(2,1)S(1)}, u32[]{:S(2)}, u32[]{:S(2)}) collective-permute-start(bf16[32,3584]{1,0:T(8,128)(2,1)} %copy-done.12), channel_id=1, source_target_pairs={{0,14},{2,12},{4,10},{6,8},{8,6},{10,4},{12,2},{14,0},{1,15},{3,13... | collective-permute-start | bytes 688136 | tf_op jit(solution)/shard_map/ppermute | solution.py:41
  80.6 35.0 %collective-permute-start.10 = (bf16[32,3584]{1,0:T(8,128)(2,1)}, bf16[32,3584]{1,0:T(8,128)(2,1)S(1)}, u32[]{:S(2)}, u32[]{:S(2)}) collective-permute-start(bf16[32,3584]{1,0:T(8,128)(2,1)} %copy-done.11), channel_id=1, source_target_pairs={{0,12},{2,14},{4,8},{6,10},{8,4},{10,6},{12,0},{14,2},{1,13},{3,15... | collective-permute-start | bytes 688136 | tf_op jit(solution)/shard_map/ppermute | solution.py:41
  80.7 36.7 %collective-permute-start.11 = (bf16[32,3584]{1,0:T(8,128)(2,1)}, bf16[32,3584]{1,0:T(8,128)(2,1)S(1)}, u32[]{:S(2)}, u32[]{:S(2)}) collective-permute-start(bf16[32,3584]{1,0:T(8,128)(2,1)} %copy-done.10), channel_id=1, source_target_pairs={{0,10},{2,8},{4,14},{6,12},{8,2},{10,0},{12,6},{14,4},{1,11},{3,9}... | collective-permute-start | bytes 688136 | tf_op jit(solution)/shard_map/ppermute | solution.py:41
  83.1 42.8 %collective-permute-start.12 = (bf16[32,3584]{1,0:T(8,128)(2,1)}, bf16[32,3584]{1,0:T(8,128)(2,1)S(1)}, u32[]{:S(2)}, u32[]{:S(2)}) collective-permute-start(bf16[32,3584]{1,0:T(8,128)(2,1)} %copy-done.9), channel_id=1, source_target_pairs={{0,8},{2,10},{4,12},{6,14},{8,0},{10,2},{12,4},{14,6},{1,9},{3,11}... | collective-permute-start | bytes 688136 | tf_op jit(solution)/shard_map/ppermute | solution.py:41
  84.4 42.3 %collective-permute-start.13 = (bf16[32,3584]{1,0:T(8,128)(2,1)}, bf16[32,3584]{1,0:T(8,128)(2,1)S(1)}, u32[]{:S(2)}, u32[]{:S(2)}) collective-permute-start(bf16[32,3584]{1,0:T(8,128)(2,1)} %copy-done.8), channel_id=1, source_target_pairs={{0,6},{2,4},{4,2},{6,0},{8,14},{10,12},{12,10},{14,8},{1,7},{3,5},... | collective-permute-start | bytes 688136 | tf_op jit(solution)/shard_map/ppermute | solution.py:41
  117.4 20.0 %collective-permute-start.30 = (bf16[32,3584]{1,0:T(8,128)(2,1)S(1)}, bf16[32,3584]{1,0:T(8,128)(2,1)S(1)}, u32[]{:S(2)}, u32[]{:S(2)}) collective-permute-start(bf16[32,3584]{1,0:T(8,128)(2,1)S(1)} %get-tuple-element.152), channel_id=1, source_target_pairs={{0,14},{2,12},{4,10},{6,8},{8,6},{10,4},{12,2},{14,0},{1,15},{3,13... | collective-permute-start | bytes 688136 | tf_op jit(solution)/shard_map/ppermute | solution.py:41
  126.7 31.3 %collective-permute-start.32 = (bf16[32,3584]{1,0:T(8,128)(2,1)S(1)}, bf16[32,3584]{1,0:T(8,128)(2,1)S(1)}, u32[]{:S(2)}, u32[]{:S(2)}) collective-permute-start(bf16[32,3584]{1,0:T(8,128)(2,1)S(1)} %get-tuple-element.154), channel_id=1, source_target_pairs={{0,10},{2,8},{4,14},{6,12},{8,2},{10,0},{12,6},{14,4},{1,11},{3,9}... | collective-permute-start | bytes 688136 | tf_op jit(solution)/shard_map/ppermute | solution.py:41
  131.1 41.7 %collective-permute-start.33 = (bf16[32,3584]{1,0:T(8,128)(2,1)S(1)}, bf16[32,3584]{1,0:T(8,128)(2,1)S(1)}, u32[]{:S(2)}, u32[]{:S(2)}) collective-permute-start(bf16[32,3584]{1,0:T(8,128)(2,1)S(1)} %get-tuple-element.155), channel_id=1, source_target_pairs={{0,8},{2,10},{4,12},{6,14},{8,0},{10,2},{12,4},{14,6},{1,9},{3,11}... | collective-permute-start | bytes 688136 | tf_op jit(solution)/shard_map/ppermute | solution.py:41
  133.4 43.2 %collective-permute-start.34 = (bf16[32,3584]{1,0:T(8,128)(2,1)S(1)}, bf16[32,3584]{1,0:T(8,128)(2,1)S(1)}, u32[]{:S(2)}, u32[]{:S(2)}) collective-permute-start(bf16[32,3584]{1,0:T(8,128)(2,1)S(1)} %get-tuple-element.156), channel_id=1, source_target_pairs={{0,6},{2,4},{4,2},{6,0},{8,14},{10,12},{12,10},{14,8},{1,7},{3,5},... | collective-permute-start | bytes 688136 | tf_op jit(solution)/shard_map/ppermute | solution.py:41
  137.4 39.2 %collective-permute-start.21 = (bf16[32,3584]{1,0:T(8,128)(2,1)S(1)}, bf16[32,3584]{1,0:T(8,128)(2,1)S(1)}, u32[]{:S(2)}, u32[]{:S(2)}) collective-permute-start(bf16[32,3584]{1,0:T(8,128)(2,1)S(1)} %get-tuple-element.142), channel_id=1, source_target_pairs={{0,2},{2,0},{4,6},{6,4},{8,10},{10,8},{12,14},{14,12},{1,3},{3,1},... | collective-permute-start | bytes 688136 | tf_op jit(solution)/shard_map/ppermute | solution.py:41
  140.9 39.0 %collective-permute-start.22 = (bf16[32,3584]{1,0:T(8,128)(2,1)S(1)}, bf16[32,3584]{1,0:T(8,128)(2,1)S(1)}, u32[]{:S(2)}, u32[]{:S(2)}) collective-permute-start(bf16[32,3584]{1,0:T(8,128)(2,1)S(1)} %get-tuple-element.143), channel_id=1, source_target_pairs={{0,4},{2,6},{4,0},{6,2},{8,12},{10,14},{12,8},{14,10},{1,5},{3,7},... | collective-permute-start | bytes 688136 | tf_op jit(solution)/shard_map/ppermute | solution.py:41
  158.0 25.3 %collective-permute-start.23 = (bf16[32,3584]{1,0:T(8,128)(2,1)S(1)}, bf16[32,3584]{1,0:T(8,128)(2,1)S(1)}, u32[]{:S(2)}, u32[]{:S(2)}) collective-permute-start(bf16[32,3584]{1,0:T(8,128)(2,1)S(1)} %get-tuple-element.144), channel_id=1, source_target_pairs={{0,14},{2,12},{4,10},{6,8},{8,6},{10,4},{12,2},{14,0},{1,15},{3,13... | collective-permute-start | bytes 688136 | tf_op jit(solution)/shard_map/ppermute | solution.py:41
  176.6 23.8 %collective-permute-start.26 = (bf16[32,3584]{1,0:T(8,128)(2,1)S(1)}, bf16[32,3584]{1,0:T(8,128)(2,1)S(1)}, u32[]{:S(2)}, u32[]{:S(2)}) collective-permute-start(bf16[32,3584]{1,0:T(8,128)(2,1)S(1)} %get-tuple-element.147), channel_id=1, source_target_pairs={{0,8},{2,10},{4,12},{6,14},{8,0},{10,2},{12,4},{14,6},{1,9},{3,11}... | collective-permute-start | bytes 688136 | tf_op jit(solution)/shard_map/ppermute | solution.py:41
  180.0 34.2 %collective-permute-start.27 = (bf16[32,3584]{1,0:T(8,128)(2,1)S(1)}, bf16[32,3584]{1,0:T(8,128)(2,1)S(1)}, u32[]{:S(2)}, u32[]{:S(2)}) collective-permute-start(bf16[32,3584]{1,0:T(8,128)(2,1)S(1)} %get-tuple-element.148), channel_id=1, source_target_pairs={{0,6},{2,4},{4,2},{6,0},{8,14},{10,12},{12,10},{14,8},{1,7},{3,5},... | collective-permute-start | bytes 688136 | tf_op jit(solution)/shard_map/ppermute | solution.py:41
  183.3 39.2 %collective-permute-start.36 = (bf16[32,3584]{1,0:T(8,128)(2,1)S(1)}, bf16[32,3584]{1,0:T(8,128)(2,1)S(1)}, u32[]{:S(2)}, u32[]{:S(2)}) collective-permute-start(bf16[32,3584]{1,0:T(8,128)(2,1)S(1)} %get-tuple-element.176), channel_id=1, source_target_pairs={{0,2},{2,0},{4,6},{6,4},{8,10},{10,8},{12,14},{14,12},{1,3},{3,1},... | collective-permute-start | bytes 688136 | tf_op jit(solution)/shard_map/ppermute | solution.py:41
  184.4 41.4 %collective-permute-start.37 = (bf16[32,3584]{1,0:T(8,128)(2,1)S(1)}, bf16[32,3584]{1,0:T(8,128)(2,1)S(1)}, u32[]{:S(2)}, u32[]{:S(2)}) collective-permute-start(bf16[32,3584]{1,0:T(8,128)(2,1)S(1)} %get-tuple-element.177), channel_id=1, source_target_pairs={{0,4},{2,6},{4,0},{6,2},{8,12},{10,14},{12,8},{14,10},{1,5},{3,7},... | collective-permute-start | bytes 688136 | tf_op jit(solution)/shard_map/ppermute | solution.py:41
  196.3 37.5 %collective-permute-start.38 = (bf16[32,3584]{1,0:T(8,128)(2,1)S(1)}, bf16[32,3584]{1,0:T(8,128)(2,1)S(1)}, u32[]{:S(2)}, u32[]{:S(2)}) collective-permute-start(bf16[32,3584]{1,0:T(8,128)(2,1)S(1)} %get-tuple-element.178), channel_id=1, source_target_pairs={{0,14},{2,12},{4,10},{6,8},{8,6},{10,4},{12,2},{14,0},{1,15},{3,13... | collective-permute-start | bytes 688136 | tf_op jit(solution)/shard_map/ppermute | solution.py:41
  200.4 35.9 %collective-permute-start.39 = (bf16[32,3584]{1,0:T(8,128)(2,1)S(1)}, bf16[32,3584]{1,0:T(8,128)(2,1)S(1)}, u32[]{:S(2)}, u32[]{:S(2)}) collective-permute-start(bf16[32,3584]{1,0:T(8,128)(2,1)S(1)} %get-tuple-element.179), channel_id=1, source_target_pairs={{0,12},{2,14},{4,8},{6,10},{8,4},{10,6},{12,0},{14,2},{1,13},{3,15... | collective-permute-start | bytes 688136 | tf_op jit(solution)/shard_map/ppermute | solution.py:41
  214.2 23.2 %collective-permute-start.40 = (bf16[32,3584]{1,0:T(8,128)(2,1)S(1)}, bf16[32,3584]{1,0:T(8,128)(2,1)S(1)}, u32[]{:S(2)}, u32[]{:S(2)}) collective-permute-start(bf16[32,3584]{1,0:T(8,128)(2,1)S(1)} %get-tuple-element.180), channel_id=1, source_target_pairs={{0,10},{2,8},{4,14},{6,12},{8,2},{10,0},{12,6},{14,4},{1,11},{3,9}... | collective-permute-start | bytes 688136 | tf_op jit(solution)/shard_map/ppermute | solution.py:41
  (44 other events, 664.3 us)
